TPU v7x, 32 devices: a whole 2x2x4 slice. The times are simulated.
32 devices in a mesh: fsdp: 16 (over z, x, core), tensor: 2 (over y).
Axes of the slice: x: 2, y: 2, z: 4, core: 2. Of those that a mesh axis runs over, the one named last changes fastest.
Arguments:
- tokens: bfloat16 [6144, 8192], P(('fsdp', 'tensor'))
- gain: bfloat16 [8192], replicated, may hold values from 0.5 to 1.5
- kv_weight: bfloat16 [8192, 2048], P('fsdp', 'tensor'), may hold values from -0.09375 to 0.09375
- block_mask: int32 [64, 16], P('fsdp', 'tensor'), may hold values from 0 to 1
- cotangent: bfloat16 [6144, 2048], P('fsdp', 'tensor'), may hold values from -0.078125 to 0.078125
Outputs:
- projected: bfloat16 [6144, 2048], P('fsdp', 'tensor')
- weight_grad: float32 [8192, 2048], P('fsdp', 'tensor')
All inputs are finite; a program needn't handle non-finite values.
Results may differ from a plain program's by a relative error of at most 0.005.
Values may be sent and summed in bfloat16 or wider, within the bound.
No kernel may reach another device: no remote copies, remote signals or barrier semaphores. Data moves between devices by JAX's collectives and lax.ppermute only.
A program may use at most 128 MiB of HBM per device.

v0:
```python
import jax
import jax.numpy as jnp
from jax import lax
from jax.sharding import PartitionSpec as P


def normalize(rows, gain):
    values = rows.astype(jnp.float32)
    square = jnp.mean(values * values, axis=-1, keepdims=True)
    return (values * lax.rsqrt(square + 1e-05) * gain.astype(jnp.float32)).astype(jnp.bfloat16)


def apply_mask(panel, mask):
    rows, cols = panel.shape
    mrows, mcols = mask.shape
    shaped = panel.reshape(mrows, rows // mrows, mcols, cols // mcols)
    kept = shaped * mask[:, None, :, None].astype(panel.dtype)
    return kept.reshape(rows, cols)


def per_device(tokens, gain, kv_weight, block_mask, cotangent):
    group = lax.all_gather(normalize(tokens, gain), "tensor", axis=0, tiled=True)
    columns = group
    total = jnp.dot(
        columns,
        apply_mask(
            lax.all_gather(kv_weight, "fsdp", axis=0, tiled=True),
            lax.all_gather(block_mask, "fsdp", axis=0, tiled=True),
        ),
        preferred_element_type=jnp.float32,
    )
    projected = total.astype(jnp.bfloat16)
    columns = group
    summed = lax.psum_scatter(
        lax.dot_general(
            columns, cotangent, (((0,), (0,)), ((), ())), preferred_element_type=jnp.float32
        ),
        "fsdp",
        scatter_dimension=0,
        tiled=True,
    )
    weight_grad = apply_mask(summed, block_mask)
    return (projected, weight_grad)


def solution(mesh):
    return jax.shard_map(
        per_device,
        mesh=mesh,
        in_specs=(
            P(("fsdp", "tensor"), None),
            P(),
            P("fsdp", "tensor"),
            P("fsdp", "tensor"),
            P("fsdp", "tensor"),
        ),
        out_specs=(P("fsdp", "tensor"), P("fsdp", "tensor")),
        check_vma=False,
    )
```

profile of v0, /device:TPU:0, one launch (start us, length us, event | category | flops | bytes accessed | tf_op | source)
XLA Modules:
  0.0 573.0 jit_solution(3337043055114946187)
XLA Ops:
  7.2 0.0 copy-start
  7.2 0.0 all-gather.4.cloned.1.call-start
  7.2 0.8 convert_element_type.21
  8.0 2.6 fusion.2
  10.6 4.4 fusion.4
  15.0 0.0 all-gather.4.cloned.1.call-update
  15.0 0.0 all-gather.6.cloned.1.call-start
  15.1 0.7 all-gather.6.cloned.1.call-update
  15.8 0.0 reduce-scatter.2.cloned.1.call-start
  15.8 82.4 %all-gather.4.cloned.1.call-done = bf16[384,8192]{1,0:T(8,128)(2,1)} async-done(((bf16[192,8192]{1,0:T(8,128)(2,1)}), bf16[384,8192]{1,0:T(8,128)(2,1)}) %all-gather.4.cloned.1.call-update) | async-done | bytes 6291472 | tf_op jit(solution)/shard_map/all_gather | solution.py:22
  98.3 0.0 copy-done
  98.3 19.1 %fusion.6 = f32[8192,1024]{1,0:T(8,128)} fusion(bf16[384,8192]{1,0:T(8,128)(2,1)} %all-gather.4.cloned.1.call-done, bf16[384,1024]{1,0:T(8,128)(2,1)S(1)} %copy-done), kind=kOutput, calls=%fused_computation.11 | convolution fusion | flops 6442450944 | bytes 40632320 | tf_op jit(solution)/shard_map/dot_general | solution.py:35
  117.3 0.0 copy-start.2
  117.3 0.0 reduce-scatter.2.cloned.1.call-update
  117.3 0.7 copy-done.2
  118.0 22.1 %all-gather = s32[16,4,8]{2,1,0:T(4,128)S(1)} all-gather(s32[1,4,8]{2,1,0:T(4,128)S(1)} %bitcast.19), channel_id=1, replica_groups=mesh['fsdp'=16,'tensor'=2] {'fsdp'}, dimensions={0}, use_global_device_ids=true | all-gather | bytes 2176 | tf_op jit(solution)/shard_map/all_gather | solution.py:28
  140.2 87.3 %all-gather.6.cloned.1.call-done = bf16[8192,1024]{1,0:T(8,128)(2,1)} async-done(((bf16[512,1024]{1,0:T(8,128)(2,1)}), bf16[8192,1024]{1,0:T(8,128)(2,1)}) %all-gather.6.cloned.1.call-update) | async-done | bytes 16777232 | tf_op jit(solution)/shard_map/all_gather | solution.py:27
  227.5 6.1 %mul.46 = bf16[64,128,8,128]{3,2,1,0:T(8,128)(2,1)} broadcast(bf16[64,8]{1,0:T(8,128)(2,1)S(1)} %bitcast.18), dimensions={0,2} | broadcast | bytes 16778240 | tf_op jit(solution)/shard_map/mul | solution.py:17
  233.6 0.0 copy-start.1
  233.6 26.4 %fusion.5 = bf16[384,1024]{1,0:T(8,128)(2,1)} fusion(bf16[384,8192]{1,0:T(8,128)(2,1)} %all-gather.4.cloned.1.call-done, bf16[8192,1024]{1,0:T(8,128)(2,1)} %all-gather.6.cloned.1.call-done, bf16[1024,8,8,128]{3,2,1,0:T(8,128)(2,1)} %bitcast.16), kind=kOutput, calls=%fused_computation.9 | convolution fusion | flops 6451232768 | bytes 40632320 | tf_op jit(solution)/shard_map/dot_general | solution.py:24
  260.0 302.7 %reduce-scatter.2.cloned.1.call-done = f32[512,1024]{1,0:T(8,128)} async-done(((f32[8192,1024]{1,0:T(8,128)}), f32[512,1024]{1,0:T(8,128)}) %reduce-scatter.2.cloned.1.call-update) | async-done | bytes 2097168 | tf_op jit(solution)/shard_map/reduce_scatter | solution.py:34
  562.7 0.2 mul.49
  562.9 3.6 bitcast_multiply_fusion.2
  566.5 0.0 copy-done.1
  (3 shorter events, 0.0 us)
Async XLA Ops:
  7.2 91.1 %copy-start = (bf16[384,1024]{1,0:T(8,128)(2,1)S(1)}, bf16[384,1024]{1,0:T(8,128)(2,1)}, u32[]{:S(2)}) copy-start(bf16[384,1024]{1,0:T(8,128)(2,1)} %param.9) | copy-start | bytes 2359300
  7.2 91.1 %all-gather.4.cloned.1.call-start = ((), (), s32[]{:S(2)}) async-start(), calls=%async_computation.1 | async-start | bytes 9437184 | tf_op jit(solution)/shard_map/all_gather | solution.py:22
  15.0 212.5 %all-gather.6.cloned.1.call-start = ((), (), s32[]{:S(2)}) async-start(), calls=%async_computation.2 | async-start | bytes 17825792 | tf_op jit(solution)/shard_map/all_gather | solution.py:27
  15.8 546.9 %reduce-scatter.2.cloned.1.call-start = ((), (), s32[]{:S(2)}) async-start(), calls=%async_computation.3 | async-start | bytes 35651584 | tf_op jit(solution)/shard_map/reduce_scatter | solution.py:34
  117.3 0.7 copy-start.2
  233.6 332.9 %copy-start.1 = (bf16[384,1024]{1,0:T(8,128)(2,1)S(1)}, bf16[384,1024]{1,0:T(8,128)(2,1)}, u32[]{:S(2)}) copy-start(bf16[384,1024]{1,0:T(8,128)(2,1)} %param.9) | copy-start | bytes 2359300
Sparse Core Ops, SparseCore 0:
  15.1 83.0 all-gather.3
  100.4 127.0 all-gather.5
  231.8 330.8 reduce-scatter.1
where the time goes:
time: 573 us
  waiting for transfers between devices  473 us (83%)
  matrix products  45.5 us (8%)
  blocking collectives  22.1 us (4%)
  between operations  13.8 us (2%)
  other arithmetic  11.4 us (2%)
  local copies, waits for them, and re-layouts  6.94 us (1%)
    reduce_scatter x1, waiting for transfers between devices, per_device(): lax.psum_scatter(lax.dot_general(columns, cotangent, (((0,), (0,)), ((),...  303 us
    all_gather x1, waiting for transfers between devices, per_device(): lax.all_gather(kv_weight, 'fsdp', axis=0, tiled=True)  87.3 us
    all_gather x1, waiting for transfers between devices, per_device(): lax.all_gather(normalize(tokens, gain), 'tensor', axis=0, tiled=True)  82.4 us
    dot_general x1, matrix products, per_device(): jnp.dot(columns, apply_mask(lax.all_gather(kv_weight, 'fsdp', axis=0, til...  26.4 us
    all_gather x1, blocking collectives, per_device(): lax.all_gather(block_mask, 'fsdp', axis=0, tiled=True)  22.1 us
    dot_general x1, matrix products, per_device(): lax.dot_general(columns, cotangent, (((0,), (0,)), ((), ())), preferred_e...  19.1 us
  transfers between devices with their start and end apart: 3, of which 3 were waited for; matrix products, arithmetic and copies ran while one was open for 9% of the time, Pallas kernels for 0%

commit v1 on v0

v1 whole, which is shorter than its diff:
```python
import functools

import jax
import jax.numpy as jnp
import numpy as np
from jax import lax
from jax.experimental import pallas as pl
from jax.experimental.pallas import tpu as pltpu
from jax.sharding import PartitionSpec as P

BF = jnp.bfloat16
F32 = jnp.float32


def orders(depth):
    order = np.array([sorted(range(depth), key=lambda d: (-abs(d - z), -d)) for z in range(depth)])
    return order, np.argsort(order, axis=1)


def norm_kernel(layers, width, index, tokens, gain, *outs):
    values = tokens[...].astype(F32)
    scale = lax.rsqrt(jnp.mean(values * values, axis=-1, keepdims=True) + 1e-05)
    for r in range(4):
        for k in range(layers):
            at = pl.ds(pl.multiple_of(index[r * layers + k] * width, width), width)
            part = tokens[:, at].astype(F32) * scale * gain[:, at].astype(F32)
            outs[r][k] = part.astype(BF)


def normalize(tokens, gain, index, layers, tile=64):
    rows, features = tokens.shape
    width = features // (4 * layers)
    return pl.pallas_call(
        functools.partial(norm_kernel, layers, width),
        out_shape=[jax.ShapeDtypeStruct((layers, rows, width), BF)] * 4,
        grid_spec=pltpu.PrefetchScalarGridSpec(
            num_scalar_prefetch=1,
            grid=(rows // tile,),
            in_specs=[
                pl.BlockSpec((tile, features), lambda i, s: (i, 0)),
                pl.BlockSpec((1, features), lambda i, s: (0, 0)),
            ],
            out_specs=[pl.BlockSpec((layers, tile, width), lambda i, s: (0, i, 0))] * 4,
        ),
        compiler_params=pltpu.CompilerParams(vmem_limit_bytes=32 * 2**20),
        name="normalize",
    )(index, tokens, gain.reshape(1, features))


def apply_mask(panel, mask):
    rows, cols = panel.shape
    mrows, mcols = mask.shape
    shaped = panel.reshape(mrows, rows // mrows, mcols, cols // mcols)
    kept = shaped * mask[:, None, :, None].astype(panel.dtype)
    return kept.reshape(rows, cols)


def pick(arrays, which, values):
    values = sorted(set(int(v) for v in values))
    out = arrays[values[0]]
    for v in values[1:]:
        out = jnp.where(which == v, arrays[v], out)
    return out


def per_device(tokens, gain, kv_weight, block_mask, cotangent):
    group, teams = lax.axis_size("fsdp"), lax.axis_size("tensor")
    layers = group // 4
    f, t = lax.axis_index("fsdp"), lax.axis_index("tensor")
    z, x, c = f // 4, (f // 2) % 2, f % 2
    rows, features = tokens.shape
    width = features // group
    cols = kv_weight.shape[1]
    order, place = orders(layers)

    def over_core(a):
        return lax.ppermute(a, "fsdp", [(i, i ^ 1) for i in range(group)])

    def over_x(a):
        return lax.ppermute(a, "fsdp", [(i, i ^ 2) for i in range(group)])

    def over_y(a):
        return [
            lax.ppermute(a, "tensor", [(i, (i + s) % teams) for i in range(teams)])
            for s in range(1, teams)
        ]

    def over_z(a, pairs):
        return lax.ppermute(a, "fsdp", [(4 * p + i, 4 * q + i) for p, q in pairs for i in range(4)])

    def turn(a):
        parts = a.reshape(teams, rows, a.shape[1])
        if teams == 2:
            back = jnp.concatenate([parts[1:], parts[:1]])
            return jnp.where(t == 0, jnp.concatenate([parts[:1], parts[1:]]), back).reshape(a.shape)
        return parts[(t - jnp.arange(teams)) % teams].reshape(a.shape)

    cot = turn(cotangent)
    cot_x = over_x(cot)
    cot_pair = over_core(jnp.concatenate([cot, cot_x]))
    half = cot.shape[0]

    masked = apply_mask(kv_weight, block_mask)
    ups, downs = [masked], [masked]
    for s in range(1, layers):
        ups.append(over_z(ups[-1], [(p, p + 1) for p in range(s - 1, layers - 1)]))
        downs.append(over_z(downs[-1], [(p, p - 1) for p in range(1, layers - s + 1)]))

    rank = jnp.asarray(order)[z]
    index = jnp.concatenate(
        [rank * 4 + (x ^ rx) * 2 + (c ^ rc) for rx in range(2) for rc in range(2)]
    ).astype(jnp.int32)
    own, core, far, diag = normalize(tokens, gain, index, layers)

    sets = [(0, 1), (1, 2), (2, layers)]
    normed = [None] * layers
    for lo, hi in sets:
        got = over_core(jnp.stack([core[lo:hi], diag[lo:hi]]))
        near = jnp.concatenate([own[lo:hi], got[0]], axis=1)
        cross = over_x(jnp.concatenate([far[lo:hi], got[1]], axis=1))
        pieces = []
        for part in [near, cross]:
            pieces.append([part] + over_y(part))
        for k in range(lo, hi):
            blocks = []
            for arrived in pieces:
                for core_rel in range(2):
                    for piece in arrived:
                        blocks.append(piece[k - lo, core_rel * rows:(core_rel + 1) * rows])
            normed[k] = jnp.concatenate(blocks)
    cots = jnp.concatenate([cot, cot_pair[:half], cot_x, cot_pair[half:]])

    terms = [
        lax.dot_general(n, cots, (((0,), (0,)), ((), ())), preferred_element_type=F32) for n in normed
    ]
    up = down = jnp.zeros((width, cols), BF)
    for s in range(1, layers):
        d = layers - s
        kp = [place[i, min(i + d, layers - 1)] for i in range(layers)]
        km = [place[i, max(i - d, 0)] for i in range(layers)]
        vp = [kp[i] for i in range(layers) if i + d < layers]
        vm = [km[i] for i in range(layers) if i - d >= 0]
        send_up = (pick(terms, jnp.asarray(kp)[z], vp) + up.astype(F32)).astype(BF)
        send_down = (pick(terms, jnp.asarray(km)[z], vm) + down.astype(F32)).astype(BF)
        up = over_z(send_up, [(p, p + 1) for p in range(s)])
        down = over_z(send_down, [(p, p - 1) for p in range(layers - s, layers)])
    weight_grad = apply_mask(terms[layers - 1] + up.astype(F32) + down.astype(F32), block_mask)

    total = jnp.dot(normed[layers - 1], masked, preferred_element_type=F32)
    for s in range(1, layers):
        ku = [place[i, max(i - s, 0)] for i in range(layers)]
        kd = [place[i, min(i + s, layers - 1)] for i in range(layers)]
        vu = [ku[i] for i in range(layers) if i - s >= 0]
        vd = [kd[i] for i in range(layers) if i + s < layers]
        if 2 * s >= layers:
            both = ups[s] + downs[s]
            which = jnp.where(z >= s, jnp.asarray(ku)[z], jnp.asarray(kd)[z])
            total += jnp.dot(pick(normed, which, vu + vd), both, preferred_element_type=F32)
        else:
            total += jnp.dot(pick(normed, jnp.asarray(ku)[z], vu), ups[s], preferred_element_type=F32)
            total += jnp.dot(pick(normed, jnp.asarray(kd)[z], vd), downs[s], preferred_element_type=F32)
    total = total.reshape(2, 2, half, cols)
    sums = total[:, 0] + over_core(total[:, 1])
    projected = turn((sums[0] + over_x(sums[1].astype(BF)).astype(F32)).astype(BF))
    return (projected, weight_grad)


def solution(mesh):
    return jax.shard_map(
        per_device,
        mesh=mesh,
        in_specs=(
            P(("fsdp", "tensor"), None),
            P(),
            P("fsdp", "tensor"),
            P("fsdp", "tensor"),
            P("fsdp", "tensor"),
        ),
        out_specs=(P("fsdp", "tensor"), P("fsdp", "tensor")),
        check_vma=False,
    )
```

time: 573 us -> 237 us (0.41)
  waiting for transfers between devices: 473 us -> 117 us
  starting transfers between devices: 0.12 us -> 46 us
  blocking collectives: 22.1 us -> 0 us
  between operations: 13.8 us -> 4.57 us
  local copies, waits for them, and re-layouts: 6.94 us -> 15.5 us
  matrix products: 45.5 us -> 38.4 us
    reduce_scatter x1 -> x0, waiting for transfers between devices: 303 us -> none  [per_device(): lax.psum_scatter(lax.dot_general(columns, cotangent, (((0,), (0,)), ((),...]
    all_gather x2 -> x0, waiting for transfers between devices: 170 us -> none  [the longest x1 87.3 us: per_device(): lax.all_gather(kv_weight, 'fsdp', axis=0, tiled=True)]
    ppermute x0 -> x28, waiting for transfers between devices: none -> 117 us  [the longest x12 72.1 us: over_z(): lax.ppermute(a, 'fsdp', [(4 * p + i, 4 * q + i) for p, q in pairs for i i...]
    ppermute x0 -> x28, starting transfers between devices: none -> 46 us  [the longest x12 32.2 us: over_z(): lax.ppermute(a, 'fsdp', [(4 * p + i, 4 * q + i) for p, q in pairs for i i...]
    all_gather x1 -> x0, blocking collectives: 22.1 us -> none  [per_device(): lax.all_gather(block_mask, 'fsdp', axis=0, tiled=True)]
    dot_general x2 -> x9, matrix products: 45.5 us -> 38.4 us  [the longest x4 12.9 us: per_device(): lax.dot_general(n, cots, (((0,), (0,)), ((), ())), preferred_element_type...]
    unnamed x6 -> x73, local copies, waits for them, and re-layouts: 0.67 us -> 7.32 us
    mul x2, local copies, waits for them, and re-layouts: 6.26 us -> 0.41 us  [apply_mask(): kept = shaped * mask[:, None, :, None].astype(panel.dtype)]
  transfers between devices with their start and end apart: 3 -> 28, of which waited for: 3 -> 11; matrix products, arithmetic and copies ran while one was open for 9% -> 21% of each run, Pallas kernels for 0% -> 1%
where the time goes in v1:
time: 237 us
  waiting for transfers between devices  117 us (49%)
  starting transfers between devices  46 us (19%)
  matrix products  38.4 us (16%)
  local copies, waits for them, and re-layouts  15.5 us (7%)
  other arithmetic  12.8 us (5%)
  between operations  4.57 us (2%)
    ppermute x12, waiting for transfers between devices, over_z(): lax.ppermute(a, 'fsdp', [(4 * p + i, 4 * q + i) for p, q in pairs for i i...  72.1 us
    ppermute x6, waiting for transfers between devices, over_y(): lax.ppermute(a, 'tensor', [(i, (i + s) % teams) for i in range(teams)])  40.3 us
    ppermute x12, starting transfers between devices, over_z(): lax.ppermute(a, 'fsdp', [(4 * p + i, 4 * q + i) for p, q in pairs for i i...  32.2 us
    dot_general x4, matrix products, per_device(): lax.dot_general(n, cots, (((0,), (0,)), ((), ())), preferred_element_type...  12.9 us
    dot_general x2, matrix products, per_device(): jnp.dot(pick(normed, which, vu + vd), both, preferred_element_type=F32)  10.3 us
    ppermute x6, starting transfers between devices, over_y(): lax.ppermute(a, 'tensor', [(i, (i + s) % teams) for i in range(teams)])  8.36 us
    unnamed x73, local copies, waits for them, and re-layouts  7.32 us
    dot_general x1, matrix products, per_device(): total = jnp.dot(normed[layers - 1], masked, preferred_element_type=F32)  6.45 us
  transfers between devices with their start and end apart: 28, of which 11 were waited for; matrix products, arithmetic and copies ran while one was open for 21% of the time, Pallas kernels for 1%

profile of v1, /device:TPU:0, one launch (start us, length us, event | category | flops | bytes accessed | tf_op | source)
XLA Modules:
  0.0 236.5 jit_solution(15053305888661412145)
XLA Ops:
  3.0 5.9 %collective-permute-start.4 = (bf16[512,1024]{1,0:T(8,128)(2,1)}, bf16[512,1024]{1,0:T(8,128)(2,1)}, u32[]{:S(2)}, u32[]{:S(2)}) collective-permute-start(bf16[512,1024]{1,0:T(8,128)(2,1)} %bitcast_multiply_fusion.1), channel_id=1, source_target_pairs={{0,8},{2,10},{4,12},{6,14},{8,16},{10,18},{12,20},{14,22},{16,24},... | collective-permute-start | bytes 3145736 | tf_op jit(solution)/shard_map/ppermute | solution.py:89
  13.0 2.3 normalize.1
  31.1 8.5 %collective-permute-done.11 = bf16[1,384,512]{2,1,0:T(8,128)(2,1)S(1)} collective-permute-done((bf16[1,384,512]{2,1,0:T(8,128)(2,1)S(1)}, bf16[1,384,512]{2,1,0:T(8,128)(2,1)S(1)}, u32[]{:S(2)}, u32[]{:S(2)}) %collective-permute-start.11) | collective-permute-done | bytes 393248 | tf_op jit(solution)/shard_map/ppermute | solution.py:84
  41.9 8.3 %collective-permute-done.6 = bf16[1,384,512]{2,1,0:T(8,128)(2,1)S(1)} collective-permute-done((bf16[1,384,512]{2,1,0:T(8,128)(2,1)S(1)}, bf16[1,384,512]{2,1,0:T(8,128)(2,1)S(1)}, u32[]{:S(2)}, u32[]{:S(2)}) %collective-permute-start.6) | collective-permute-done | bytes 393248 | tf_op jit(solution)/shard_map/ppermute | solution.py:84
  55.6 4.5 %collective-permute-done.7 = bf16[1,384,512]{2,1,0:T(8,128)(2,1)S(1)} collective-permute-done((bf16[1,384,512]{2,1,0:T(8,128)(2,1)S(1)}, bf16[1,384,512]{2,1,0:T(8,128)(2,1)S(1)}, u32[]{:S(2)}, u32[]{:S(2)}) %collective-permute-start.7) | collective-permute-done | bytes 393248 | tf_op jit(solution)/shard_map/ppermute | solution.py:80
  60.6 17.5 %collective-permute-done.13 = bf16[1,384,512]{2,1,0:T(8,128)(2,1)S(1)} collective-permute-done((bf16[1,384,512]{2,1,0:T(8,128)(2,1)S(1)}, bf16[1,384,512]{2,1,0:T(8,128)(2,1)S(1)}, u32[]{:S(2)}, u32[]{:S(2)}) %collective-permute-start.13) | collective-permute-done | bytes 393248 | tf_op jit(solution)/shard_map/ppermute | solution.py:84
  80.5 6.0 %collective-permute-done.8 = bf16[1,384,512]{2,1,0:T(8,128)(2,1)S(1)} collective-permute-done((bf16[1,384,512]{2,1,0:T(8,128)(2,1)S(1)}, bf16[1,384,512]{2,1,0:T(8,128)(2,1)S(1)}, u32[]{:S(2)}, u32[]{:S(2)}) %collective-permute-start.8) | collective-permute-done | bytes 393248 | tf_op jit(solution)/shard_map/ppermute | solution.py:84
  90.3 20.7 %collective-permute-done.15 = bf16[512,1024]{1,0:T(8,128)(2,1)S(1)} collective-permute-done((bf16[512,1024]{1,0:T(8,128)(2,1)}, bf16[512,1024]{1,0:T(8,128)(2,1)S(1)}, u32[]{:S(2)}, u32[]{:S(2)}) %collective-permute-start.15) | collective-permute-done | bytes 1048608 | tf_op jit(solution)/shard_map/ppermute | solution.py:89
  114.5 6.5 %fusion.47 = f32[1536,1024]{1,0:T(8,128)} fusion(bf16[1536,512]{1,0:T(8,128)(2,1)S(1)} %get-tuple-element.20, bf16[512,1024]{1,0:T(8,128)(2,1)} %bitcast_multiply_fusion.1), kind=kOutput, calls=%fused_computation.125 | convolution fusion | flops 1610612736 | bytes 8912896 | tf_op jit(solution)/shard_map/dot_general | solution.py:149
  122.2 5.8 %fusion.48 = f32[1536,1024]{1,0:T(8,128)} fusion(bf16[1536,512]{1,0:T(8,128)(2,1)S(1)} %get-tuple-element.21, bf16[512,1024]{1,0:T(8,128)(2,1)} %collective-permute-done.4), kind=kOutput, calls=%fused_computation.126 | convolution fusion | flops 1610612736 | bytes 8912896 | tf_op jit(solution)/shard_map/dot_general | solution.py:160
  128.1 3.0 %fusion.5 = f32[1536,1024]{1,0:T(8,128)S(1)} fusion(bf16[512,1024]{1,0:T(8,128)(2,1)} %collective-permute-done.9, bf16[1536,512]{1,0:T(8,128)(2,1)S(1)} %get-tuple-element.21, bf16[1536,512]{1,0:T(8,128)(2,1)S(1)} %fusion.18, pred[]{:T(512)} %bitcast.24), kind=kOutput, calls=%fused_computation.17 | convolution fusion | flops 1611399168 | bytes 10485761 | tf_op jit(solution)/shard_map/dot_general | solution.py:161
  133.9 8.4 %add_add_fusion = f32[1536,1024]{1,0:T(8,128)S(1)} fusion(f32[1536,1024]{1,0:T(8,128)S(1)} %fusion.3, f32[1536,1024]{1,0:T(8,128)S(1)} %fusion.5, f32[1536,1024]{1,0:T(8,128)} %fusion.47, f32[1536,1024]{1,0:T(8,128)} %fusion.48, bf16[1536,512]{1,0:T(8,128)(2,1)} %copy-done.5, bf16[512,1024]{1,0:T(8,128)(2,1)} %copy-done.11, ...), kind=kOutput, calls=%fused_computation | convolution fusion | flops 1617428480 | bytes 35127296 | tf_op jit(solution)/shard_map/dot_general | solution.py:158
  144.2 3.3 %fusion.46 = (bf16[512,1024]{1,0:T(8,128)(2,1)S(1)}, f32[512,1024]{1,0:T(8,128)S(1)}) fusion(bf16[1536,512]{1,0:T(8,128)(2,1)S(1)} %copy-done.6, bf16[384,1024]{1,0:T(8,128)(2,1)S(1)} %copy-done.19, bf16[384,1024]{1,0:T(8,128)(2,1)} %collective-permute-done.20, bf16[384,1024]{1,0:T(8,128)(2,1)S(1)} %copy-done.18, bf16[384,1024]{1,0:T(8,128)(2,1)} %bitcast.61), kind=kOutput, calls=%fused_computation.124 | convolution fusion | flops 1623719936 | bytes 7864320 | tf_op jit(solution)/shard_map/dot_general | solution.py:134
  147.5 3.6 %collective-permute-start.22 = (bf16[512,1024]{1,0:T(8,128)(2,1)S(1)}, bf16[512,1024]{1,0:T(8,128)(2,1)S(1)}, u32[]{:S(2)}, u32[]{:S(2)}) collective-permute-start(bf16[512,1024]{1,0:T(8,128)(2,1)S(1)} %get-tuple-element.58), channel_id=1, source_target_pairs={{0,8},{2,10},{4,12},{6,14},{1,9},{3,11},{5,13},{7,15}} | collective-permute-start | bytes 3145736 | tf_op jit(solution)/shard_map/ppermute | solution.py:89
  153.0 3.2 %fusion.39 = f32[512,1024]{1,0:T(8,128)S(1)} fusion(bf16[1536,512]{1,0:T(8,128)(2,1)S(1)} %copy-done.3, bf16[384,1024]{1,0:T(8,128)(2,1)S(1)} %copy-done.19, bf16[384,1024]{1,0:T(8,128)(2,1)} %collective-permute-done.20, bf16[384,1024]{1,0:T(8,128)(2,1)S(1)} %copy-done.18, bf16[384,1024]{1,0:T(8,128)(2,1)} %bitcast.61), kind=kOutput, calls=%fused_computation.117 | convolution fusion | flops 1623195648 | bytes 6815744 | tf_op jit(solution)/shard_map/dot_general | solution.py:134
  156.2 16.4 %collective-permute-done.22 = bf16[512,1024]{1,0:T(8,128)(2,1)S(1)} collective-permute-done((bf16[512,1024]{1,0:T(8,128)(2,1)S(1)}, bf16[512,1024]{1,0:T(8,128)(2,1)S(1)}, u32[]{:S(2)}, u32[]{:S(2)}) %collective-permute-start.22) | collective-permute-done | bytes 1048608 | tf_op jit(solution)/shard_map/ppermute | solution.py:89
  173.4 4.5 %collective-permute-start.23 = (bf16[512,1024]{1,0:T(8,128)(2,1)S(1)}, bf16[512,1024]{1,0:T(8,128)(2,1)S(1)}, u32[]{:S(2)}, u32[]{:S(2)}) collective-permute-start(bf16[512,1024]{1,0:T(8,128)(2,1)S(1)} %get-tuple-element.10), channel_id=1, source_target_pairs={{0,8},{2,10},{4,12},{6,14},{8,16},{10,18},{12,20},{14,22},{1,9},{3... | collective-permute-start | bytes 3145736 | tf_op jit(solution)/shard_map/ppermute | solution.py:89
  178.9 3.2 %fusion.40 = f32[512,1024]{1,0:T(8,128)S(1)} fusion(bf16[1536,512]{1,0:T(8,128)(2,1)S(1)} %copy-done.9, bf16[384,1024]{1,0:T(8,128)(2,1)S(1)} %copy-done.19, bf16[384,1024]{1,0:T(8,128)(2,1)} %collective-permute-done.20, bf16[384,1024]{1,0:T(8,128)(2,1)S(1)} %copy-done.18, bf16[384,1024]{1,0:T(8,128)(2,1)} %bitcast.61), kind=kOutput, calls=%fused_computation.118 | convolution fusion | flops 1623195648 | bytes 6815744 | tf_op jit(solution)/shard_map/dot_general | solution.py:134
  182.0 16.4 %collective-permute-done.23 = bf16[512,1024]{1,0:T(8,128)(2,1)S(1)} collective-permute-done((bf16[512,1024]{1,0:T(8,128)(2,1)S(1)}, bf16[512,1024]{1,0:T(8,128)(2,1)S(1)}, u32[]{:S(2)}, u32[]{:S(2)}) %collective-permute-start.23) | collective-permute-done | bytes 1048608 | tf_op jit(solution)/shard_map/ppermute | solution.py:89
  199.3 9.8 %collective-permute-start.24 = (bf16[512,1024]{1,0:T(8,128)(2,1)S(1)}, bf16[512,1024]{1,0:T(8,128)(2,1)S(1)}, u32[]{:S(2)}, u32[]{:S(2)}) collective-permute-start(bf16[512,1024]{1,0:T(8,128)(2,1)S(1)} %get-tuple-element.12), channel_id=1, source_target_pairs={{0,8},{2,10},{4,12},{6,14},{8,16},{10,18},{12,20},{14,22},{16,24},... | collective-permute-start | bytes 3145736 | tf_op jit(solution)/shard_map/ppermute | solution.py:89
  212.8 3.2 %fusion.41 = f32[512,1024]{1,0:T(8,128)S(1)} fusion(bf16[1536,512]{1,0:T(8,128)(2,1)S(1)} %copy-done.22, bf16[384,1024]{1,0:T(8,128)(2,1)S(1)} %copy-done.19, bf16[384,1024]{1,0:T(8,128)(2,1)} %collective-permute-done.20, bf16[384,1024]{1,0:T(8,128)(2,1)S(1)} %copy-done.18, bf16[384,1024]{1,0:T(8,128)(2,1)} %bitcast.61), kind=kOutput, calls=%fused_computation.119 | convolution fusion | flops 1623195648 | bytes 6815744 | tf_op jit(solution)/shard_map/dot_general | solution.py:134
  216.0 12.6 %collective-permute-done.24 = bf16[512,1024]{1,0:T(8,128)(2,1)S(1)} collective-permute-done((bf16[512,1024]{1,0:T(8,128)(2,1)S(1)}, bf16[512,1024]{1,0:T(8,128)(2,1)S(1)}, u32[]{:S(2)}, u32[]{:S(2)}) %collective-permute-start.24) | collective-permute-done | bytes 1048608 | tf_op jit(solution)/shard_map/ppermute | solution.py:89
  228.6 4.2 %collective-permute-done.27 = bf16[512,1024]{1,0:T(8,128)(2,1)S(1)} collective-permute-done((bf16[512,1024]{1,0:T(8,128)(2,1)S(1)}, bf16[512,1024]{1,0:T(8,128)(2,1)S(1)}, u32[]{:S(2)}, u32[]{:S(2)}) %collective-permute-start.27) | collective-permute-done | bytes 1048608 | tf_op jit(solution)/shard_map/ppermute | solution.py:89
  232.9 2.3 bitcast_multiply_fusion
  (158 shorter events, 52.0 us)
Async XLA Ops:
  3.0 76.6 %collective-permute-start.4 = (bf16[512,1024]{1,0:T(8,128)(2,1)}, bf16[512,1024]{1,0:T(8,128)(2,1)}, u32[]{:S(2)}, u32[]{:S(2)}) collective-permute-start(bf16[512,1024]{1,0:T(8,128)(2,1)} %bitcast_multiply_fusion.1), channel_id=1, source_target_pairs={{0,8},{2,10},{4,12},{6,14},{8,16},{10,18},{12,20},{14,22},{16,24},... | collective-permute-start | bytes 3145736 | tf_op jit(solution)/shard_map/ppermute | solution.py:89
  8.9 70.8 %collective-permute-start.9 = (bf16[512,1024]{1,0:T(8,128)(2,1)}, bf16[512,1024]{1,0:T(8,128)(2,1)}, u32[]{:S(2)}, u32[]{:S(2)}) collective-permute-start(bf16[512,1024]{1,0:T(8,128)(2,1)} %bitcast_multiply_fusion.1), channel_id=1, source_target_pairs={{8,0},{10,2},{12,4},{14,6},{16,8},{18,10},{20,12},{22,14},{24,16},... | collective-permute-start | bytes 3145736 | tf_op jit(solution)/shard_map/ppermute | solution.py:89
  16.9 11.0 %collective-permute-start.10 = (bf16[2,1,192,512]{3,2,1,0:T(8,128)(2,1)}, bf16[2,1,192,512]{3,2,1,0:T(8,128)(2,1)S(1)}, u32[]{:S(2)}, u32[]{:S(2)}) collective-permute-start(bf16[2,1,192,512]{3,2,1,0:T(8,128)(2,1)} %pad_maximum_fusion.8), channel_id=1, source_target_pairs={{0,2},{2,0},{4,6},{6,4},{8,10},{10,8},{12,14},{14,12},{16,18},{18,... | collective-permute-start | bytes 1179656 | tf_op jit(solution)/shard_map/ppermute | solution.py:77
  19.2 34.2 %collective-permute-start.20 = (bf16[384,1024]{1,0:T(8,128)(2,1)}, bf16[384,1024]{1,0:T(8,128)(2,1)}, u32[]{:S(2)}, u32[]{:S(2)}) collective-permute-start(bf16[384,1024]{1,0:T(8,128)(2,1)} %bitcast.61), channel_id=1, source_target_pairs={{0,4},{2,6},{4,0},{6,2},{8,12},{10,14},{12,8},{14,10},{16,20},{18,... | collective-permute-start | bytes 2359304 | tf_op jit(solution)/shard_map/ppermute | solution.py:80
  27.9 13.4 %collective-permute-start = (bf16[2,2,192,512]{3,2,1,0:T(8,128)(2,1)S(1)}, bf16[2,2,192,512]{3,2,1,0:T(8,128)(2,1)S(1)}, u32[]{:S(2)}, u32[]{:S(2)}) collective-permute-start(bf16[2,2,192,512]{3,2,1,0:T(8,128)(2,1)S(1)} %pad_maximum_fusion.2), channel_id=1, source_target_pairs={{0,2},{2,0},{4,6},{6,4},{8,10},{10,8},{12,14},{14,12},{16,18},{18,... | collective-permute-start | bytes 2359304 | tf_op jit(solution)/shard_map/ppermute | solution.py:77
  28.4 11.3 %collective-permute-start.11 = (bf16[1,384,512]{2,1,0:T(8,128)(2,1)S(1)}, bf16[1,384,512]{2,1,0:T(8,128)(2,1)S(1)}, u32[]{:S(2)}, u32[]{:S(2)}) collective-permute-start(bf16[1,384,512]{2,1,0:T(8,128)(2,1)S(1)} %pad_maximum_fusion.9), channel_id=1, source_target_pairs={{0,1},{1,0},{2,3},{3,2},{4,5},{5,4},{6,7},{7,6},{8,9},{9,8},{10,11... | collective-permute-start | bytes 1179656 | tf_op jit(solution)/shard_map/ppermute | solution.py:84
  39.7 10.5 %collective-permute-start.6 = (bf16[1,384,512]{2,1,0:T(8,128)(2,1)S(1)}, bf16[1,384,512]{2,1,0:T(8,128)(2,1)S(1)}, u32[]{:S(2)}, u32[]{:S(2)}) collective-permute-start(bf16[1,384,512]{2,1,0:T(8,128)(2,1)S(1)} %pad_maximum_fusion.6), channel_id=1, source_target_pairs={{0,1},{1,0},{2,3},{3,2},{4,5},{5,4},{6,7},{7,6},{8,9},{9,8},{10,11... | collective-permute-start | bytes 1179656 | tf_op jit(solution)/shard_map/ppermute | solution.py:84
  41.3 10.5 %collective-permute-start.12 = (bf16[1,384,512]{2,1,0:T(8,128)(2,1)S(1)}, bf16[1,384,512]{2,1,0:T(8,128)(2,1)S(1)}, u32[]{:S(2)}, u32[]{:S(2)}) collective-permute-start(bf16[1,384,512]{2,1,0:T(8,128)(2,1)S(1)} %pad_maximum_fusion.10), channel_id=1, source_target_pairs={{0,4},{2,6},{4,0},{6,2},{8,12},{10,14},{12,8},{14,10},{16,20},{18,... | collective-permute-start | bytes 1179656 | tf_op jit(solution)/shard_map/ppermute | solution.py:80
  51.8 37.6 %collective-permute-start.1 = (bf16[2,384,512]{2,1,0:T(8,128)(2,1)S(1)}, bf16[2,384,512]{2,1,0:T(8,128)(2,1)S(1)}, u32[]{:S(2)}, u32[]{:S(2)}) collective-permute-start(bf16[2,384,512]{2,1,0:T(8,128)(2,1)S(1)} %pad_maximum_fusion.3), channel_id=1, source_target_pairs={{0,1},{1,0},{2,3},{3,2},{4,5},{5,4},{6,7},{7,6},{8,9},{9,8},{10,11... | collective-permute-start | bytes 2359304 | tf_op jit(solution)/shard_map/ppermute | solution.py:84
  53.4 24.6 %collective-permute-start.13 = (bf16[1,384,512]{2,1,0:T(8,128)(2,1)S(1)}, bf16[1,384,512]{2,1,0:T(8,128)(2,1)S(1)}, u32[]{:S(2)}, u32[]{:S(2)}) collective-permute-start(bf16[1,384,512]{2,1,0:T(8,128)(2,1)S(1)} %collective-permute-done.12), channel_id=1, source_target_pairs={{0,1},{1,0},{2,3},{3,2},{4,5},{5,4},{6,7},{7,6},{8,9},{9,8},{10,11... | collective-permute-start | bytes 1179656 | tf_op jit(solution)/shard_map/ppermute | solution.py:84
  60.0 27.8 %collective-permute-start.2 = (bf16[2,384,512]{2,1,0:T(8,128)(2,1)S(1)}, bf16[2,384,512]{2,1,0:T(8,128)(2,1)S(1)}, u32[]{:S(2)}, u32[]{:S(2)}) collective-permute-start(bf16[2,384,512]{2,1,0:T(8,128)(2,1)S(1)} %pad_maximum_fusion.4), channel_id=1, source_target_pairs={{0,4},{2,6},{4,0},{6,2},{8,12},{10,14},{12,8},{14,10},{16,20},{18,... | collective-permute-start | bytes 2359304 | tf_op jit(solution)/shard_map/ppermute | solution.py:80
  79.7 41.3 %collective-permute-start.21 = (bf16[768,1024]{1,0:T(8,128)(2,1)S(1)}, bf16[768,1024]{1,0:T(8,128)(2,1)S(1)}, u32[]{:S(2)}, u32[]{:S(2)}) collective-permute-start(bf16[768,1024]{1,0:T(8,128)(2,1)S(1)} %pad_maximum_fusion.1), channel_id=1, source_target_pairs={{0,2},{2,0},{4,6},{6,4},{8,10},{10,8},{12,14},{14,12},{16,18},{18,... | collective-permute-start | bytes 4718600 | tf_op jit(solution)/shard_map/ppermute | solution.py:77
  86.5 24.5 %collective-permute-start.15 = (bf16[512,1024]{1,0:T(8,128)(2,1)}, bf16[512,1024]{1,0:T(8,128)(2,1)S(1)}, u32[]{:S(2)}, u32[]{:S(2)}) collective-permute-start(bf16[512,1024]{1,0:T(8,128)(2,1)} %collective-permute-done.9), channel_id=1, source_target_pairs={{8,0},{10,2},{12,4},{14,6},{16,8},{18,10},{20,12},{22,14},{9,1},{1... | collective-permute-start | bytes 3145736 | tf_op jit(solution)/shard_map/ppermute | solution.py:89
  87.9 26.5 %collective-permute-start.3 = (bf16[2,384,512]{2,1,0:T(8,128)(2,1)S(1)}, bf16[2,384,512]{2,1,0:T(8,128)(2,1)S(1)}, u32[]{:S(2)}, u32[]{:S(2)}) collective-permute-start(bf16[2,384,512]{2,1,0:T(8,128)(2,1)S(1)} %collective-permute-done.2), channel_id=1, source_target_pairs={{0,1},{1,0},{2,3},{3,2},{4,5},{5,4},{6,7},{7,6},{8,9},{9,8},{10,11... | collective-permute-start | bytes 2359304 | tf_op jit(solution)/shard_map/ppermute | solution.py:84
  89.6 41.5 %collective-permute-start.16 = (bf16[512,1024]{1,0:T(8,128)(2,1)S(1)}, bf16[512,1024]{1,0:T(8,128)(2,1)S(1)}, u32[]{:S(2)}, u32[]{:S(2)}) collective-permute-start(bf16[512,1024]{1,0:T(8,128)(2,1)S(1)} %collective-permute-done.14), channel_id=1, source_target_pairs={{16,24},{18,26},{20,28},{22,30},{17,25},{19,27},{21,29},{23,31}} | collective-permute-start | bytes 3145736 | tf_op jit(solution)/shard_map/ppermute | solution.py:89
  111.0 22.9 %collective-permute-start.17 = (bf16[512,1024]{1,0:T(8,128)(2,1)S(1)}, bf16[512,1024]{1,0:T(8,128)(2,1)}, u32[]{:S(2)}, u32[]{:S(2)}) collective-permute-start(bf16[512,1024]{1,0:T(8,128)(2,1)S(1)} %collective-permute-done.15), channel_id=1, source_target_pairs={{8,0},{10,2},{12,4},{14,6},{9,1},{11,3},{13,5},{15,7}} | collective-permute-start | bytes 3145736 | tf_op jit(solution)/shard_map/ppermute | solution.py:89
  142.6 67.7 %collective-permute-start.18 = (f32[2,384,1024]{2,1,0:T(8,128)S(1)}, f32[2,384,1024]{2,1,0:T(8,128)S(1)}, u32[]{:S(2)}, u32[]{:S(2)}) collective-permute-start(f32[2,384,1024]{2,1,0:T(8,128)S(1)} %slice_bitcast_fusion), channel_id=1, source_target_pairs={{0,2},{2,0},{4,6},{6,4},{8,10},{10,8},{12,14},{14,12},{16,18},{18,... | collective-permute-start | bytes 9437192 | tf_op jit(solution)/shard_map/ppermute | solution.py:77
  147.5 25.1 %collective-permute-start.22 = (bf16[512,1024]{1,0:T(8,128)(2,1)S(1)}, bf16[512,1024]{1,0:T(8,128)(2,1)S(1)}, u32[]{:S(2)}, u32[]{:S(2)}) collective-permute-start(bf16[512,1024]{1,0:T(8,128)(2,1)S(1)} %get-tuple-element.58), channel_id=1, source_target_pairs={{0,8},{2,10},{4,12},{6,14},{1,9},{3,11},{5,13},{7,15}} | collective-permute-start | bytes 3145736 | tf_op jit(solution)/shard_map/ppermute | solution.py:89
  151.1 21.5 %collective-permute-start.25 = (bf16[512,1024]{1,0:T(8,128)(2,1)S(1)}, bf16[512,1024]{1,0:T(8,128)(2,1)S(1)}, u32[]{:S(2)}, u32[]{:S(2)}) collective-permute-start(bf16[512,1024]{1,0:T(8,128)(2,1)S(1)} %get-tuple-element.58), channel_id=1, source_target_pairs={{24,16},{26,18},{28,20},{30,22},{25,17},{27,19},{29,21},{31,23}} | collective-permute-start | bytes 3145736 | tf_op jit(solution)/shard_map/ppermute | solution.py:89
  173.4 25.1 %collective-permute-start.23 = (bf16[512,1024]{1,0:T(8,128)(2,1)S(1)}, bf16[512,1024]{1,0:T(8,128)(2,1)S(1)}, u32[]{:S(2)}, u32[]{:S(2)}) collective-permute-start(bf16[512,1024]{1,0:T(8,128)(2,1)S(1)} %get-tuple-element.10), channel_id=1, source_target_pairs={{0,8},{2,10},{4,12},{6,14},{8,16},{10,18},{12,20},{14,22},{1,9},{3... | collective-permute-start | bytes 3145736 | tf_op jit(solution)/shard_map/ppermute | solution.py:89
  177.9 20.6 %collective-permute-start.26 = (bf16[512,1024]{1,0:T(8,128)(2,1)S(1)}, bf16[512,1024]{1,0:T(8,128)(2,1)S(1)}, u32[]{:S(2)}, u32[]{:S(2)}) collective-permute-start(bf16[512,1024]{1,0:T(8,128)(2,1)S(1)} %get-tuple-element.11), channel_id=1, source_target_pairs={{16,8},{18,10},{20,12},{22,14},{24,16},{26,18},{28,20},{30,22},{17... | collective-permute-start | bytes 3145736 | tf_op jit(solution)/shard_map/ppermute | solution.py:89
  199.3 29.3 %collective-permute-start.24 = (bf16[512,1024]{1,0:T(8,128)(2,1)S(1)}, bf16[512,1024]{1,0:T(8,128)(2,1)S(1)}, u32[]{:S(2)}, u32[]{:S(2)}) collective-permute-start(bf16[512,1024]{1,0:T(8,128)(2,1)S(1)} %get-tuple-element.12), channel_id=1, source_target_pairs={{0,8},{2,10},{4,12},{6,14},{8,16},{10,18},{12,20},{14,22},{16,24},... | collective-permute-start | bytes 3145736 | tf_op jit(solution)/shard_map/ppermute | solution.py:89
  209.1 23.7 %collective-permute-start.27 = (bf16[512,1024]{1,0:T(8,128)(2,1)S(1)}, bf16[512,1024]{1,0:T(8,128)(2,1)S(1)}, u32[]{:S(2)}, u32[]{:S(2)}) collective-permute-start(bf16[512,1024]{1,0:T(8,128)(2,1)S(1)} %get-tuple-element.13), channel_id=1, source_target_pairs={{8,0},{10,2},{12,4},{14,6},{16,8},{18,10},{20,12},{22,14},{24,16},... | collective-permute-start | bytes 3145736 | tf_op jit(solution)/shard_map/ppermute | solution.py:89
  211.2 24.0 %collective-permute-start.19 = (bf16[384,1024]{1,0:T(8,128)(2,1)S(1)}, bf16[384,1024]{1,0:T(8,128)(2,1)S(1)}, u32[]{:S(2)}, u32[]{:S(2)}) collective-permute-start(bf16[384,1024]{1,0:T(8,128)(2,1)S(1)} %fusion.11), channel_id=1, source_target_pairs={{0,4},{2,6},{4,0},{6,2},{8,12},{10,14},{12,8},{14,10},{16,20},{18,... | collective-permute-start | bytes 2359304 | tf_op jit(solution)/shard_map/ppermute | solution.py:80
  (31 other events, 291.6 us)

commit v2 on v0

v2 whole, which is shorter than its diff:
```python
import functools

import jax
import jax.numpy as jnp
import numpy as np
from jax import lax
from jax.experimental import pallas as pl
from jax.experimental.pallas import tpu as pltpu
from jax.sharding import PartitionSpec as P

BF = jnp.bfloat16
F32 = jnp.float32
PARTS = 1


def orders(depth):
    order = np.array([sorted(range(depth), key=lambda d: (-abs(d - z), -d)) for z in range(depth)])
    return order, np.argsort(order, axis=1)


def lookup(table, where):
    out = jnp.int32(int(table[0]))
    for i in range(1, len(table)):
        out = jnp.where(where == i, jnp.int32(int(table[i])), out)
    return out


def norm_kernel(order, width, spot, tokens, gain, held, own, first, later, far, token):
    layers = len(order)
    values = tokens[...].astype(F32)
    scale = lax.rsqrt(jnp.mean(values * values, axis=-1, keepdims=True) + 1e-05)
    for k in range(layers):
        layer = lookup(order[:, k], spot[0]) * 4
        outs = [(own.at[k], 0, 0), (first.at[0] if k == 0 else later.at[0, k - 1], 0, 1)]
        outs += [(far.at[k], 1, 0), (first.at[1] if k == 0 else later.at[1, k - 1], 1, 1)]
        for out, rx, rc in outs:
            place = layer + jnp.bitwise_xor(spot[1], rx) * 2 + jnp.bitwise_xor(spot[2], rc)
            at = pl.ds(pl.multiple_of(place * width, width), width)
            part = tokens[:, at].astype(F32) * scale * gain[:, at].astype(F32)
            out[...] = part.astype(BF)
    token[...] = jnp.zeros_like(token)


def normalize(tokens, gain, spot, held, order, tile=64):
    layers = len(order)
    rows, features = tokens.shape
    width = features // (4 * layers)
    shapes = [(layers, rows, width), (2, rows, width), (2, layers - 1, rows, width), (layers, rows, width)]
    blocks = [pl.BlockSpec((layers, tile, width), lambda i: (0, i, 0))]
    blocks.append(pl.BlockSpec((2, tile, width), lambda i: (0, i, 0)))
    blocks.append(pl.BlockSpec((2, layers - 1, tile, width), lambda i: (0, 0, i, 0)))
    blocks.append(blocks[0])
    return pl.pallas_call(
        functools.partial(norm_kernel, order, width),
        out_shape=[jax.ShapeDtypeStruct(shape, BF) for shape in shapes] + [jax.ShapeDtypeStruct((8, 128), F32)],
        grid=(rows // tile,),
        in_specs=[
            pl.BlockSpec(memory_space=pltpu.SMEM),
            pl.BlockSpec((tile, features), lambda i: (i, 0)),
            pl.BlockSpec((1, features), lambda i: (0, 0)),
            pl.BlockSpec(memory_space=pl.ANY),
        ],
        out_specs=blocks + [pl.BlockSpec((8, 128), lambda i: (0, 0))],
        compiler_params=pltpu.CompilerParams(vmem_limit_bytes=60 * 2**20),
        name="normalize",
    )(spot, tokens, gain.reshape(1, features), held)


def whole(shape):
    return pl.BlockSpec(shape, lambda i: (0,) * len(shape))


def at(shape, *where):
    return pl.BlockSpec(shape, lambda i: where)


HELD = pl.BlockSpec(memory_space=pl.ANY)
SCALARS = pl.BlockSpec(memory_space=pltpu.SMEM)


class Line:
    def __init__(self):
        self.token = None

    def call(self, name, kernel, ins, outs, wait=(), alias=None, grid=(1,), cost=(0, 1)):
        held = list(wait) + ([] if self.token is None else [self.token])
        n_in, n_held, n_out = len(ins), len(held), len(outs)

        def body(*refs):
            refs, token = refs[:-1], refs[-1]
            kernel(*refs[:n_in], *refs[n_in + n_held:])
            token[...] = jnp.zeros_like(token)

        result = pl.pallas_call(
            body,
            out_shape=[o for o, _ in outs] + [jax.ShapeDtypeStruct((8, 128), F32)],
            grid=grid,
            in_specs=[spec for _, spec in ins] + [HELD] * n_held,
            out_specs=[spec for _, spec in outs] + [whole((8, 128))],
            input_output_aliases=alias or {},
            compiler_params=pltpu.CompilerParams(vmem_limit_bytes=32 * 2**20),
            cost_estimate=pl.CostEstimate(flops=cost[0], bytes_accessed=cost[1], transcendentals=0),
            name=name,
        )(*[a for a, _ in ins], *held)
        self.token = result[-1]
        return result[:-1]

    def gate(self, *arrays):
        outs = [(jax.ShapeDtypeStruct(a.shape, a.dtype), HELD) for a in arrays]
        alias = {i: i for i in range(len(arrays))}
        out = self.call("gate", lambda *refs: None, [(a, HELD) for a in arrays], outs, alias=alias)
        return out if len(out) > 1 else out[0]

    def join(self, name, pieces, **more):
        rows = sum(block[-2] for _, block, _ in pieces)
        cols = pieces[0][1][-1]

        def kernel(*refs):
            ins, out = refs[:-1], refs[-1]
            row = 0
            for ref in ins:
                flat = ref.shape[-2:]
                out[row:row + flat[0], :] = ref[...].reshape(flat)
                row += flat[0]

        shape = jax.ShapeDtypeStruct((rows, cols), pieces[0][0].dtype)
        ins = [(a, at(block, *where)) for a, block, where in pieces]
        return self.call(name, kernel, ins, [(shape, whole((rows, cols)))], **more)[0]


def per_device(tokens, gain, kv_weight, block_mask, cotangent):
    group, teams = lax.axis_size("fsdp"), lax.axis_size("tensor")
    layers = group // 4
    f, t = lax.axis_index("fsdp"), lax.axis_index("tensor")
    z, x, c = f // 4, (f // 2) % 2, f % 2
    rows, features = tokens.shape
    width = features // group
    cols = kv_weight.shape[1]
    order, place = orders(layers)
    line = Line()

    def over_core(a):
        return lax.ppermute(a, "fsdp", [(i, i ^ 1) for i in range(group)])

    def over_x(a):
        return lax.ppermute(a, "fsdp", [(i, i ^ 2) for i in range(group)])

    def over_y(a):
        return [
            lax.ppermute(a, "tensor", [(i, (i + s) % teams) for i in range(teams)])
            for s in range(1, teams)
        ]

    def over_z(a, pairs):
        return lax.ppermute(a, "fsdp", [(4 * p + i, 4 * q + i) for p, q in pairs for i in range(4)])

    spot = (jnp.stack([z, x, c, t]).astype(jnp.int32), SCALARS)

    def turn_kernel(spot, a, out):
        for i in range(teams):
            j = lax.rem(spot[3] + teams - i, teams)
            out[i * rows:(i + 1) * rows, :] = a[pl.ds(pl.multiple_of(j * rows, rows), rows), :]

    own_shape = cotangent.shape
    cot = line.call(
        "turn", turn_kernel, [spot, (cotangent, whole(own_shape))],
        [(jax.ShapeDtypeStruct(own_shape, BF), whole(own_shape))],
    )[0]
    cot_x = over_x(cot)

    cot_core = over_core(cot)

    own, first, later, far, line.token = normalize(tokens, gain, spot[0], line.token, order)
    first = over_core(first)
    later = over_core(later)
    cot_core = line.gate(cot_core)

    mrows, mcols = block_mask.shape
    tall, wide = width // mrows, cols // mcols

    def mask_kernel(mask, a, out):
        for i in range(mrows):
            for j in range(mcols):
                spot = (slice(i * tall, (i + 1) * tall), slice(j * wide, (j + 1) * wide))
                out[spot] = (a[spot].astype(F32) * mask[i, j].astype(F32)).astype(BF)

    panel = (width, cols)
    masked = line.call(
        "mask", mask_kernel, [(block_mask, SCALARS), (kv_weight, whole(panel))],
        [(jax.ShapeDtypeStruct(panel, BF), whole(panel))],
    )[0]
    up_weight = [masked, over_z(masked, [(p, p + 1) for p in range(layers - 1)])]
    down_weight = [masked, over_z(masked, [(p, p - 1) for p in range(1, layers)])]

    one, two = (1, rows, width), (1, 1, rows, width)

    def near_of(k):
        return [(own, one, (k, 0, 0)), (first, one, (0, 0, 0)) if k == 0 else (later, two, (0, k - 1, 0, 0))]

    def cross_of(k):
        return [(far, one, (k, 0, 0)), (first, one, (1, 0, 0)) if k == 0 else (later, two, (1, k - 1, 0, 0))]

    normed, terms = [None] * layers, [None] * layers
    pair = (2 * rows, width)
    cross_0 = over_x(line.join("cross", cross_of(0)))
    near_0 = line.join("near", near_of(0))
    near_y = over_y(near_0)

    cross_1 = line.join("cross", cross_of(1))
    rest = line.join("cross", [p for k in range(2, layers) for p in cross_of(k)])

    cut = (own_shape[0] // 2, cols)

    def split_kernel(a, low, high):
        low[...] = a[:cut[0]]
        high[...] = a[cut[0]:]

    parts = line.call(
        "split", split_kernel, [(cot_x, whole(own_shape))], [(jax.ShapeDtypeStruct(cut, BF), whole(cut))] * 2
    )
    parts = [over_core(part) for part in parts]

    def add_terms(k, pieces):
        normed[k] = line.join("rows", pieces)
        terms[k] = lax.dot_general(
            normed[k], cots, (((0,), (0,)), ((), ())), preferred_element_type=F32
        )

    def send(s, h, halves, sums):
        d = layers - s
        ups, downs = [(p, p + 1) for p in range(s)], [(p, p - 1) for p in range(layers - s, layers)]
        ku = [place[i, i + d] if i + d < layers else -1 for i in range(layers)]
        kd = [place[i, i - d] if i - d >= 0 else -1 for i in range(layers)]
        single = 2 * s <= layers
        ways = [[max(u, v) for u, v in zip(ku, kd)]] if single else [ku, kd]
        known = sorted({int(k) for w in ways for k in w if k >= 0})
        shape = (width // halves, cols)

        def kernel(spot, *refs):
            which = [lookup(w, spot[0]) for w in ways]
            inside = [
                jnp.where((spot[0] >= 1) & (spot[0] < s), 1, 0),
                jnp.where((spot[0] < layers - 1) & (spot[0] >= layers - s), 1, 0),
            ]
            held, arrived, outs = refs[:len(known)], refs[len(known):len(known) + len(sums)], refs[len(known) + len(sums):]
            for w, out in enumerate(outs):
                for i, k in enumerate(known):
                    if k not in ways[w]:
                        continue

                    @pl.when(which[w] == k)
                    def _():
                        total = held[i][...]
                        if len(arrived) == 1:
                            total += jnp.where(inside[0] + inside[1] > 0, arrived[0][...].astype(F32), 0.0)
                        elif arrived and single:
                            total += jnp.where(inside[0] > 0, arrived[0][...].astype(F32), 0.0)
                            total += jnp.where(inside[1] > 0, arrived[1][...].astype(F32), 0.0)
                        elif arrived:
                            total += jnp.where(inside[w] > 0, arrived[w][...].astype(F32), 0.0)
                        out[...] = total.astype(BF)

                @pl.when(which[w] < 0)
                def _():
                    out[...] = jnp.zeros_like(out)

        ins = [spot] + [(terms[k], at(shape, h, 0)) for k in known] + [(a, whole(shape)) for a in sums]
        outs = [(jax.ShapeDtypeStruct(shape, BF), whole(shape))] * len(ways)
        out = line.call("sums", kernel, ins, outs)
        if 2 * s < layers - 1:
            return [over_z(out[0], ups + downs)]
        return [over_z(out[0], ups), over_z(out[-1], downs)]

    def gather(near, near_y, cross, cross_y, places=(0, 0)):
        blocks = [(a, pair, (places[0], 0)) for a in [near, *near_y]]
        return blocks + [(a, pair, (places[1], 0)) for a in [cross, *cross_y]]

    cross_0 = line.gate(cross_0)
    cross_y = over_y(cross_0)
    cross_1 = over_x(cross_1)
    pieces = [(a, (rows, cols), (i, 0)) for i in range(teams) for a in (cot, cot_core)]
    for i in range(teams):
        pieces.append((cot_x, (rows, cols), (i, 0)))
        pieces.append((parts[2 * i // teams], (rows, cols), (i % (teams // 2), 0)))
    cots = line.join("cotangents", pieces)
    up, down = line.gate(up_weight[1], down_weight[1])
    up_weight[1], down_weight[1] = up, down
    for s in range(2, layers - 1):
        up_weight.append(over_z(up_weight[-1], [(p, p + 1) for p in range(s - 1, layers - 1)]))
        down_weight.append(over_z(down_weight[-1], [(p, p - 1) for p in range(1, layers - s + 1)]))
    add_terms(0, gather(near_0, near_y, cross_0, cross_y))
    sums = [send(1, h, PARTS, []) for h in range(PARTS)]

    late, late_y = {}, {}

    def start_late(k):
        pieces = near_of(k) + ([(cross_1, pair, (0, 0))] if k == 1 else [(rest, pair, (k - 2, 0))])
        late[k] = line.join("late", pieces)
        late_y[k] = over_y(late[k])

    def end_late(k):
        add_terms(k, gather(late[k], late_y[k], late[k], late_y[k], (0, 1)))

    start_late(1)
    rest = over_x(line.gate(rest))
    end_late(1)

    def last_kernel(spot, up, down, out):
        @pl.when(spot[0] == layers - 2)
        def _():
            out[...] = up[...]

        @pl.when(spot[0] != layers - 2)
        def _():
            out[...] = down[...]

    last = line.call(
        "last",
        last_kernel,
        [spot] + [(a, whole(panel)) for a in (up_weight[-1], down_weight[-1])],
        [(jax.ShapeDtypeStruct(panel, BF), whole(panel))],
    )[0]
    last = over_z(last, [(layers - 2, layers - 1), (1, 0)])
    for k in range(2, layers):
        start_late(k)
    for s in range(2, layers):
        sums = [send(s, h, PARTS, sums[h]) for h in range(PARTS)]
        end_late(s)

    def weight_of(d):
        spots = [int(order[i, d]) - i for i in range(layers)]
        options = {}
        for i, away in enumerate(spots):
            if abs(away) == layers - 1:
                options.setdefault("last", (last, []))[1].append(i)
            elif away > 0:
                options.setdefault(away, (down_weight[away], []))[1].append(i)
            else:
                options.setdefault(away, (up_weight[-away], []))[1].append(i)
        options = list(options.values())
        out = options[0][0]
        for arr, layers_of in options[1:]:
            hit = functools.reduce(jnp.logical_or, [z == i for i in layers_of])
            out = jnp.where(hit, arr, out)
        return out

    weight = [weight_of(k) for k in range(layers)]

    def project(side):
        def kernel(*refs):
            rows_of, weights, keep, send_out = refs[:layers], refs[layers:2 * layers], refs[-2], refs[-1]
            total = jnp.dot(rows_of[0][...], weights[0][...], preferred_element_type=F32)
            for k in range(1, layers):
                total += jnp.dot(rows_of[k][...], weights[k][...], preferred_element_type=F32)
            keep[...] = total[:rows]
            send_out[...] = total[rows:].astype(BF)

        ins = [(n, pl.BlockSpec(pair, lambda i: (side * teams + i, 0))) for n in normed]
        ins += [(w, whole((width, cols))) for w in weight]
        shape = (teams * rows, cols)
        outs = [(jax.ShapeDtypeStruct(shape, d), pl.BlockSpec((rows, cols), lambda i: (i, 0))) for d in (F32, BF)]
        cost = (0, 1)
        return line.call("project", kernel, ins, outs, grid=(teams,), cost=cost)

    full = (teams * rows, cols)

    def add_kernel(kept, sent, out):
        out[...] = (kept[...] + sent[...].astype(F32)).astype(BF)

    kept_x, sent_x = project(1)
    sent_x = over_core(sent_x)
    kept, sent = project(0)
    cross_sum = over_x(
        line.call(
            "cross_sum", add_kernel, [(kept_x, whole(full)), (sent_x, whole(full))],
            [(jax.ShapeDtypeStruct(full, BF), whole(full))],
        )[0]
    )
    sent = over_core(sent)

    half = width // PARTS

    def own_kernel(h):
        def kernel(mask, term, up, down, *refs):
            out = refs[-1]
            for i in range(half // tall):
                for j in range(mcols):
                    spot = (slice(i * tall, (i + 1) * tall), slice(j * wide, (j + 1) * wide))
                    total = term[spot] + up[spot].astype(F32) + down[spot].astype(F32)
                    out[spot] = total * mask[h * (half // tall) + i, j].astype(F32)
        return kernel

    weight_grad = None
    for h in range(PARTS):
        up, down = sums[h]
        ins = [(block_mask, SCALARS), (terms[layers - 1], at((half, cols), h, 0))]
        ins += [(up, whole((half, cols))), (down, whole((half, cols)))]
        alias = None
        if weight_grad is not None:
            ins.append((weight_grad, HELD))
            alias = {4: 0}
        outs = [(jax.ShapeDtypeStruct((width, cols), F32), at((half, cols), h, 0))]
        weight_grad = line.call("own_gradient", own_kernel(h), ins, outs, alias=alias)[0]

    def last_sum(spot, kept, sent, arrived, out):
        total = (kept[...] + sent[...].astype(F32) + arrived[...].astype(F32)).astype(BF)
        for i in range(teams):
            j = lax.rem(spot[3] + teams - i, teams)
            out[pl.ds(pl.multiple_of(j * rows, rows), rows), :] = total[i * rows:(i + 1) * rows]

    projected = line.call(
        "projected", last_sum, [spot] + [(a, whole(full)) for a in (kept, sent, cross_sum)],
        [(jax.ShapeDtypeStruct(full, BF), whole(full))],
    )[0]
    return (projected, weight_grad)


def solution(mesh):
    return jax.shard_map(
        per_device,
        mesh=mesh,
        in_specs=(
            P(("fsdp", "tensor"), None),
            P(),
            P("fsdp", "tensor"),
            P("fsdp", "tensor"),
            P("fsdp", "tensor"),
        ),
        out_specs=(P("fsdp", "tensor"), P("fsdp", "tensor")),
        check_vma=False,
    )
```

time: 573 us -> 162 us (0.28)
  waiting for transfers between devices: 473 us -> 78.6 us
  starting transfers between devices: 0.12 us -> 39.1 us
  matrix products: 45.5 us -> 7.25 us
  Pallas kernels: 0 us -> 27.9 us
  blocking collectives: 22.1 us -> 0 us
  between operations: 13.8 us -> 1.17 us
  other arithmetic: 11.4 us -> 1.59 us
    reduce_scatter x1 -> x0, waiting for transfers between devices: 303 us -> none  [per_device(): lax.psum_scatter(lax.dot_general(columns, cotangent, (((0,), (0,)), ((),...]
    all_gather x2 -> x0, waiting for transfers between devices: 170 us -> none  [the longest x1 87.3 us: per_device(): lax.all_gather(kv_weight, 'fsdp', axis=0, tiled=True)]
    ppermute x0 -> x27, waiting for transfers between devices: none -> 78.6 us  [the longest x10 36.3 us: over_z(): lax.ppermute(a, 'fsdp', [(4 * p + i, 4 * q + i) for p, q in pairs for i i...]
    ppermute x0 -> x27, starting transfers between devices: none -> 39.1 us  [the longest x10 23.3 us: over_z(): lax.ppermute(a, 'fsdp', [(4 * p + i, 4 * q + i) for p, q in pairs for i i...]
    dot_general x2 -> x4, matrix products: 45.5 us -> 7.25 us  [add_terms(): lax.dot_general(normed[k], cots, (((0,), (0,)), ((), ())), preferred_elem...]
    pallas_call x0 -> x29, Pallas kernels: none -> 27.9 us  [the longest x28 22.7 us: call(): pl.pallas_call(body, out_shape=[o for o, _ in outs] + [jax.ShapeDtypeStru...]
    all_gather x1 -> x0, blocking collectives: 22.1 us -> none  [per_device(): lax.all_gather(block_mask, 'fsdp', axis=0, tiled=True)]
    mul x2 -> x0, local copies, waits for them, and re-layouts: 6.26 us -> none  [apply_mask(): kept = shaped * mask[:, None, :, None].astype(panel.dtype)]
  transfers between devices with their start and end apart: 3 -> 27, of which waited for: 3 -> 14; matrix products, arithmetic and copies ran while one was open for 9% -> 5% of each run, Pallas kernels for 0% -> 10%
where the time goes in v2:
time: 162 us; the launch traced here: 161 us
  waiting for transfers between devices  78.6 us (49%)
  starting transfers between devices  39.1 us (24%)
  Pallas kernels  27.9 us (17%)
  matrix products  7.25 us (4%)
  local copies, waits for them, and re-layouts  5.55 us (3%)
    ppermute x10, waiting for transfers between devices, over_z(): lax.ppermute(a, 'fsdp', [(4 * p + i, 4 * q + i) for p, q in pairs for i i...  36.3 us
    ppermute x5, waiting for transfers between devices, over_y(): lax.ppermute(a, 'tensor', [(i, (i + s) % teams) for i in range(teams)])  27.5 us
    ppermute x10, starting transfers between devices, over_z(): lax.ppermute(a, 'fsdp', [(4 * p + i, 4 * q + i) for p, q in pairs for i i...  23.3 us
    pallas_call x28, Pallas kernels, call(): pl.pallas_call(body, out_shape=[o for o, _ in outs] + [jax.ShapeDtypeStru...  22.7 us
    ppermute x5, waiting for transfers between devices, over_x(): return lax.ppermute(a, 'fsdp', [(i, i ^ 2) for i in range(group)])  14.2 us
    ppermute x5, starting transfers between devices, over_x(): return lax.ppermute(a, 'fsdp', [(i, i ^ 2) for i in range(group)])  8.74 us
    dot_general x4, matrix products, add_terms(): lax.dot_general(normed[k], cots, (((0,), (0,)), ((), ())), preferred_elem...  7.25 us
    pallas_call x1, Pallas kernels, normalize(): pl.pallas_call(functools.partial(norm_kernel, order, width), out_shape=[j...  5.25 us
  transfers between devices with their start and end apart: 27, of which 14 were waited for; matrix products, arithmetic and copies ran while one was open for 5% of the time, Pallas kernels for 10%

profile of v2, /device:TPU:0, one launch (start us, length us, event | category | flops | bytes accessed | tf_op | source)
XLA Modules:
  0.0 161.1 jit_solution(15745123774546600270)
XLA Ops:
  4.4 5.2 %normalize.1 = (bf16[4,192,512]{2,1,0:T(8,128)(2,1)}, bf16[2,192,512]{2,1,0:T(8,128)(2,1)}, bf16[2,3,192,512]{3,2,1,0:T(8,128)(2,1)}, bf16[4,192,512]{2,1,0:T(8,128)(2,1)}, f32[8,128]{1,0:T(8,128)}) custom-call(s32[4]{0:T(128)} %copy-done.18, bf16[192,8192]{1,0:T(8,128)(2,1)} %tokens.1, bf16[1,8192]{1,0:T(2,128)(2,1)} %reshape.7.gain, f32[8,128]{1,0:T(8,128)} %copy-done.22), custom_call_target="tpu_custom_call" | custom-call | tf_op jit(solution)/shard_map/normalize/pallas_call | solution.py:53
  10.3 2.9 %collective-permute-start.4 = (bf16[384,1024]{1,0:T(8,128)(2,1)S(1)}, bf16[384,1024]{1,0:T(8,128)(2,1)S(1)}, u32[]{:S(2)}, u32[]{:S(2)}) collective-permute-start(bf16[384,1024]{1,0:T(8,128)(2,1)S(1)} %get-tuple-element.71.refs_0_.refs_2_), channel_id=1, source_target_pairs={{0,4},{2,6},{4,0},{6,2},{8,12},{10,14},{12,8},{14,10},{16,20},{18,... | collective-permute-start | bytes 2359304 | tf_op jit(solution)/shard_map/ppermute | solution.py:146
  16.6 5.8 %collective-permute-start.7 = (bf16[512,1024]{1,0:T(8,128)(2,1)S(1)}, bf16[512,1024]{1,0:T(8,128)(2,1)S(1)}, u32[]{:S(2)}, u32[]{:S(2)}) collective-permute-start(bf16[512,1024]{1,0:T(8,128)(2,1)S(1)} %get-tuple-element.84.refs_7_), channel_id=1, source_target_pairs={{0,8},{2,10},{4,12},{6,14},{8,16},{10,18},{12,20},{14,22},{16,24},... | collective-permute-start | bytes 3145736 | tf_op jit(solution)/shard_map/ppermute | solution.py:155
  22.5 2.0 %collective-permute-start.3 = (bf16[384,512]{1,0:T(8,128)(2,1)S(1)}, bf16[384,512]{1,0:T(8,128)(2,1)S(1)}, u32[]{:S(2)}, u32[]{:S(2)}) collective-permute-start(bf16[384,512]{1,0:T(8,128)(2,1)S(1)} %get-tuple-element.77), channel_id=1, source_target_pairs={{0,4},{2,6},{4,0},{6,2},{8,12},{10,14},{12,8},{14,10},{16,20},{18,... | collective-permute-start | bytes 1179656 | tf_op jit(solution)/shard_map/ppermute | solution.py:146
  24.6 6.9 %collective-permute-done.4.refs_0_.refs_4_.refs_6_ = bf16[384,1024]{1,0:T(8,128)(2,1)S(1)} collective-permute-done((bf16[384,1024]{1,0:T(8,128)(2,1)S(1)}, bf16[384,1024]{1,0:T(8,128)(2,1)S(1)}, u32[]{:S(2)}, u32[]{:S(2)}) %collective-permute-start.4) | collective-permute-done | bytes 786464 | tf_op jit(solution)/shard_map/ppermute | solution.py:146
  32.2 7.2 %collective-permute-done.3.refs_0_ = bf16[384,512]{1,0:T(8,128)(2,1)S(1)} collective-permute-done((bf16[384,512]{1,0:T(8,128)(2,1)S(1)}, bf16[384,512]{1,0:T(8,128)(2,1)S(1)}, u32[]{:S(2)}, u32[]{:S(2)}) %collective-permute-start.3) | collective-permute-done | bytes 393248 | tf_op jit(solution)/shard_map/ppermute | solution.py:146
  47.1 4.4 %collective-permute-done.2.refs_1_ = bf16[384,512]{1,0:T(8,128)(2,1)S(1)} collective-permute-done((bf16[384,512]{1,0:T(8,128)(2,1)S(1)}, bf16[384,512]{1,0:T(8,128)(2,1)S(1)}, u32[]{:S(2)}, u32[]{:S(2)}) %collective-permute-start.2) | collective-permute-done | bytes 393248 | tf_op jit(solution)/shard_map/ppermute | solution.py:150
  51.5 7.0 %collective-permute-done.6.refs_3_ = bf16[384,512]{1,0:T(8,128)(2,1)S(1)} collective-permute-done((bf16[384,512]{1,0:T(8,128)(2,1)S(1)}, bf16[384,512]{1,0:T(8,128)(2,1)S(1)}, u32[]{:S(2)}, u32[]{:S(2)}) %collective-permute-start.6) | collective-permute-done | bytes 393248 | tf_op jit(solution)/shard_map/ppermute | solution.py:150
  58.6 1.8 %fusion.refs_1_ = f32[512,1024]{1,0:T(8,128)S(1)} fusion(bf16[1536,512]{1,0:T(8,128)(2,1)S(1)} %get-tuple-element.91.refs_0_, bf16[1536,1024]{1,0:T(8,128)(2,1)S(1)} %get-tuple-element.93), kind=kOutput, calls=%fused_computation.4 | convolution fusion | flops 1610612736 | bytes 6815744 | tf_op jit(solution)/shard_map/dot_general | solution.py:225
  64.2 3.5 %collective-permute-start.17 = (bf16[512,1024]{1,0:T(8,128)(2,1)S(1)}, bf16[512,1024]{1,0:T(8,128)(2,1)S(1)}, u32[]{:S(2)}, u32[]{:S(2)}) collective-permute-start(bf16[512,1024]{1,0:T(8,128)(2,1)S(1)} %get-tuple-element.107), channel_id=1, source_target_pairs={{0,8},{2,10},{4,12},{6,14},{24,16},{26,18},{28,20},{30,22},{1,9},{... | collective-permute-start | bytes 3145736 | tf_op jit(solution)/shard_map/ppermute | solution.py:155
  67.7 11.6 %collective-permute-done.12.refs_1_.refs_3_ = bf16[768,512]{1,0:T(8,128)(2,1)S(1)} collective-permute-done((bf16[768,512]{1,0:T(8,128)(2,1)S(1)}, bf16[768,512]{1,0:T(8,128)(2,1)S(1)}, u32[]{:S(2)}, u32[]{:S(2)}) %collective-permute-start.12) | collective-permute-done | bytes 786464 | tf_op jit(solution)/shard_map/ppermute | solution.py:150
  79.5 2.2 %last.1 = (bf16[512,1024]{1,0:T(8,128)(2,1)}, f32[8,128]{1,0:T(8,128)S(1)}) custom-call(s32[4]{0:T(128)S(1)} %copy-done.19, bf16[512,1024]{1,0:T(8,128)(2,1)S(1)} %collective-permute-done.14.refs_1_, bf16[512,1024]{1,0:T(8,128)(2,1)S(1)} %collective-permute-done.15.refs_2_, f32[8,128]{1,0:T(8,128)S(1)} %get-tuple-element.104.refs_3_), custom_call_target="tpu_custom_call" | custom-call | bytes 1 | tf_op jit(solution)/shard_map/last/pallas_call | solution.py:94
  85.6 2.3 %collective-permute-done.17.refs_3_ = bf16[512,1024]{1,0:T(8,128)(2,1)S(1)} collective-permute-done((bf16[512,1024]{1,0:T(8,128)(2,1)S(1)}, bf16[512,1024]{1,0:T(8,128)(2,1)S(1)}, u32[]{:S(2)}, u32[]{:S(2)}) %collective-permute-start.17) | collective-permute-done | bytes 1048608 | tf_op jit(solution)/shard_map/ppermute | solution.py:155
  87.9 1.9 %sums.4 = (bf16[512,1024]{1,0:T(8,128)(2,1)}, f32[8,128]{1,0:T(8,128)S(1)}) custom-call(s32[4]{0:T(128)S(1)} %copy-done.19, f32[512,1024]{1,0:T(8,128)S(1)} %fusion.refs_1_, f32[512,1024]{1,0:T(8,128)S(1)} %fusion.1.refs_2_.refs_1_, bf16[512,1024]{1,0:T(8,128)(2,1)S(1)} %collective-permute-done.17.refs_3_, f32[8,128]{1,0:T(8,128)S(1)} %get-tuple-element.109.refs_4_), custom_call_target="tpu_custom_call" | custom-call | bytes 1 | tf_op jit(solution)/shard_map/sums/pallas_call | solution.py:94
  91.4 5.0 %collective-permute-start.19 = (bf16[512,1024]{1,0:T(8,128)(2,1)}, bf16[512,1024]{1,0:T(8,128)(2,1)}, u32[]{:S(2)}, u32[]{:S(2)}) collective-permute-start(bf16[512,1024]{1,0:T(8,128)(2,1)} %get-tuple-element.113), channel_id=1, source_target_pairs={{0,8},{2,10},{4,12},{6,14},{8,16},{10,18},{12,20},{14,22},{1,9},{3... | collective-permute-start | bytes 3145736 | tf_op jit(solution)/shard_map/ppermute | solution.py:155
  98.3 4.5 %collective-permute-done.16.refs_1_.refs_3_ = bf16[768,512]{1,0:T(8,128)(2,1)} collective-permute-done((bf16[768,512]{1,0:T(8,128)(2,1)}, bf16[768,512]{1,0:T(8,128)(2,1)}, u32[]{:S(2)}, u32[]{:S(2)}) %collective-permute-start.16) | collective-permute-done | bytes 786464 | tf_op jit(solution)/shard_map/ppermute | solution.py:150
  106.1 9.0 %collective-permute-done.19.refs_3_ = bf16[512,1024]{1,0:T(8,128)(2,1)} collective-permute-done((bf16[512,1024]{1,0:T(8,128)(2,1)}, bf16[512,1024]{1,0:T(8,128)(2,1)}, u32[]{:S(2)}, u32[]{:S(2)}) %collective-permute-start.19) | collective-permute-done | bytes 1048608 | tf_op jit(solution)/shard_map/ppermute | solution.py:155
  115.2 2.1 %sums.5 = (bf16[512,1024]{1,0:T(8,128)(2,1)S(1)}, bf16[512,1024]{1,0:T(8,128)(2,1)S(1)}, f32[8,128]{1,0:T(8,128)S(1)}) custom-call(s32[4]{0:T(128)S(1)} %copy-done.19, f32[512,1024]{1,0:T(8,128)S(1)} %fusion.1.refs_2_.refs_1_, f32[512,1024]{1,0:T(8,128)S(1)} %fusion.2.refs_2_, bf16[512,1024]{1,0:T(8,128)(2,1)} %collective-permute-done.19.refs_3_, ...), custom_call_target="tpu_custom_call" | custom-call | bytes 1 | tf_op jit(solution)/shard_map/sums/pallas_call | solution.py:94
  117.2 3.0 %collective-permute-done.21 = bf16[512,1024]{1,0:T(8,128)(2,1)} collective-permute-done((bf16[512,1024]{1,0:T(8,128)(2,1)}, bf16[512,1024]{1,0:T(8,128)(2,1)}, u32[]{:S(2)}, u32[]{:S(2)}) %collective-permute-start.21) | collective-permute-done | bytes 1048608 | tf_op jit(solution)/shard_map/ppermute | solution.py:155
  123.6 3.6 %project.2 = (f32[384,1024]{1,0:T(8,128)S(1)}, bf16[384,1024]{1,0:T(8,128)(2,1)S(1)}, f32[8,128]{1,0:T(8,128)S(1)}) custom-call(bf16[1536,512]{1,0:T(8,128)(2,1)S(1)} %copy-done.3, bf16[1536,512]{1,0:T(8,128)(2,1)S(1)} %copy-done.5, bf16[1536,512]{1,0:T(8,128)(2,1)S(1)} %get-tuple-element.111.refs_2_, bf16[1536,512]{1,0:T(8,128)(2,1)S(1)} %get-tuple-element.116.refs_3_, ...), custom_call_target="tpu_custom_call" | custom-call | bytes 1 | tf_op jit(solution)/shard_map/project/pallas_call | solution.py:94
  130.2 3.6 %project.3 = (f32[384,1024]{1,0:T(8,128)S(1)}, bf16[384,1024]{1,0:T(8,128)(2,1)S(1)}, f32[8,128]{1,0:T(8,128)S(1)}) custom-call(bf16[1536,512]{1,0:T(8,128)(2,1)S(1)} %copy-done.3, bf16[1536,512]{1,0:T(8,128)(2,1)S(1)} %copy-done.5, bf16[1536,512]{1,0:T(8,128)(2,1)S(1)} %get-tuple-element.111.refs_2_, bf16[1536,512]{1,0:T(8,128)(2,1)S(1)} %get-tuple-element.116.refs_3_, ...), custom_call_target="tpu_custom_call" | custom-call | bytes 1 | tf_op jit(solution)/shard_map/project/pallas_call | solution.py:94
  136.9 15.1 %collective-permute-done.25.refs_2_ = bf16[512,1024]{1,0:T(8,128)(2,1)S(1)} collective-permute-done((bf16[512,1024]{1,0:T(8,128)(2,1)S(1)}, bf16[512,1024]{1,0:T(8,128)(2,1)S(1)}, u32[]{:S(2)}, u32[]{:S(2)}) %collective-permute-start.25) | collective-permute-done | bytes 1048608 | tf_op jit(solution)/shard_map/ppermute | solution.py:155
  152.0 5.3 %collective-permute-done.26.refs_3_ = bf16[512,1024]{1,0:T(8,128)(2,1)S(1)} collective-permute-done((bf16[512,1024]{1,0:T(8,128)(2,1)S(1)}, bf16[512,1024]{1,0:T(8,128)(2,1)S(1)}, u32[]{:S(2)}, u32[]{:S(2)}) %collective-permute-start.26) | collective-permute-done | bytes 1048608 | tf_op jit(solution)/shard_map/ppermute | solution.py:155
  157.2 2.3 %own_gradient.1 = (f32[512,1024]{1,0:T(8,128)}, f32[8,128]{1,0:T(8,128)S(1)}) custom-call(s32[4,8]{1,0:T(4,128)S(1)} %copy-done.20, f32[512,1024]{1,0:T(8,128)S(1)} %fusion.3.refs_1_, bf16[512,1024]{1,0:T(8,128)(2,1)S(1)} %collective-permute-done.25.refs_2_, bf16[512,1024]{1,0:T(8,128)(2,1)S(1)} %collective-permute-done.26.refs_3_, ...), custom_call_target="tpu_custom_call" | custom-call | bytes 1 | tf_op jit(solution)/shard_map/own_gradient/pallas_call | solution.py:94
  (116 shorter events, 41.8 us)
Async XLA Ops:
  9.7 14.8 %collective-permute-start.5 = (bf16[2,3,192,512]{3,2,1,0:T(8,128)(2,1)}, bf16[2,3,192,512]{3,2,1,0:T(8,128)(2,1)S(1)}, u32[]{:S(2)}, u32[]{:S(2)}) collective-permute-start(bf16[2,3,192,512]{3,2,1,0:T(8,128)(2,1)} %get-tuple-element.78), channel_id=1, source_target_pairs={{0,2},{2,0},{4,6},{6,4},{8,10},{10,8},{12,14},{14,12},{16,18},{18,... | collective-permute-start | bytes 3538952 | tf_op jit(solution)/shard_map/ppermute | solution.py:143
  10.3 21.3 %collective-permute-start.4 = (bf16[384,1024]{1,0:T(8,128)(2,1)S(1)}, bf16[384,1024]{1,0:T(8,128)(2,1)S(1)}, u32[]{:S(2)}, u32[]{:S(2)}) collective-permute-start(bf16[384,1024]{1,0:T(8,128)(2,1)S(1)} %get-tuple-element.71.refs_0_.refs_2_), channel_id=1, source_target_pairs={{0,4},{2,6},{4,0},{6,2},{8,12},{10,14},{12,8},{14,10},{16,20},{18,... | collective-permute-start | bytes 2359304 | tf_op jit(solution)/shard_map/ppermute | solution.py:146
  15.3 28.5 %collective-permute-start.8 = (bf16[512,1024]{1,0:T(8,128)(2,1)S(1)}, bf16[512,1024]{1,0:T(8,128)(2,1)S(1)}, u32[]{:S(2)}, u32[]{:S(2)}) collective-permute-start(bf16[512,1024]{1,0:T(8,128)(2,1)S(1)} %get-tuple-element.84.refs_7_), channel_id=1, source_target_pairs={{8,0},{10,2},{12,4},{14,6},{16,8},{18,10},{20,12},{22,14},{24,16},... | collective-permute-start | bytes 3145736 | tf_op jit(solution)/shard_map/ppermute | solution.py:155
  16.6 28.4 %collective-permute-start.7 = (bf16[512,1024]{1,0:T(8,128)(2,1)S(1)}, bf16[512,1024]{1,0:T(8,128)(2,1)S(1)}, u32[]{:S(2)}, u32[]{:S(2)}) collective-permute-start(bf16[512,1024]{1,0:T(8,128)(2,1)S(1)} %get-tuple-element.84.refs_7_), channel_id=1, source_target_pairs={{0,8},{2,10},{4,12},{6,14},{8,16},{10,18},{12,20},{14,22},{16,24},... | collective-permute-start | bytes 3145736 | tf_op jit(solution)/shard_map/ppermute | solution.py:155
  22.5 16.9 %collective-permute-start.3 = (bf16[384,512]{1,0:T(8,128)(2,1)S(1)}, bf16[384,512]{1,0:T(8,128)(2,1)S(1)}, u32[]{:S(2)}, u32[]{:S(2)}) collective-permute-start(bf16[384,512]{1,0:T(8,128)(2,1)S(1)} %get-tuple-element.77), channel_id=1, source_target_pairs={{0,4},{2,6},{4,0},{6,2},{8,12},{10,14},{12,8},{14,10},{16,20},{18,... | collective-permute-start | bytes 1179656 | tf_op jit(solution)/shard_map/ppermute | solution.py:146
  31.6 9.6 %collective-permute-start.9 = (bf16[192,1024]{1,0:T(8,128)(2,1)S(1)}, bf16[192,1024]{1,0:T(8,128)(2,1)S(1)}, u32[]{:S(2)}, u32[]{:S(2)}) collective-permute-start(bf16[192,1024]{1,0:T(8,128)(2,1)S(1)} %get-tuple-element.86), channel_id=1, source_target_pairs={{0,2},{2,0},{4,6},{6,4},{8,10},{10,8},{12,14},{14,12},{16,18},{18,... | collective-permute-start | bytes 1179656 | tf_op jit(solution)/shard_map/ppermute | solution.py:143
  31.7 9.8 %collective-permute-start.10 = (bf16[192,1024]{1,0:T(8,128)(2,1)S(1)}, bf16[192,1024]{1,0:T(8,128)(2,1)S(1)}, u32[]{:S(2)}, u32[]{:S(2)}) collective-permute-start(bf16[192,1024]{1,0:T(8,128)(2,1)S(1)} %get-tuple-element.87), channel_id=1, source_target_pairs={{0,2},{2,0},{4,6},{6,4},{8,10},{10,8},{12,14},{14,12},{16,18},{18,... | collective-permute-start | bytes 1179656 | tf_op jit(solution)/shard_map/ppermute | solution.py:143
  39.4 12.0 %collective-permute-start.2 = (bf16[384,512]{1,0:T(8,128)(2,1)S(1)}, bf16[384,512]{1,0:T(8,128)(2,1)S(1)}, u32[]{:S(2)}, u32[]{:S(2)}) collective-permute-start(bf16[384,512]{1,0:T(8,128)(2,1)S(1)} %get-tuple-element.76.refs_0_), channel_id=1, source_target_pairs={{0,1},{1,0},{2,3},{3,2},{4,5},{5,4},{6,7},{7,6},{8,9},{9,8},{10,11... | collective-permute-start | bytes 1179656 | tf_op jit(solution)/shard_map/ppermute | solution.py:150
  41.2 17.2 %collective-permute-start.6 = (bf16[384,512]{1,0:T(8,128)(2,1)S(1)}, bf16[384,512]{1,0:T(8,128)(2,1)S(1)}, u32[]{:S(2)}, u32[]{:S(2)}) collective-permute-start(bf16[384,512]{1,0:T(8,128)(2,1)S(1)} %get-tuple-element.83.refs_2_), channel_id=1, source_target_pairs={{0,1},{1,0},{2,3},{3,2},{4,5},{5,4},{6,7},{7,6},{8,9},{9,8},{10,11... | collective-permute-start | bytes 1179656 | tf_op jit(solution)/shard_map/ppermute | solution.py:150
  41.5 19.6 %collective-permute-start.11 = (bf16[384,512]{1,0:T(8,128)(2,1)S(1)}, bf16[384,512]{1,0:T(8,128)(2,1)S(1)}, u32[]{:S(2)}, u32[]{:S(2)}) collective-permute-start(bf16[384,512]{1,0:T(8,128)(2,1)S(1)} %get-tuple-element.92), channel_id=1, source_target_pairs={{0,4},{2,6},{4,0},{6,2},{8,12},{10,14},{12,8},{14,10},{16,20},{18,... | collective-permute-start | bytes 1179656 | tf_op jit(solution)/shard_map/ppermute | solution.py:146
  45.1 34.4 %collective-permute-start.14 = (bf16[512,1024]{1,0:T(8,128)(2,1)S(1)}, bf16[512,1024]{1,0:T(8,128)(2,1)S(1)}, u32[]{:S(2)}, u32[]{:S(2)}) collective-permute-start(bf16[512,1024]{1,0:T(8,128)(2,1)S(1)} %get-tuple-element.102), channel_id=1, source_target_pairs={{8,16},{10,18},{12,20},{14,22},{16,24},{18,26},{20,28},{22,30},{9,... | collective-permute-start | bytes 3145736 | tf_op jit(solution)/shard_map/ppermute | solution.py:155
  45.8 33.7 %collective-permute-start.15 = (bf16[512,1024]{1,0:T(8,128)(2,1)S(1)}, bf16[512,1024]{1,0:T(8,128)(2,1)S(1)}, u32[]{:S(2)}, u32[]{:S(2)}) collective-permute-start(bf16[512,1024]{1,0:T(8,128)(2,1)S(1)} %get-tuple-element.103), channel_id=1, source_target_pairs={{8,0},{10,2},{12,4},{14,6},{16,8},{18,10},{20,12},{22,14},{9,1},{1... | collective-permute-start | bytes 3145736 | tf_op jit(solution)/shard_map/ppermute | solution.py:155
  61.1 18.2 %collective-permute-start.12 = (bf16[768,512]{1,0:T(8,128)(2,1)S(1)}, bf16[768,512]{1,0:T(8,128)(2,1)S(1)}, u32[]{:S(2)}, u32[]{:S(2)}) collective-permute-start(bf16[768,512]{1,0:T(8,128)(2,1)S(1)} %get-tuple-element.96.refs_0_.refs_2_), channel_id=1, source_target_pairs={{0,1},{1,0},{2,3},{3,2},{4,5},{5,4},{6,7},{7,6},{8,9},{9,8},{10,11... | collective-permute-start | bytes 2359304 | tf_op jit(solution)/shard_map/ppermute | solution.py:150
  62.7 19.0 %collective-permute-start.13 = (bf16[768,512]{1,0:T(8,128)(2,1)S(1)}, bf16[768,512]{1,0:T(8,128)(2,1)S(1)}, u32[]{:S(2)}, u32[]{:S(2)}) collective-permute-start(bf16[768,512]{1,0:T(8,128)(2,1)S(1)} %get-tuple-element.101), channel_id=1, source_target_pairs={{0,4},{2,6},{4,0},{6,2},{8,12},{10,14},{12,8},{14,10},{16,20},{18,... | collective-permute-start | bytes 2359304 | tf_op jit(solution)/shard_map/ppermute | solution.py:146
  64.2 23.8 %collective-permute-start.17 = (bf16[512,1024]{1,0:T(8,128)(2,1)S(1)}, bf16[512,1024]{1,0:T(8,128)(2,1)S(1)}, u32[]{:S(2)}, u32[]{:S(2)}) collective-permute-start(bf16[512,1024]{1,0:T(8,128)(2,1)S(1)} %get-tuple-element.107), channel_id=1, source_target_pairs={{0,8},{2,10},{4,12},{6,14},{24,16},{26,18},{28,20},{30,22},{1,9},{... | collective-permute-start | bytes 3145736 | tf_op jit(solution)/shard_map/ppermute | solution.py:155
  82.6 20.2 %collective-permute-start.16 = (bf16[768,512]{1,0:T(8,128)(2,1)}, bf16[768,512]{1,0:T(8,128)(2,1)}, u32[]{:S(2)}, u32[]{:S(2)}) collective-permute-start(bf16[768,512]{1,0:T(8,128)(2,1)} %get-tuple-element.106.refs_0_.refs_2_), channel_id=1, source_target_pairs={{0,1},{1,0},{2,3},{3,2},{4,5},{5,4},{6,7},{7,6},{8,9},{9,8},{10,11... | collective-permute-start | bytes 2359304 | tf_op jit(solution)/shard_map/ppermute | solution.py:150
  89.8 16.3 %collective-permute-start.20 = (bf16[512,1024]{1,0:T(8,128)(2,1)}, bf16[512,1024]{1,0:T(8,128)(2,1)}, u32[]{:S(2)}, u32[]{:S(2)}) collective-permute-start(bf16[512,1024]{1,0:T(8,128)(2,1)} %get-tuple-element.113), channel_id=1, source_target_pairs={{16,8},{18,10},{20,12},{22,14},{24,16},{26,18},{28,20},{30,22},{17... | collective-permute-start | bytes 3145736 | tf_op jit(solution)/shard_map/ppermute | solution.py:155
  91.4 23.7 %collective-permute-start.19 = (bf16[512,1024]{1,0:T(8,128)(2,1)}, bf16[512,1024]{1,0:T(8,128)(2,1)}, u32[]{:S(2)}, u32[]{:S(2)}) collective-permute-start(bf16[512,1024]{1,0:T(8,128)(2,1)} %get-tuple-element.113), channel_id=1, source_target_pairs={{0,8},{2,10},{4,12},{6,14},{8,16},{10,18},{12,20},{14,22},{1,9},{3... | collective-permute-start | bytes 3145736 | tf_op jit(solution)/shard_map/ppermute | solution.py:155
  96.4 23.8 %collective-permute-start.21 = (bf16[512,1024]{1,0:T(8,128)(2,1)}, bf16[512,1024]{1,0:T(8,128)(2,1)}, u32[]{:S(2)}, u32[]{:S(2)}) collective-permute-start(bf16[512,1024]{1,0:T(8,128)(2,1)} %get-tuple-element.117), channel_id=1, source_target_pairs={{16,24},{18,26},{20,28},{22,30},{8,0},{10,2},{12,4},{14,6},{17,25}... | collective-permute-start | bytes 3145736 | tf_op jit(solution)/shard_map/ppermute | solution.py:155
  97.7 24.1 %collective-permute-start.18 = (bf16[768,512]{1,0:T(8,128)(2,1)}, bf16[768,512]{1,0:T(8,128)(2,1)S(1)}, u32[]{:S(2)}, u32[]{:S(2)}) collective-permute-start(bf16[768,512]{1,0:T(8,128)(2,1)} %copy-done.14), channel_id=1, source_target_pairs={{0,1},{1,0},{2,3},{3,2},{4,5},{5,4},{6,7},{7,6},{8,9},{9,8},{10,11... | collective-permute-start | bytes 2359304 | tf_op jit(solution)/shard_map/ppermute | solution.py:150
  127.3 24.6 %collective-permute-start.25 = (bf16[512,1024]{1,0:T(8,128)(2,1)S(1)}, bf16[512,1024]{1,0:T(8,128)(2,1)S(1)}, u32[]{:S(2)}, u32[]{:S(2)}) collective-permute-start(bf16[512,1024]{1,0:T(8,128)(2,1)S(1)} %get-tuple-element.126), channel_id=1, source_target_pairs={{0,8},{2,10},{4,12},{6,14},{8,16},{10,18},{12,20},{14,22},{16,24},... | collective-permute-start | bytes 3145736 | tf_op jit(solution)/shard_map/ppermute | solution.py:155
  128.7 28.5 %collective-permute-start.26 = (bf16[512,1024]{1,0:T(8,128)(2,1)S(1)}, bf16[512,1024]{1,0:T(8,128)(2,1)S(1)}, u32[]{:S(2)}, u32[]{:S(2)}) collective-permute-start(bf16[512,1024]{1,0:T(8,128)(2,1)S(1)} %get-tuple-element.127), channel_id=1, source_target_pairs={{8,0},{10,2},{12,4},{14,6},{16,8},{18,10},{20,12},{22,14},{24,16},... | collective-permute-start | bytes 3145736 | tf_op jit(solution)/shard_map/ppermute | solution.py:155
  133.8 25.7 %collective-permute-start.22 = (bf16[384,1024]{1,0:T(8,128)(2,1)S(1)}, bf16[384,1024]{1,0:T(8,128)(2,1)S(1)}, u32[]{:S(2)}, u32[]{:S(2)}) collective-permute-start(bf16[384,1024]{1,0:T(8,128)(2,1)S(1)} %get-tuple-element.121), channel_id=1, source_target_pairs={{0,2},{2,0},{4,6},{6,4},{8,10},{10,8},{12,14},{14,12},{16,18},{18,... | collective-permute-start | bytes 2359304 | tf_op jit(solution)/shard_map/ppermute | solution.py:143
  134.5 25.0 %collective-permute-start.24 = (bf16[384,1024]{1,0:T(8,128)(2,1)S(1)}, bf16[384,1024]{1,0:T(8,128)(2,1)S(1)}, u32[]{:S(2)}, u32[]{:S(2)}) collective-permute-start(bf16[384,1024]{1,0:T(8,128)(2,1)S(1)} %get-tuple-element.125), channel_id=1, source_target_pairs={{0,4},{2,6},{4,0},{6,2},{8,12},{10,14},{12,8},{14,10},{16,20},{18,... | collective-permute-start | bytes 2359304 | tf_op jit(solution)/shard_map/ppermute | solution.py:146
  (28 other events, 195.4 us)

commit v3 on v0

v3 whole, which is shorter than its diff:
```python
import functools

import jax
import jax.numpy as jnp
import numpy as np
from jax import lax
from jax.experimental import pallas as pl
from jax.experimental.pallas import tpu as pltpu
from jax.sharding import PartitionSpec as P

BF = jnp.bfloat16
F32 = jnp.float32


def orders(depth):
    def rank(z):
        return lambda d: (-abs(d - z), abs(2 * d - depth + 1))

    order = np.array([sorted(range(depth), key=rank(z)) for z in range(depth)])
    return order, np.argsort(order, axis=1)


def lookup(table, where):
    out = jnp.int32(int(table[0]))
    for i in range(1, len(table)):
        out = jnp.where(where == i, jnp.int32(int(table[i])), out)
    return out


def lookup(table, where):
    out = jnp.int32(int(table[0]))
    for i in range(1, len(table)):
        out = jnp.where(where == i, jnp.int32(int(table[i])), out)
    return out


def spot():
    f = lax.axis_index("fsdp")
    return lax.div(f, 4), lax.rem(lax.div(f, 2), 2), lax.rem(f, 2), lax.axis_index("tensor")


def norm_kernel(order, width, tokens, gain, token, *outs):
    layers = len(order)
    z, x, c, _ = spot()
    values = tokens[...].astype(F32)
    scale = lax.rsqrt(jnp.mean(values * values, axis=-1, keepdims=True) + 1e-05)
    for k in range(layers):
        own, far, swap = outs[k], outs[layers + k], outs[2 * layers + k]
        layer = lookup(order[:, k], z) * 4
        for out, rx, rc in [(own, 0, 0), (swap.at[0], 0, 1), (far, 1, 0), (swap.at[1], 1, 1)]:
            place = layer + jnp.bitwise_xor(x, rx) * 2 + jnp.bitwise_xor(c, rc)
            at = pl.ds(pl.multiple_of(place * width, width), width)
            part = tokens[:, at].astype(F32) * scale * gain[:, at].astype(F32)
            out[...] = part.astype(BF)


def normalize(tokens, gain, order, tile=64):
    layers = len(order)
    rows, features = tokens.shape
    width = features // (4 * layers)
    single = jax.ShapeDtypeStruct((rows, width), BF)
    pair = jax.ShapeDtypeStruct((2, rows, width), BF)
    token, *outs = pl.pallas_call(
        functools.partial(norm_kernel, order, width),
        out_shape=[jax.ShapeDtypeStruct((8, 128), F32)] + [single] * (2 * layers) + [pair] * layers,
        grid=(rows // tile,),
        in_specs=[
            pl.BlockSpec((tile, features), lambda i: (i, 0)),
            pl.BlockSpec((1, features), lambda i: (0, 0)),
        ],
        out_specs=[pl.BlockSpec(memory_space=pl.ANY)]
        + [pl.BlockSpec((tile, width), lambda i: (i, 0))] * (2 * layers)
        + [pl.BlockSpec((2, tile, width), lambda i: (0, i, 0))] * layers,
        compiler_params=pltpu.CompilerParams(vmem_limit_bytes=24 * 2**20),
        name="normalize",
    )(tokens, gain.reshape(1, features))
    return outs[:layers], outs[layers:2 * layers], outs[2 * layers:], token


def whole(shape):
    return pl.BlockSpec(shape, lambda i: (0,) * len(shape))


def at(shape, *where):
    return pl.BlockSpec(shape, lambda i: where)


HELD = pl.BlockSpec(memory_space=pl.ANY)
SCALARS = pl.BlockSpec(memory_space=pltpu.SMEM)


class Line:
    def __init__(self):
        self.token = None

    def run(self, name, jobs, through=(), grid=(1,)):
        n_in = sum(len(ins) for _, ins, _ in jobs)
        held = list(through) + ([] if self.token is None else [self.token])

        def body(*refs):
            outs = refs[n_in + len(held):]
            i = o = 0
            for kernel, ins, made in jobs:
                kernel(*refs[i:i + len(ins)], *outs[o:o + len(made)])
                i, o = i + len(ins), o + len(made)

        made = [out for _, _, outs in jobs for out in outs]
        result = pl.pallas_call(
            body,
            out_shape=[shape for shape, _ in made]
            + [jax.ShapeDtypeStruct(a.shape, a.dtype) for a in through] + [jax.ShapeDtypeStruct((8, 128), F32)],
            grid=grid,
            in_specs=[spec for _, ins, _ in jobs for _, spec in ins] + [HELD] * len(held),
            out_specs=[spec for _, spec in made] + [HELD] * (len(through) + 1),
            input_output_aliases={n_in + i: len(made) + i for i in range(len(through))},
            compiler_params=pltpu.CompilerParams(vmem_limit_bytes=32 * 2**20),
            cost_estimate=pl.CostEstimate(flops=0, bytes_accessed=1, transcendentals=0),
            name=name,
        )(*[a for _, ins, _ in jobs for a, _ in ins], *held)
        self.token = result[-1]
        return result[:len(made)], result[len(made):-1]


def new(shape, dtype=BF):
    return jax.ShapeDtypeStruct(shape, dtype), whole(shape)


def join(pieces):
    def kernel(*refs):
        ins, out = refs[:-1], refs[-1]
        row = 0
        for ref in ins:
            flat = ref.shape[-2:]
            out[row:row + flat[0], :] = ref[...].reshape(flat)
            row += flat[0]

    shape = (sum(block[-2] for _, block, _ in pieces), pieces[0][1][-1])
    return kernel, [(a, at(block, *where)) for a, block, where in pieces], [new(shape)]


def per_device(tokens, gain, kv_weight, block_mask, cotangent):
    group, teams = lax.axis_size("fsdp"), lax.axis_size("tensor")
    layers = group // 4
    rows, features = tokens.shape
    width = features // group
    cols = kv_weight.shape[1]
    flat, one, pair, panel = (rows, width), (1, rows, width), (2 * rows, width), (width, cols)
    mrows, mcols = block_mask.shape
    tall, wide = width // mrows, cols // mcols
    blocks = [
        ((i, j), (slice(i * tall, (i + 1) * tall), slice(j * wide, (j + 1) * wide)))
        for i in range(mrows) for j in range(mcols)
    ]
    order, place = orders(layers)
    line = Line()

    def over_core(a):
        return lax.ppermute(a, "fsdp", [(i, i ^ 1) for i in range(group)])

    def over_x(a):
        return lax.ppermute(a, "fsdp", [(i, i ^ 2) for i in range(group)])

    def over_y(a):
        return [
            lax.ppermute(a, "tensor", [(i, (i + s) % teams) for i in range(teams)])
            for s in range(1, teams)
        ]

    def over_z(a, pairs):
        return lax.ppermute(a, "fsdp", [(4 * p + i, 4 * q + i) for p, q in pairs for i in range(4)])

    def partner(p, side):
        q = p + 1 if p % 2 == side else p - 1
        return q if 0 <= q < layers else p

    def over_edges(a, side):
        return over_z(a, [(p, partner(p, side)) for p in range(layers)])

    own, far, swaps, line.token = normalize(tokens, gain, order)
    swaps = [over_core(a) for a in swaps]

    def near_of(k):
        return [(own[k], flat, (0, 0)), (swaps[k], one, (0, 0, 0))]

    def cross_of(k):
        return [(far[k], flat, (0, 0)), (swaps[k], one, (1, 0, 0))]

    (cross_0, near_0), _ = line.run("first", [join(cross_of(0)), join(near_of(0))])
    cross_0, near_y = over_x(cross_0), over_y(near_0)

    def turn_kernel(a, out):
        for i in range(teams):
            j = lax.rem(spot()[3] + teams - i, teams)
            out[i * rows:(i + 1) * rows, :] = a[pl.ds(pl.multiple_of(j * rows, rows), rows), :]

    def mask_kernel(mask, a, out):
        for spot_in, where in blocks:
            out[where] = (a[where].astype(F32) * mask[spot_in].astype(F32)).astype(BF)

    own_shape, cut = cotangent.shape, (cotangent.shape[0] // 2, cols)
    (cot, masked), _ = line.run(
        "turn_and_mask",
        [
            (turn_kernel, [(cotangent, whole(own_shape))], [new(own_shape)]),
            (mask_kernel, [(block_mask, SCALARS), (kv_weight, whole(panel))], [new(panel)]),
        ],
    )
    cot_x, cot_core = over_x(cot), over_core(cot)
    came = {1: [over_edges(masked, i) for i in range(2)]}

    _, (cross_0, cot_core, *near_y) = line.run("arrived", [], [cross_0, cot_core, *near_y])
    cross_y = over_y(cross_0)
    (near_rest,), _ = line.run("later", [join([p for k in range(1, layers) for p in near_of(k)])])
    (cross_1,), _ = line.run("later", [join(cross_of(1))])
    (rest,), _ = line.run("later", [join([p for k in range(2, layers) for p in cross_of(k)])])
    near_rest_y, cross_1 = over_y(near_rest), over_x(cross_1)

    def split_kernel(a, low, high):
        low[...] = a[:cut[0]]
        high[...] = a[cut[0]:]

    parts, (*cross_y, even, odd) = line.run(
        "split", [(split_kernel, [(cot_x, whole(own_shape))], [new(cut), new(cut)])], [*cross_y, *came[1]]
    )
    came[1] = [even, odd]
    parts = [over_core(part) for part in parts]
    came[2] = [None, over_edges(came[1][0], 1)]
    pieces = [(a, (rows, cols), (i, 0)) for i in range(teams) for a in (cot, cot_core)]
    for i in range(teams):
        pieces.append((cot_x, (rows, cols), (i, 0)))
        pieces.append((parts[2 * i // teams], (rows, cols), (i % (teams // 2), 0)))

    def gather(near, near_y, cross, cross_y, places):
        arrays = [(a, pair, (places[0], 0)) for a in [near, *near_y]]
        return join(arrays + [(a, pair, (places[1], 0)) for a in [cross, *cross_y]])

    def terms_of(a):
        return lax.dot_general(a, cots, (((0,), (0,)), ((), ())), preferred_element_type=F32)

    def going(t, side):
        before, cases = came[t - 1][1 - side], {}
        for p in range(layers):
            q = partner(p, side)
            ahead = layers - 1 - p if q > p else p
            behind = layers - 1 - ahead
            if q == p:
                continue
            if t <= behind + 1:
                cases.setdefault((None, True), []).append(p)
            else:
                far = p + (layers - t + 1) * (q - p)
                cases.setdefault((int(place[p, far]), behind > 0), []).append(p)
        if list(cases) == [(None, True)]:
            return None
        used = [k for k, _ in cases if k is not None]
        ins = [(terms[k], whole(panel)) for k in used] + [(before, whole(panel))]

        def kernel(*refs):
            out = refs[-1]
            for (k, add), layers_of in cases.items():
                @pl.when(functools.reduce(jnp.logical_or, [spot()[0] == p for p in layers_of]))
                def _():
                    if k is None:
                        out[...] = refs[-2][...]
                    elif add:
                        out[...] = (refs[used.index(k)][...] + refs[-2][...].astype(F32)).astype(BF)
                    else:
                        out[...] = refs[used.index(k)][...].astype(BF)

        return kernel, ins, [new(panel)]

    def phase(t, sides, through=()):
        jobs = [going(t, i) for i in sides]
        made, through = line.run("phase", [job for job in jobs if job], through)
        made = list(made)
        came.setdefault(t, [None, None])
        for i, job in zip(sides, jobs):
            came[t][i] = over_edges(made.pop(0) if job else came[t - 1][1 - i], i)
        return through

    (cots, normed_0), _ = line.run("head", [join(pieces), gather(near_0, near_y, cross_0, cross_y, (0, 0))])
    normed, terms = [normed_0], [terms_of(normed_0)]
    phase(2, [0])
    _, (cross_1, rest, *near_rest_y) = line.run("arrived", [], [cross_1, rest, *near_rest_y])
    cross_1_y, rest = over_y(cross_1), over_x(rest)
    (normed_1,), _ = line.run("rows", [gather(near_rest, near_rest_y, cross_1, cross_1_y, (0, 0))])
    normed.append(normed_1)
    terms.append(terms_of(normed_1))
    phase(3, [0, 1])
    if layers > 3:
        rest, _ = line.run("arrived", [join([(rest, pair, (k, 0))]) for k in range(layers - 2)])
    rest_y = [over_y(a) for a in rest]
    more, _ = line.run(
        "rows",
        [gather(near_rest, near_rest_y, rest[k - 2], rest_y[k - 2], (k - 1, 0)) for k in range(2, layers)],
    )
    normed += more
    terms += [terms_of(a) for a in more]
    for t in range(4, layers + 1):
        phase(t, [0, 1])

    def choose(k):
        cases = {}
        for i in range(layers):
            d = int(order[i, k])
            cases.setdefault((abs(d - i), (i - 1 if d < i else i) % 2 if d != i else 0), []).append(i)

        def kernel(*refs):
            out = refs[-1]
            for n, layers_of in enumerate(cases.values()):
                def copy(n=n):
                    out[...] = refs[n][...]

                if len(cases) == 1:
                    copy()
                else:
                    pl.when(functools.reduce(jnp.logical_or, [spot()[0] == i for i in layers_of]))(copy)

        return kernel, [(came[s][i] if s else masked, whole(panel)) for s, i in cases], [new(panel)]

    weight, _ = line.run("weights", [choose(k) for k in range(layers)])

    half = max(teams // 2, 1)
    part = (half * rows, cols)

    def project(side, h):
        def kernel(*refs):
            rows_of, weights, keep, send = refs[:layers], refs[layers:2 * layers], refs[-2], refs[-1]
            total = jnp.dot(rows_of[0][...], weights[0][...], preferred_element_type=F32)
            for k in range(1, layers):
                total += jnp.dot(rows_of[k][...], weights[k][...], preferred_element_type=F32)
            keep[...] = total[:rows]
            send[...] = total[rows:].astype(BF)

        ins = [(n, pl.BlockSpec(pair, lambda i: (side * teams + h * half + i, 0))) for n in normed]
        ins += [(w, whole(panel)) for w in weight]
        outs = [
            (jax.ShapeDtypeStruct(part, d), pl.BlockSpec((rows, cols), lambda i: (i, 0))) for d in (F32, BF)
        ]
        kept, sent = line.run("project", [(kernel, ins, outs)], grid=(half,))[0]
        return kept, over_core(sent)

    def add_kernel(kept, sent, out):
        out[...] = (kept[...] + sent[...].astype(F32)).astype(BF)

    halves = range(teams // half)
    theirs = [project(1, h) for h in halves]
    arrived = []
    mine = []
    for h in halves:
        (a,), _ = line.run("cross_sum", [(add_kernel, [(a, whole(part)) for a in theirs[h]], [new(part)])])
        arrived.append(over_x(a))
        mine.append(project(0, h))

    def own_kernel(mask, term, even, odd, out):
        z = spot()[0]
        last = [jnp.where((z > 0) & (z < layers - 1), 1.0, 0.0).astype(F32), jnp.float32(1)]
        for spot_in, where in blocks:
            total = term[where]
            for i, a in enumerate([even, odd]):
                alone = partner(0, i) == 0
                total += a[where].astype(F32) * last[0] if alone else a[where].astype(F32)
            out[where] = total * mask[spot_in].astype(F32)

    ins = [(block_mask, SCALARS)] + [(a, whole(panel)) for a in [terms[layers - 1], *came[layers]]]
    (weight_grad,), _ = line.run("own_gradient", [(own_kernel, ins, [new(panel, F32)])])

    def last_sum(*refs):
        out = refs[-1]
        for h in halves:
            kept, sent, a = refs[3 * h:3 * h + 3]
            total = (kept[...] + sent[...].astype(F32) + a[...].astype(F32)).astype(BF)
            for i in range(half):
                j = lax.rem(spot()[3] + teams - h * half - i, teams)
                out[pl.ds(pl.multiple_of(j * rows, rows), rows), :] = total[i * rows:(i + 1) * rows]

    ins = [(a, whole(part)) for h in halves for a in (*mine[h], arrived[h])]
    (projected,), _ = line.run("projected", [(last_sum, ins, [new((teams * rows, cols))])])
    return (projected, weight_grad)


def solution(mesh):
    return jax.shard_map(
        per_device,
        mesh=mesh,
        in_specs=(
            P(("fsdp", "tensor"), None),
            P(),
            P("fsdp", "tensor"),
            P("fsdp", "tensor"),
            P("fsdp", "tensor"),
        ),
        out_specs=(P("fsdp", "tensor"), P("fsdp", "tensor")),
        check_vma=False,
    )
```

time: 573 us -> 134 us (0.23)
  waiting for transfers between devices: 473 us -> 76.1 us
  matrix products: 45.5 us -> 7.37 us
  starting transfers between devices: 0.12 us -> 30.5 us
  blocking collectives: 22.1 us -> 0 us
  Pallas kernels: 0 us -> 15.3 us
  between operations: 13.8 us -> 0.95 us
  other arithmetic: 11.4 us -> 0 us
    reduce_scatter x1 -> x0, waiting for transfers between devices: 303 us -> none  [per_device(): lax.psum_scatter(lax.dot_general(columns, cotangent, (((0,), (0,)), ((),...]
    all_gather x2 -> x0, waiting for transfers between devices: 170 us -> none  [the longest x1 87.3 us: per_device(): lax.all_gather(kv_weight, 'fsdp', axis=0, tiled=True)]
    ppermute x0 -> x31, waiting for transfers between devices: none -> 76.1 us  [the longest x6 38.5 us: over_y(): lax.ppermute(a, 'tensor', [(i, (i + s) % teams) for i in range(teams)])]
    dot_general x2 -> x4, matrix products: 45.5 us -> 7.37 us  [terms_of(): lax.dot_general(a, cots, (((0,), (0,)), ((), ())), preferred_element_type...]
    ppermute x0 -> x31, starting transfers between devices: none -> 30.5 us  [the longest x8 12.6 us: over_z(): lax.ppermute(a, 'fsdp', [(4 * p + i, 4 * q + i) for p, q in pairs for i i...]
    all_gather x1 -> x0, blocking collectives: 22.1 us -> none  [per_device(): lax.all_gather(block_mask, 'fsdp', axis=0, tiled=True)]
    pallas_call x0 -> x25, Pallas kernels: none -> 15.3 us  [the longest x24 13.6 us: run(): pl.pallas_call(body, out_shape=[shape for shape, _ in made] + [jax.ShapeD...]
    mul x2 -> x0, local copies, waits for them, and re-layouts: 6.26 us -> none  [apply_mask(): kept = shaped * mask[:, None, :, None].astype(panel.dtype)]
  transfers between devices with their start and end apart: 3 -> 31, of which waited for: 3 -> 12; matrix products, arithmetic and copies ran while one was open for 9% -> 6% of each run, Pallas kernels for 0% -> 9%
where the time goes in v3:
time: 134 us; the launch traced here: 133 us
  waiting for transfers between devices  76.1 us (57%)
  starting transfers between devices  30.5 us (23%)
  Pallas kernels  15.3 us (11%)
  matrix products  7.37 us (6%)
  local copies, waits for them, and re-layouts  2.63 us (2%)
    ppermute x6, waiting for transfers between devices, over_y(): lax.ppermute(a, 'tensor', [(i, (i + s) % teams) for i in range(teams)])  38.5 us
    ppermute x6, waiting for transfers between devices, over_x(): return lax.ppermute(a, 'fsdp', [(i, i ^ 2) for i in range(group)])  24.7 us
    pallas_call x24, Pallas kernels, run(): pl.pallas_call(body, out_shape=[shape for shape, _ in made] + [jax.ShapeD...  13.6 us
    ppermute x8, starting transfers between devices, over_z(): lax.ppermute(a, 'fsdp', [(4 * p + i, 4 * q + i) for p, q in pairs for i i...  12.6 us
    ppermute x8, waiting for transfers between devices, over_z(): lax.ppermute(a, 'fsdp', [(4 * p + i, 4 * q + i) for p, q in pairs for i i...  10.4 us
    ppermute x6, starting transfers between devices, over_y(): lax.ppermute(a, 'tensor', [(i, (i + s) % teams) for i in range(teams)])  8.42 us
    dot_general x4, matrix products, terms_of(): lax.dot_general(a, cots, (((0,), (0,)), ((), ())), preferred_element_type...  7.37 us
    ppermute x6, starting transfers between devices, over_x(): return lax.ppermute(a, 'fsdp', [(i, i ^ 2) for i in range(group)])  6.53 us
  transfers between devices with their start and end apart: 31, of which 12 were waited for; matrix products, arithmetic and copies ran while one was open for 6% of the time, Pallas kernels for 9%

profile of v3, /device:TPU:0, one launch (start us, length us, event | category | flops | bytes accessed | tf_op | source)
XLA Modules:
  0.0 132.8 jit_solution(8712568401539582566)
XLA Ops:
  1.4 1.9 %copy-done = bf16[192,8192]{1,0:T(8,128)(2,1)S(1)} copy-done((bf16[192,8192]{1,0:T(8,128)(2,1)S(1)}, bf16[192,8192]{1,0:T(8,128)(2,1)}, u32[]{:S(2)}) %copy-start) | copy-done | bytes 3145752
  8.3 2.7 %collective-permute-start.3 = (bf16[384,512]{1,0:T(8,128)(2,1)S(1)}, bf16[384,512]{1,0:T(8,128)(2,1)S(1)}, u32[]{:S(2)}, u32[]{:S(2)}) collective-permute-start(bf16[384,512]{1,0:T(8,128)(2,1)S(1)} %get-tuple-element.91.refs_8_), channel_id=1, source_target_pairs={{0,1},{1,0},{2,3},{3,2},{4,5},{5,4},{6,7},{7,6},{8,9},{9,8},{10,11... | collective-permute-start | bytes 1179656 | tf_op jit(solution)/shard_map/ppermute | solution.py:165
  14.7 5.8 %collective-permute-done.3.refs_2_ = bf16[384,512]{1,0:T(8,128)(2,1)S(1)} collective-permute-done((bf16[384,512]{1,0:T(8,128)(2,1)S(1)}, bf16[384,512]{1,0:T(8,128)(2,1)S(1)}, u32[]{:S(2)}, u32[]{:S(2)}) %collective-permute-start.3) | collective-permute-done | bytes 393248 | tf_op jit(solution)/shard_map/ppermute | solution.py:165
  26.3 13.5 %collective-permute-done.4.refs_0_.refs_4_.refs_6_ = bf16[384,1024]{1,0:T(8,128)(2,1)S(1)} collective-permute-done((bf16[384,1024]{1,0:T(8,128)(2,1)S(1)}, bf16[384,1024]{1,0:T(8,128)(2,1)S(1)}, u32[]{:S(2)}, u32[]{:S(2)}) %collective-permute-start.4) | collective-permute-done | bytes 786464 | tf_op jit(solution)/shard_map/ppermute | solution.py:161
  43.0 1.8 %fusion.refs_0_.refs_2_ = f32[512,1024]{1,0:T(8,128)S(1)} fusion(bf16[1536,512]{1,0:T(8,128)(2,1)S(1)} %get-tuple-element.114.refs_0_, bf16[1536,1024]{1,0:T(8,128)(2,1)S(1)} %get-tuple-element.118), kind=kOutput, calls=%fused_computation | convolution fusion | flops 1610612736 | bytes 6815744 | tf_op jit(solution)/shard_map/dot_general | solution.py:238
  45.0 4.4 %collective-permute-start.18 = (bf16[512,1024]{1,0:T(8,128)(2,1)S(1)}, bf16[512,1024]{1,0:T(8,128)(2,1)S(1)}, u32[]{:S(2)}, u32[]{:S(2)}) collective-permute-start(bf16[512,1024]{1,0:T(8,128)(2,1)S(1)} %get-tuple-element.128), channel_id=1, source_target_pairs={{0,8},{2,10},{4,12},{6,14},{8,0},{10,2},{12,4},{14,6},{16,24},{18,... | collective-permute-start | bytes 3145736 | tf_op jit(solution)/shard_map/ppermute | solution.py:170
  49.4 2.2 %collective-permute-done.13.refs_0_ = bf16[384,512]{1,0:T(8,128)(2,1)S(1)} collective-permute-done((bf16[384,512]{1,0:T(8,128)(2,1)S(1)}, bf16[384,512]{1,0:T(8,128)(2,1)S(1)}, u32[]{:S(2)}, u32[]{:S(2)}) %collective-permute-start.13) | collective-permute-done | bytes 393248 | tf_op jit(solution)/shard_map/ppermute | solution.py:161
  51.6 8.9 %collective-permute-done.14.refs_2_ = bf16[1152,512]{1,0:T(8,128)(2,1)S(1)} collective-permute-done((bf16[1152,512]{1,0:T(8,128)(2,1)S(1)}, bf16[1152,512]{1,0:T(8,128)(2,1)S(1)}, u32[]{:S(2)}, u32[]{:S(2)}) %collective-permute-start.14) | collective-permute-done | bytes 1179680 | tf_op jit(solution)/shard_map/ppermute | solution.py:165
  62.5 8.3 %collective-permute-done.15.refs_3_ = bf16[384,512]{1,0:T(8,128)(2,1)S(1)} collective-permute-done((bf16[384,512]{1,0:T(8,128)(2,1)S(1)}, bf16[384,512]{1,0:T(8,128)(2,1)S(1)}, u32[]{:S(2)}, u32[]{:S(2)}) %collective-permute-start.15) | collective-permute-done | bytes 393248 | tf_op jit(solution)/shard_map/ppermute | solution.py:165
  70.9 1.8 %fusion.1.refs_0_.refs_3_ = f32[512,1024]{1,0:T(8,128)S(1)} fusion(bf16[1536,512]{1,0:T(8,128)(2,1)S(1)} %get-tuple-element.125.refs_1_, bf16[1536,1024]{1,0:T(8,128)(2,1)S(1)} %get-tuple-element.118), kind=kOutput, calls=%fused_computation.1 | convolution fusion | flops 1610612736 | bytes 6815744 | tf_op jit(solution)/shard_map/dot_general | solution.py:238
  72.9 1.8 %collective-permute-start.21 = (bf16[512,1024]{1,0:T(8,128)(2,1)S(1)}, bf16[512,1024]{1,0:T(8,128)(2,1)S(1)}, u32[]{:S(2)}, u32[]{:S(2)}) collective-permute-start(bf16[512,1024]{1,0:T(8,128)(2,1)S(1)} %get-tuple-element.136), channel_id=1, source_target_pairs={{0,8},{2,10},{4,12},{6,14},{8,0},{10,2},{12,4},{14,6},{16,24},{18,... | collective-permute-start | bytes 3145736 | tf_op jit(solution)/shard_map/ppermute | solution.py:170
  75.4 5.1 %collective-permute-done.16.refs_0_.refs_1_ = bf16[768,512]{1,0:T(8,128)(2,1)S(1)} collective-permute-done((bf16[768,512]{1,0:T(8,128)(2,1)S(1)}, bf16[768,512]{1,0:T(8,128)(2,1)S(1)}, u32[]{:S(2)}, u32[]{:S(2)}) %collective-permute-start.16) | collective-permute-done | bytes 786464 | tf_op jit(solution)/shard_map/ppermute | solution.py:161
  82.6 10.0 %collective-permute-done.19.refs_3_ = bf16[384,512]{1,0:T(8,128)(2,1)S(1)} collective-permute-done((bf16[384,512]{1,0:T(8,128)(2,1)S(1)}, bf16[384,512]{1,0:T(8,128)(2,1)S(1)}, u32[]{:S(2)}, u32[]{:S(2)}) %collective-permute-start.19) | collective-permute-done | bytes 393248 | tf_op jit(solution)/shard_map/ppermute | solution.py:165
  92.6 5.5 %collective-permute-done.20.refs_7_ = bf16[384,512]{1,0:T(8,128)(2,1)S(1)} collective-permute-done((bf16[384,512]{1,0:T(8,128)(2,1)S(1)}, bf16[384,512]{1,0:T(8,128)(2,1)S(1)}, u32[]{:S(2)}, u32[]{:S(2)}) %collective-permute-start.20) | collective-permute-done | bytes 393248 | tf_op jit(solution)/shard_map/ppermute | solution.py:165
  98.3 1.8 %fusion.2.refs_0_.refs_1_ = f32[512,1024]{1,0:T(8,128)S(1)} fusion(bf16[1536,512]{1,0:T(8,128)(2,1)S(1)} %get-tuple-element.134.refs_2_, bf16[1536,1024]{1,0:T(8,128)(2,1)S(1)} %get-tuple-element.118), kind=kOutput, calls=%fused_computation.2 | convolution fusion | flops 1610612736 | bytes 6815744 | tf_op jit(solution)/shard_map/dot_general | solution.py:238
  100.3 2.0 %collective-permute-start.29 = (bf16[512,1024]{1,0:T(8,128)(2,1)S(1)}, bf16[512,1024]{1,0:T(8,128)(2,1)S(1)}, u32[]{:S(2)}, u32[]{:S(2)}) collective-permute-start(bf16[512,1024]{1,0:T(8,128)(2,1)S(1)} %get-tuple-element.160), channel_id=1, source_target_pairs={{0,8},{2,10},{4,12},{6,14},{8,0},{10,2},{12,4},{14,6},{16,24},{18,... | collective-permute-start | bytes 3145736 | tf_op jit(solution)/shard_map/ppermute | solution.py:170
  103.5 1.8 %project.4 = (f32[192,1024]{1,0:T(8,128)S(1)}, bf16[192,1024]{1,0:T(8,128)(2,1)S(1)}, f32[8,128]{1,0:T(8,128)S(1)}) custom-call(bf16[1536,512]{1,0:T(8,128)(2,1)S(1)} %get-tuple-element.114.refs_0_, bf16[1536,512]{1,0:T(8,128)(2,1)S(1)} %get-tuple-element.125.refs_1_, bf16[1536,512]{1,0:T(8,128)(2,1)S(1)} %get-tuple-element.134.refs_2_, ...), custom_call_target="tpu_custom_call" | custom-call | bytes 1 | tf_op jit(solution)/shard_map/project/pallas_call | solution.py:108
  105.4 1.8 %project.5 = (f32[192,1024]{1,0:T(8,128)S(1)}, bf16[192,1024]{1,0:T(8,128)(2,1)S(1)}, f32[8,128]{1,0:T(8,128)S(1)}) custom-call(bf16[1536,512]{1,0:T(8,128)(2,1)S(1)} %get-tuple-element.114.refs_0_, bf16[1536,512]{1,0:T(8,128)(2,1)S(1)} %get-tuple-element.125.refs_1_, bf16[1536,512]{1,0:T(8,128)(2,1)S(1)} %get-tuple-element.134.refs_2_, ...), custom_call_target="tpu_custom_call" | custom-call | bytes 1 | tf_op jit(solution)/shard_map/project/pallas_call | solution.py:108
  107.9 1.8 %project.6 = (f32[192,1024]{1,0:T(8,128)S(1)}, bf16[192,1024]{1,0:T(8,128)(2,1)S(1)}, f32[8,128]{1,0:T(8,128)S(1)}) custom-call(bf16[1536,512]{1,0:T(8,128)(2,1)S(1)} %get-tuple-element.114.refs_0_, bf16[1536,512]{1,0:T(8,128)(2,1)S(1)} %get-tuple-element.125.refs_1_, bf16[1536,512]{1,0:T(8,128)(2,1)S(1)} %get-tuple-element.134.refs_2_, ...), custom_call_target="tpu_custom_call" | custom-call | bytes 1 | tf_op jit(solution)/shard_map/project/pallas_call | solution.py:108
  109.8 1.8 %project.7 = (f32[192,1024]{1,0:T(8,128)S(1)}, bf16[192,1024]{1,0:T(8,128)(2,1)S(1)}, f32[8,128]{1,0:T(8,128)S(1)}) custom-call(bf16[1536,512]{1,0:T(8,128)(2,1)S(1)} %get-tuple-element.114.refs_0_, bf16[1536,512]{1,0:T(8,128)(2,1)S(1)} %get-tuple-element.125.refs_1_, bf16[1536,512]{1,0:T(8,128)(2,1)S(1)} %get-tuple-element.134.refs_2_, ...), custom_call_target="tpu_custom_call" | custom-call | bytes 1 | tf_op jit(solution)/shard_map/project/pallas_call | solution.py:108
  112.5 10.3 %collective-permute-done.29.refs_2_ = bf16[512,1024]{1,0:T(8,128)(2,1)S(1)} collective-permute-done((bf16[512,1024]{1,0:T(8,128)(2,1)S(1)}, bf16[512,1024]{1,0:T(8,128)(2,1)S(1)}, u32[]{:S(2)}, u32[]{:S(2)}) %collective-permute-start.29) | collective-permute-done | bytes 1048608 | tf_op jit(solution)/shard_map/ppermute | solution.py:170
  123.6 1.8 %fusion.3.refs_1_ = f32[512,1024]{1,0:T(8,128)S(1)} fusion(bf16[1536,512]{1,0:T(8,128)(2,1)S(1)} %get-tuple-element.135.refs_3_, bf16[1536,1024]{1,0:T(8,128)(2,1)S(1)} %get-tuple-element.118), kind=kOutput, calls=%fused_computation.3 | convolution fusion | flops 1610612736 | bytes 6815744 | tf_op jit(solution)/shard_map/dot_general | solution.py:238
  125.4 2.3 %own_gradient.1 = (f32[512,1024]{1,0:T(8,128)}, f32[8,128]{1,0:T(8,128)S(1)}) custom-call(s32[4,8]{1,0:T(4,128)S(1)} %copy-done.3, f32[512,1024]{1,0:T(8,128)S(1)} %fusion.3.refs_1_, bf16[512,1024]{1,0:T(8,128)(2,1)S(1)} %collective-permute-done.29.refs_2_, bf16[512,1024]{1,0:T(8,128)(2,1)S(1)} %collective-permute-done.30.refs_3_, ...), custom_call_target="tpu_custom_call" | custom-call | bytes 1 | tf_op jit(solution)/shard_map/own_gradient/pallas_call | solution.py:108
  127.8 3.9 %collective-permute-done.25.refs_2_ = bf16[192,1024]{1,0:T(8,128)(2,1)S(1)} collective-permute-done((bf16[192,1024]{1,0:T(8,128)(2,1)S(1)}, bf16[192,1024]{1,0:T(8,128)(2,1)S(1)}, u32[]{:S(2)}, u32[]{:S(2)}) %collective-permute-start.25) | collective-permute-done | bytes 393248 | tf_op jit(solution)/shard_map/ppermute | solution.py:161
  (76 shorter events, 28.7 us)
Async XLA Ops:
  5.5 8.5 %collective-permute-start.10 = (bf16[2,192,512]{2,1,0:T(8,128)(2,1)S(1)}, bf16[2,192,512]{2,1,0:T(8,128)(2,1)S(1)}, u32[]{:S(2)}, u32[]{:S(2)}) collective-permute-start(bf16[2,192,512]{2,1,0:T(8,128)(2,1)S(1)} %get-tuple-element.101), channel_id=1, source_target_pairs={{0,2},{2,0},{4,6},{6,4},{8,10},{10,8},{12,14},{14,12},{16,18},{18,... | collective-permute-start | bytes 1179656 | tf_op jit(solution)/shard_map/ppermute | solution.py:158
  7.8 14.5 %collective-permute-start.2 = (bf16[384,1024]{1,0:T(8,128)(2,1)S(1)}, bf16[384,1024]{1,0:T(8,128)(2,1)S(1)}, u32[]{:S(2)}, u32[]{:S(2)}) collective-permute-start(bf16[384,1024]{1,0:T(8,128)(2,1)S(1)} %get-tuple-element.89.refs_0_.refs_2_), channel_id=1, source_target_pairs={{0,2},{2,0},{4,6},{6,4},{8,10},{10,8},{12,14},{14,12},{16,18},{18,... | collective-permute-start | bytes 2359304 | tf_op jit(solution)/shard_map/ppermute | solution.py:158
  8.3 12.3 %collective-permute-start.3 = (bf16[384,512]{1,0:T(8,128)(2,1)S(1)}, bf16[384,512]{1,0:T(8,128)(2,1)S(1)}, u32[]{:S(2)}, u32[]{:S(2)}) collective-permute-start(bf16[384,512]{1,0:T(8,128)(2,1)S(1)} %get-tuple-element.91.refs_8_), channel_id=1, source_target_pairs={{0,1},{1,0},{2,3},{3,2},{4,5},{5,4},{6,7},{7,6},{8,9},{9,8},{10,11... | collective-permute-start | bytes 1179656 | tf_op jit(solution)/shard_map/ppermute | solution.py:165
  10.9 11.4 %collective-permute-start.1 = (bf16[384,512]{1,0:T(8,128)(2,1)S(1)}, bf16[384,512]{1,0:T(8,128)(2,1)S(1)}, u32[]{:S(2)}, u32[]{:S(2)}) collective-permute-start(bf16[384,512]{1,0:T(8,128)(2,1)S(1)} %get-tuple-element.90), channel_id=1, source_target_pairs={{0,4},{2,6},{4,0},{6,2},{8,12},{10,14},{12,8},{14,10},{16,20},{18,... | collective-permute-start | bytes 1179656 | tf_op jit(solution)/shard_map/ppermute | solution.py:161
  12.4 27.4 %collective-permute-start.6 = (bf16[512,1024]{1,0:T(8,128)(2,1)S(1)}, bf16[512,1024]{1,0:T(8,128)(2,1)S(1)}, u32[]{:S(2)}, u32[]{:S(2)}) collective-permute-start(bf16[512,1024]{1,0:T(8,128)(2,1)S(1)} %get-tuple-element.95.refs_5_), channel_id=1, source_target_pairs={{0,8},{2,10},{4,12},{6,14},{8,0},{10,2},{12,4},{14,6},{16,24},{18,... | collective-permute-start | bytes 3145736 | tf_op jit(solution)/shard_map/ppermute | solution.py:170
  14.0 25.8 %collective-permute-start.7 = (bf16[512,1024]{1,0:T(8,128)(2,1)S(1)}, bf16[512,1024]{1,0:T(8,128)(2,1)S(1)}, u32[]{:S(2)}, u32[]{:S(2)}) collective-permute-start(bf16[512,1024]{1,0:T(8,128)(2,1)S(1)} %get-tuple-element.95.refs_5_), channel_id=1, source_target_pairs={{0,0},{2,2},{4,4},{6,6},{8,16},{10,18},{12,20},{14,22},{16,8},{18,... | collective-permute-start | bytes 3145736 | tf_op jit(solution)/shard_map/ppermute | solution.py:170
  20.6 19.2 %collective-permute-start.4 = (bf16[384,1024]{1,0:T(8,128)(2,1)S(1)}, bf16[384,1024]{1,0:T(8,128)(2,1)S(1)}, u32[]{:S(2)}, u32[]{:S(2)}) collective-permute-start(bf16[384,1024]{1,0:T(8,128)(2,1)S(1)} %get-tuple-element.89.refs_0_.refs_2_), channel_id=1, source_target_pairs={{0,4},{2,6},{4,0},{6,2},{8,12},{10,14},{12,8},{14,10},{16,20},{18,... | collective-permute-start | bytes 2359304 | tf_op jit(solution)/shard_map/ppermute | solution.py:161
  24.0 15.8 %collective-permute-start.5 = (bf16[384,512]{1,0:T(8,128)(2,1)S(1)}, bf16[384,512]{1,0:T(8,128)(2,1)S(1)}, u32[]{:S(2)}, u32[]{:S(2)}) collective-permute-start(bf16[384,512]{1,0:T(8,128)(2,1)S(1)} %get-tuple-element.94.refs_10_), channel_id=1, source_target_pairs={{0,1},{1,0},{2,3},{3,2},{4,5},{5,4},{6,7},{7,6},{8,9},{9,8},{10,11... | collective-permute-start | bytes 1179656 | tf_op jit(solution)/shard_map/ppermute | solution.py:165
  25.6 34.8 %collective-permute-start.14 = (bf16[1152,512]{1,0:T(8,128)(2,1)S(1)}, bf16[1152,512]{1,0:T(8,128)(2,1)S(1)}, u32[]{:S(2)}, u32[]{:S(2)}) collective-permute-start(bf16[1152,512]{1,0:T(8,128)(2,1)S(1)} %get-tuple-element.115.refs_0_.refs_4_), channel_id=1, source_target_pairs={{0,1},{1,0},{2,3},{3,2},{4,5},{5,4},{6,7},{7,6},{8,9},{9,8},{10,11... | collective-permute-start | bytes 3538952 | tf_op jit(solution)/shard_map/ppermute | solution.py:165
  40.5 11.1 %collective-permute-start.13 = (bf16[384,512]{1,0:T(8,128)(2,1)S(1)}, bf16[384,512]{1,0:T(8,128)(2,1)S(1)}, u32[]{:S(2)}, u32[]{:S(2)}) collective-permute-start(bf16[384,512]{1,0:T(8,128)(2,1)S(1)} %get-tuple-element.116), channel_id=1, source_target_pairs={{0,4},{2,6},{4,0},{6,2},{8,12},{10,14},{12,8},{14,10},{16,20},{18,... | collective-permute-start | bytes 1179656 | tf_op jit(solution)/shard_map/ppermute | solution.py:161
  42.0 30.8 %collective-permute-start.17 = (bf16[512,1024]{1,0:T(8,128)(2,1)S(1)}, bf16[512,1024]{1,0:T(8,128)(2,1)S(1)}, u32[]{:S(2)}, u32[]{:S(2)}) collective-permute-start(bf16[512,1024]{1,0:T(8,128)(2,1)S(1)} %get-tuple-element.127.refs_4_), channel_id=1, source_target_pairs={{0,0},{2,2},{4,4},{6,6},{8,16},{10,18},{12,20},{14,22},{16,8},{18,... | collective-permute-start | bytes 3145736 | tf_op jit(solution)/shard_map/ppermute | solution.py:170
  45.0 27.8 %collective-permute-start.18 = (bf16[512,1024]{1,0:T(8,128)(2,1)S(1)}, bf16[512,1024]{1,0:T(8,128)(2,1)S(1)}, u32[]{:S(2)}, u32[]{:S(2)}) collective-permute-start(bf16[512,1024]{1,0:T(8,128)(2,1)S(1)} %get-tuple-element.128), channel_id=1, source_target_pairs={{0,8},{2,10},{4,12},{6,14},{8,0},{10,2},{12,4},{14,6},{16,24},{18,... | collective-permute-start | bytes 3145736 | tf_op jit(solution)/shard_map/ppermute | solution.py:170
  60.5 10.3 %collective-permute-start.15 = (bf16[384,512]{1,0:T(8,128)(2,1)S(1)}, bf16[384,512]{1,0:T(8,128)(2,1)S(1)}, u32[]{:S(2)}, u32[]{:S(2)}) collective-permute-start(bf16[384,512]{1,0:T(8,128)(2,1)S(1)} %get-tuple-element.123.refs_2_), channel_id=1, source_target_pairs={{0,1},{1,0},{2,3},{3,2},{4,5},{5,4},{6,7},{7,6},{8,9},{9,8},{10,11... | collective-permute-start | bytes 1179656 | tf_op jit(solution)/shard_map/ppermute | solution.py:165
  62.0 18.5 %collective-permute-start.16 = (bf16[768,512]{1,0:T(8,128)(2,1)S(1)}, bf16[768,512]{1,0:T(8,128)(2,1)S(1)}, u32[]{:S(2)}, u32[]{:S(2)}) collective-permute-start(bf16[768,512]{1,0:T(8,128)(2,1)S(1)} %get-tuple-element.126), channel_id=1, source_target_pairs={{0,4},{2,6},{4,0},{6,2},{8,12},{10,14},{12,8},{14,10},{16,20},{18,... | collective-permute-start | bytes 2359304 | tf_op jit(solution)/shard_map/ppermute | solution.py:161
  72.9 27.3 %collective-permute-start.21 = (bf16[512,1024]{1,0:T(8,128)(2,1)S(1)}, bf16[512,1024]{1,0:T(8,128)(2,1)S(1)}, u32[]{:S(2)}, u32[]{:S(2)}) collective-permute-start(bf16[512,1024]{1,0:T(8,128)(2,1)S(1)} %get-tuple-element.136), channel_id=1, source_target_pairs={{0,8},{2,10},{4,12},{6,14},{8,0},{10,2},{12,4},{14,6},{16,24},{18,... | collective-permute-start | bytes 3145736 | tf_op jit(solution)/shard_map/ppermute | solution.py:170
  74.7 25.5 %collective-permute-start.22 = (bf16[512,1024]{1,0:T(8,128)(2,1)S(1)}, bf16[512,1024]{1,0:T(8,128)(2,1)S(1)}, u32[]{:S(2)}, u32[]{:S(2)}) collective-permute-start(bf16[512,1024]{1,0:T(8,128)(2,1)S(1)} %get-tuple-element.137), channel_id=1, source_target_pairs={{0,0},{2,2},{4,4},{6,6},{8,16},{10,18},{12,20},{14,22},{16,8},{18,... | collective-permute-start | bytes 3145736 | tf_op jit(solution)/shard_map/ppermute | solution.py:170
  80.5 12.1 %collective-permute-start.19 = (bf16[384,512]{1,0:T(8,128)(2,1)S(1)}, bf16[384,512]{1,0:T(8,128)(2,1)S(1)}, u32[]{:S(2)}, u32[]{:S(2)}) collective-permute-start(bf16[384,512]{1,0:T(8,128)(2,1)S(1)} %get-tuple-element.131.refs_2_), channel_id=1, source_target_pairs={{0,1},{1,0},{2,3},{3,2},{4,5},{5,4},{6,7},{7,6},{8,9},{9,8},{10,11... | collective-permute-start | bytes 1179656 | tf_op jit(solution)/shard_map/ppermute | solution.py:165
  81.1 17.0 %collective-permute-start.20 = (bf16[384,512]{1,0:T(8,128)(2,1)S(1)}, bf16[384,512]{1,0:T(8,128)(2,1)S(1)}, u32[]{:S(2)}, u32[]{:S(2)}) collective-permute-start(bf16[384,512]{1,0:T(8,128)(2,1)S(1)} %get-tuple-element.132.refs_6_), channel_id=1, source_target_pairs={{0,1},{1,0},{2,3},{3,2},{4,5},{5,4},{6,7},{7,6},{8,9},{9,8},{10,11... | collective-permute-start | bytes 1179656 | tf_op jit(solution)/shard_map/ppermute | solution.py:165
  100.3 22.5 %collective-permute-start.29 = (bf16[512,1024]{1,0:T(8,128)(2,1)S(1)}, bf16[512,1024]{1,0:T(8,128)(2,1)S(1)}, u32[]{:S(2)}, u32[]{:S(2)}) collective-permute-start(bf16[512,1024]{1,0:T(8,128)(2,1)S(1)} %get-tuple-element.160), channel_id=1, source_target_pairs={{0,8},{2,10},{4,12},{6,14},{8,0},{10,2},{12,4},{14,6},{16,24},{18,... | collective-permute-start | bytes 3145736 | tf_op jit(solution)/shard_map/ppermute | solution.py:170
  102.3 23.1 %collective-permute-start.30 = (bf16[512,1024]{1,0:T(8,128)(2,1)S(1)}, bf16[512,1024]{1,0:T(8,128)(2,1)S(1)}, u32[]{:S(2)}, u32[]{:S(2)}) collective-permute-start(bf16[512,1024]{1,0:T(8,128)(2,1)S(1)} %get-tuple-element.161), channel_id=1, source_target_pairs={{0,0},{2,2},{4,4},{6,6},{8,16},{10,18},{12,20},{14,22},{16,8},{18,... | collective-permute-start | bytes 3145736 | tf_op jit(solution)/shard_map/ppermute | solution.py:170
  111.7 16.1 %collective-permute-start.27 = (bf16[192,1024]{1,0:T(8,128)(2,1)S(1)}, bf16[192,1024]{1,0:T(8,128)(2,1)S(1)}, u32[]{:S(2)}, u32[]{:S(2)}) collective-permute-start(bf16[192,1024]{1,0:T(8,128)(2,1)S(1)} %get-tuple-element.158), channel_id=1, source_target_pairs={{0,2},{2,0},{4,6},{6,4},{8,10},{10,8},{12,14},{14,12},{16,18},{18,... | collective-permute-start | bytes 1179656 | tf_op jit(solution)/shard_map/ppermute | solution.py:158
  111.7 16.0 %collective-permute-start.28 = (bf16[192,1024]{1,0:T(8,128)(2,1)S(1)}, bf16[192,1024]{1,0:T(8,128)(2,1)S(1)}, u32[]{:S(2)}, u32[]{:S(2)}) collective-permute-start(bf16[192,1024]{1,0:T(8,128)(2,1)S(1)} %get-tuple-element.159), channel_id=1, source_target_pairs={{0,4},{2,6},{4,0},{6,2},{8,12},{10,14},{12,8},{14,10},{16,20},{18,... | collective-permute-start | bytes 1179656 | tf_op jit(solution)/shard_map/ppermute | solution.py:161
  112.3 15.4 %collective-permute-start.24 = (bf16[192,1024]{1,0:T(8,128)(2,1)S(1)}, bf16[192,1024]{1,0:T(8,128)(2,1)S(1)}, u32[]{:S(2)}, u32[]{:S(2)}) collective-permute-start(bf16[192,1024]{1,0:T(8,128)(2,1)S(1)} %get-tuple-element.151), channel_id=1, source_target_pairs={{0,2},{2,0},{4,6},{6,4},{8,10},{10,8},{12,14},{14,12},{16,18},{18,... | collective-permute-start | bytes 1179656 | tf_op jit(solution)/shard_map/ppermute | solution.py:158
  122.8 8.8 %collective-permute-start.25 = (bf16[192,1024]{1,0:T(8,128)(2,1)S(1)}, bf16[192,1024]{1,0:T(8,128)(2,1)S(1)}, u32[]{:S(2)}, u32[]{:S(2)}) collective-permute-start(bf16[192,1024]{1,0:T(8,128)(2,1)S(1)} %get-tuple-element.152), channel_id=1, source_target_pairs={{0,4},{2,6},{4,0},{6,2},{8,12},{10,14},{12,8},{14,10},{16,20},{18,... | collective-permute-start | bytes 1179656 | tf_op jit(solution)/shard_map/ppermute | solution.py:161
  (11 other events, 30.2 us)

commit v4 on v3

--- a/solution.py
+++ b/solution.py
@@ -348,7 +348,9 @@
     arrived = []
     mine = []
     for h in halves:
-        (a,), _ = line.run("cross_sum", [(add_kernel, [(a, whole(part)) for a in theirs[h]], [new(part)])])
+        (a,), (terms[-1],) = line.run(
+            "cross_sum", [(add_kernel, [(a, whole(part)) for a in theirs[h]], [new(part)])], [terms[-1]]
+        )
         arrived.append(over_x(a))
         mine.append(project(0, h))
 

time: 134 us -> 132 us (0.985)
  waiting for transfers between devices: 76.1 us -> 72.7 us
  starting transfers between devices: 30.5 us -> 32.8 us
    ppermute x6, waiting for transfers between devices: 38.5 us -> 32.1 us  [over_y(): lax.ppermute(a, 'tensor', [(i, (i + s) % teams) for i in range(teams)])]
    ppermute x6, waiting for transfers between devices: 24.7 us -> 29.2 us  [over_x(): return lax.ppermute(a, 'fsdp', [(i, i ^ 2) for i in range(group)])]
    ppermute x8, starting transfers between devices: 12.6 us -> 15.3 us  [over_z(): lax.ppermute(a, 'fsdp', [(4 * p + i, 4 * q + i) for p, q in pairs for i i...]
    ppermute x8, waiting for transfers between devices: 10.4 us -> 8.84 us  [over_z(): lax.ppermute(a, 'fsdp', [(4 * p + i, 4 * q + i) for p, q in pairs for i i...]
  transfers between devices with their start and end apart: 31 -> 31, of which waited for: 12 -> 14; matrix products, arithmetic and copies ran while one was open for 6% -> 6% of each run, Pallas kernels for 9% -> 9%
where the time goes in v4:
time: 132 us
  waiting for transfers between devices  72.7 us (55%)
  starting transfers between devices  32.8 us (25%)
  Pallas kernels  15.3 us (12%)
  matrix products  7.37 us (6%)
  local copies, waits for them, and re-layouts  2.63 us (2%)
    ppermute x6, waiting for transfers between devices, over_y(): lax.ppermute(a, 'tensor', [(i, (i + s) % teams) for i in range(teams)])  32.1 us
    ppermute x6, waiting for transfers between devices, over_x(): return lax.ppermute(a, 'fsdp', [(i, i ^ 2) for i in range(group)])  29.2 us
    ppermute x8, starting transfers between devices, over_z(): lax.ppermute(a, 'fsdp', [(4 * p + i, 4 * q + i) for p, q in pairs for i i...  15.3 us
    pallas_call x24, Pallas kernels, run(): pl.pallas_call(body, out_shape=[shape for shape, _ in made] + [jax.ShapeD...  13.6 us
    ppermute x8, waiting for transfers between devices, over_z(): lax.ppermute(a, 'fsdp', [(4 * p + i, 4 * q + i) for p, q in pairs for i i...  8.84 us
    dot_general x4, matrix products, terms_of(): lax.dot_general(a, cots, (((0,), (0,)), ((), ())), preferred_element_type...  7.37 us
    ppermute x6, starting transfers between devices, over_y(): lax.ppermute(a, 'tensor', [(i, (i + s) % teams) for i in range(teams)])  7.27 us
    ppermute x6, starting transfers between devices, over_x(): return lax.ppermute(a, 'fsdp', [(i, i ^ 2) for i in range(group)])  6.95 us
  transfers between devices with their start and end apart: 31, of which 14 were waited for; matrix products, arithmetic and copies ran while one was open for 6% of the time, Pallas kernels for 9%

profile of v4, /device:TPU:0, one launch (start us, length us, event | category | flops | bytes accessed | tf_op | source)
XLA Modules:
  0.0 131.8 jit_solution(3251470972393694329)
XLA Ops:
  1.4 1.9 %copy-done = bf16[192,8192]{1,0:T(8,128)(2,1)S(1)} copy-done((bf16[192,8192]{1,0:T(8,128)(2,1)S(1)}, bf16[192,8192]{1,0:T(8,128)(2,1)}, u32[]{:S(2)}) %copy-start) | copy-done | bytes 3145752
  8.3 2.6 %collective-permute-start.1 = (bf16[384,512]{1,0:T(8,128)(2,1)S(1)}, bf16[384,512]{1,0:T(8,128)(2,1)S(1)}, u32[]{:S(2)}, u32[]{:S(2)}) collective-permute-start(bf16[384,512]{1,0:T(8,128)(2,1)S(1)} %get-tuple-element.92), channel_id=1, source_target_pairs={{0,4},{2,6},{4,0},{6,2},{8,12},{10,14},{12,8},{14,10},{16,20},{18,... | collective-permute-start | bytes 1179656 | tf_op jit(solution)/shard_map/ppermute | solution.py:161
  13.2 4.4 %collective-permute-start.6 = (bf16[512,1024]{1,0:T(8,128)(2,1)S(1)}, bf16[512,1024]{1,0:T(8,128)(2,1)S(1)}, u32[]{:S(2)}, u32[]{:S(2)}) collective-permute-start(bf16[512,1024]{1,0:T(8,128)(2,1)S(1)} %get-tuple-element.97.refs_5_), channel_id=1, source_target_pairs={{0,8},{2,10},{4,12},{6,14},{8,0},{10,2},{12,4},{14,6},{16,24},{18,... | collective-permute-start | bytes 3145736 | tf_op jit(solution)/shard_map/ppermute | solution.py:170
  17.6 3.0 %collective-permute-done.1.refs_0_ = bf16[384,512]{1,0:T(8,128)(2,1)S(1)} collective-permute-done((bf16[384,512]{1,0:T(8,128)(2,1)S(1)}, bf16[384,512]{1,0:T(8,128)(2,1)S(1)}, u32[]{:S(2)}, u32[]{:S(2)}) %collective-permute-start.1) | collective-permute-done | bytes 393248 | tf_op jit(solution)/shard_map/ppermute | solution.py:161
  26.3 13.5 %collective-permute-done.4.refs_0_.refs_4_.refs_6_ = bf16[384,1024]{1,0:T(8,128)(2,1)S(1)} collective-permute-done((bf16[384,1024]{1,0:T(8,128)(2,1)S(1)}, bf16[384,1024]{1,0:T(8,128)(2,1)S(1)}, u32[]{:S(2)}, u32[]{:S(2)}) %collective-permute-start.4) | collective-permute-done | bytes 786464 | tf_op jit(solution)/shard_map/ppermute | solution.py:161
  43.1 1.8 %fusion.refs_0_.refs_2_ = f32[512,1024]{1,0:T(8,128)S(1)} fusion(bf16[1536,512]{1,0:T(8,128)(2,1)S(1)} %get-tuple-element.116.refs_0_, bf16[1536,1024]{1,0:T(8,128)(2,1)S(1)} %get-tuple-element.120), kind=kOutput, calls=%fused_computation | convolution fusion | flops 1610612736 | bytes 6815744 | tf_op jit(solution)/shard_map/dot_general | solution.py:238
  45.1 4.2 %collective-permute-start.18 = (bf16[512,1024]{1,0:T(8,128)(2,1)S(1)}, bf16[512,1024]{1,0:T(8,128)(2,1)S(1)}, u32[]{:S(2)}, u32[]{:S(2)}) collective-permute-start(bf16[512,1024]{1,0:T(8,128)(2,1)S(1)} %get-tuple-element.130), channel_id=1, source_target_pairs={{0,8},{2,10},{4,12},{6,14},{8,0},{10,2},{12,4},{14,6},{16,24},{18,... | collective-permute-start | bytes 3145736 | tf_op jit(solution)/shard_map/ppermute | solution.py:170
  49.4 2.8 %collective-permute-done.13.refs_0_ = bf16[384,512]{1,0:T(8,128)(2,1)S(1)} collective-permute-done((bf16[384,512]{1,0:T(8,128)(2,1)S(1)}, bf16[384,512]{1,0:T(8,128)(2,1)S(1)}, u32[]{:S(2)}, u32[]{:S(2)}) %collective-permute-start.13) | collective-permute-done | bytes 393248 | tf_op jit(solution)/shard_map/ppermute | solution.py:161
  52.1 8.3 %collective-permute-done.14.refs_2_ = bf16[1152,512]{1,0:T(8,128)(2,1)S(1)} collective-permute-done((bf16[1152,512]{1,0:T(8,128)(2,1)S(1)}, bf16[1152,512]{1,0:T(8,128)(2,1)S(1)}, u32[]{:S(2)}, u32[]{:S(2)}) %collective-permute-start.14) | collective-permute-done | bytes 1179680 | tf_op jit(solution)/shard_map/ppermute | solution.py:165
  62.5 8.3 %collective-permute-done.15.refs_3_ = bf16[384,512]{1,0:T(8,128)(2,1)S(1)} collective-permute-done((bf16[384,512]{1,0:T(8,128)(2,1)S(1)}, bf16[384,512]{1,0:T(8,128)(2,1)S(1)}, u32[]{:S(2)}, u32[]{:S(2)}) %collective-permute-start.15) | collective-permute-done | bytes 393248 | tf_op jit(solution)/shard_map/ppermute | solution.py:165
  70.9 1.8 %fusion.1.refs_0_.refs_3_ = f32[512,1024]{1,0:T(8,128)S(1)} fusion(bf16[1536,512]{1,0:T(8,128)(2,1)S(1)} %get-tuple-element.127.refs_1_, bf16[1536,1024]{1,0:T(8,128)(2,1)S(1)} %get-tuple-element.120), kind=kOutput, calls=%fused_computation.1 | convolution fusion | flops 1610612736 | bytes 6815744 | tf_op jit(solution)/shard_map/dot_general | solution.py:238
  75.4 5.1 %collective-permute-done.16.refs_0_.refs_1_ = bf16[768,512]{1,0:T(8,128)(2,1)S(1)} collective-permute-done((bf16[768,512]{1,0:T(8,128)(2,1)S(1)}, bf16[768,512]{1,0:T(8,128)(2,1)S(1)}, u32[]{:S(2)}, u32[]{:S(2)}) %collective-permute-start.16) | collective-permute-done | bytes 786464 | tf_op jit(solution)/shard_map/ppermute | solution.py:161
  82.6 10.0 %collective-permute-done.19.refs_3_ = bf16[384,512]{1,0:T(8,128)(2,1)S(1)} collective-permute-done((bf16[384,512]{1,0:T(8,128)(2,1)S(1)}, bf16[384,512]{1,0:T(8,128)(2,1)S(1)}, u32[]{:S(2)}, u32[]{:S(2)}) %collective-permute-start.19) | collective-permute-done | bytes 393248 | tf_op jit(solution)/shard_map/ppermute | solution.py:165
  92.6 5.5 %collective-permute-done.20.refs_7_ = bf16[384,512]{1,0:T(8,128)(2,1)S(1)} collective-permute-done((bf16[384,512]{1,0:T(8,128)(2,1)S(1)}, bf16[384,512]{1,0:T(8,128)(2,1)S(1)}, u32[]{:S(2)}, u32[]{:S(2)}) %collective-permute-start.20) | collective-permute-done | bytes 393248 | tf_op jit(solution)/shard_map/ppermute | solution.py:165
  98.3 1.8 %fusion.2.refs_0_.refs_1_ = f32[512,1024]{1,0:T(8,128)S(1)} fusion(bf16[1536,512]{1,0:T(8,128)(2,1)S(1)} %get-tuple-element.136.refs_2_, bf16[1536,1024]{1,0:T(8,128)(2,1)S(1)} %get-tuple-element.120), kind=kOutput, calls=%fused_computation.2 | convolution fusion | flops 1610612736 | bytes 6815744 | tf_op jit(solution)/shard_map/dot_general | solution.py:238
  100.3 2.0 %collective-permute-start.29 = (bf16[512,1024]{1,0:T(8,128)(2,1)S(1)}, bf16[512,1024]{1,0:T(8,128)(2,1)S(1)}, u32[]{:S(2)}, u32[]{:S(2)}) collective-permute-start(bf16[512,1024]{1,0:T(8,128)(2,1)S(1)} %get-tuple-element.164), channel_id=1, source_target_pairs={{0,8},{2,10},{4,12},{6,14},{8,0},{10,2},{12,4},{14,6},{16,24},{18,... | collective-permute-start | bytes 3145736 | tf_op jit(solution)/shard_map/ppermute | solution.py:170
  103.5 1.8 %project.4 = (f32[192,1024]{1,0:T(8,128)S(1)}, bf16[192,1024]{1,0:T(8,128)(2,1)S(1)}, f32[8,128]{1,0:T(8,128)S(1)}) custom-call(bf16[1536,512]{1,0:T(8,128)(2,1)S(1)} %get-tuple-element.116.refs_0_, bf16[1536,512]{1,0:T(8,128)(2,1)S(1)} %get-tuple-element.127.refs_1_, bf16[1536,512]{1,0:T(8,128)(2,1)S(1)} %get-tuple-element.136.refs_2_, ...), custom_call_target="tpu_custom_call" | custom-call | bytes 1 | tf_op jit(solution)/shard_map/project/pallas_call | solution.py:108
  105.4 1.8 %project.5 = (f32[192,1024]{1,0:T(8,128)S(1)}, bf16[192,1024]{1,0:T(8,128)(2,1)S(1)}, f32[8,128]{1,0:T(8,128)S(1)}) custom-call(bf16[1536,512]{1,0:T(8,128)(2,1)S(1)} %get-tuple-element.116.refs_0_, bf16[1536,512]{1,0:T(8,128)(2,1)S(1)} %get-tuple-element.127.refs_1_, bf16[1536,512]{1,0:T(8,128)(2,1)S(1)} %get-tuple-element.136.refs_2_, ...), custom_call_target="tpu_custom_call" | custom-call | bytes 1 | tf_op jit(solution)/shard_map/project/pallas_call | solution.py:108
  107.8 1.8 %fusion.3.refs_2_ = f32[512,1024]{1,0:T(8,128)S(1)} fusion(bf16[1536,512]{1,0:T(8,128)(2,1)S(1)} %get-tuple-element.137.refs_3_, bf16[1536,1024]{1,0:T(8,128)(2,1)S(1)} %get-tuple-element.120), kind=kOutput, calls=%fused_computation.3 | convolution fusion | flops 1610612736 | bytes 6815744 | tf_op jit(solution)/shard_map/dot_general | solution.py:238
  110.3 1.8 %project.6 = (f32[192,1024]{1,0:T(8,128)S(1)}, bf16[192,1024]{1,0:T(8,128)(2,1)S(1)}, f32[8,128]{1,0:T(8,128)S(1)}) custom-call(bf16[1536,512]{1,0:T(8,128)(2,1)S(1)} %get-tuple-element.116.refs_0_, bf16[1536,512]{1,0:T(8,128)(2,1)S(1)} %get-tuple-element.127.refs_1_, bf16[1536,512]{1,0:T(8,128)(2,1)S(1)} %get-tuple-element.136.refs_2_, ...), custom_call_target="tpu_custom_call" | custom-call | bytes 1 | tf_op jit(solution)/shard_map/project/pallas_call | solution.py:108
  112.2 1.8 %project.7 = (f32[192,1024]{1,0:T(8,128)S(1)}, bf16[192,1024]{1,0:T(8,128)(2,1)S(1)}, f32[8,128]{1,0:T(8,128)S(1)}) custom-call(bf16[1536,512]{1,0:T(8,128)(2,1)S(1)} %get-tuple-element.116.refs_0_, bf16[1536,512]{1,0:T(8,128)(2,1)S(1)} %get-tuple-element.127.refs_1_, bf16[1536,512]{1,0:T(8,128)(2,1)S(1)} %get-tuple-element.136.refs_2_, ...), custom_call_target="tpu_custom_call" | custom-call | bytes 1 | tf_op jit(solution)/shard_map/project/pallas_call | solution.py:108
  114.6 8.2 %collective-permute-done.29.refs_2_ = bf16[512,1024]{1,0:T(8,128)(2,1)S(1)} collective-permute-done((bf16[512,1024]{1,0:T(8,128)(2,1)S(1)}, bf16[512,1024]{1,0:T(8,128)(2,1)S(1)}, u32[]{:S(2)}, u32[]{:S(2)}) %collective-permute-start.29) | collective-permute-done | bytes 1048608 | tf_op jit(solution)/shard_map/ppermute | solution.py:170
  123.4 2.4 %own_gradient.1 = (f32[512,1024]{1,0:T(8,128)}, f32[8,128]{1,0:T(8,128)S(1)}) custom-call(s32[4,8]{1,0:T(4,128)S(1)} %copy-done.3, f32[512,1024]{1,0:T(8,128)S(1)} %get-tuple-element.163.refs_1_, bf16[512,1024]{1,0:T(8,128)(2,1)S(1)} %collective-permute-done.29.refs_2_, bf16[512,1024]{1,0:T(8,128)(2,1)S(1)} %collective-permute-done.30.refs_3_, ...), custom_call_target="tpu_custom_call" | custom-call | bytes 1 | tf_op jit(solution)/shard_map/own_gradient/pallas_call | solution.py:108
  125.8 4.9 %collective-permute-done.28.refs_5_ = bf16[192,1024]{1,0:T(8,128)(2,1)S(1)} collective-permute-done((bf16[192,1024]{1,0:T(8,128)(2,1)S(1)}, bf16[192,1024]{1,0:T(8,128)(2,1)S(1)}, u32[]{:S(2)}, u32[]{:S(2)}) %collective-permute-start.28) | collective-permute-done | bytes 393248 | tf_op jit(solution)/shard_map/ppermute | solution.py:161
  (76 shorter events, 29.3 us)
Async XLA Ops:
  5.5 7.6 %collective-permute-start.8 = (bf16[2,192,512]{2,1,0:T(8,128)(2,1)S(1)}, bf16[2,192,512]{2,1,0:T(8,128)(2,1)S(1)}, u32[]{:S(2)}, u32[]{:S(2)}) collective-permute-start(bf16[2,192,512]{2,1,0:T(8,128)(2,1)S(1)} %get-tuple-element.99), channel_id=1, source_target_pairs={{0,2},{2,0},{4,6},{6,4},{8,10},{10,8},{12,14},{14,12},{16,18},{18,... | collective-permute-start | bytes 1179656 | tf_op jit(solution)/shard_map/ppermute | solution.py:158
  7.8 14.5 %collective-permute-start.2 = (bf16[384,1024]{1,0:T(8,128)(2,1)S(1)}, bf16[384,1024]{1,0:T(8,128)(2,1)S(1)}, u32[]{:S(2)}, u32[]{:S(2)}) collective-permute-start(bf16[384,1024]{1,0:T(8,128)(2,1)S(1)} %get-tuple-element.91.refs_0_.refs_2_), channel_id=1, source_target_pairs={{0,2},{2,0},{4,6},{6,4},{8,10},{10,8},{12,14},{14,12},{16,18},{18,... | collective-permute-start | bytes 2359304 | tf_op jit(solution)/shard_map/ppermute | solution.py:158
  8.3 12.3 %collective-permute-start.1 = (bf16[384,512]{1,0:T(8,128)(2,1)S(1)}, bf16[384,512]{1,0:T(8,128)(2,1)S(1)}, u32[]{:S(2)}, u32[]{:S(2)}) collective-permute-start(bf16[384,512]{1,0:T(8,128)(2,1)S(1)} %get-tuple-element.92), channel_id=1, source_target_pairs={{0,4},{2,6},{4,0},{6,2},{8,12},{10,14},{12,8},{14,10},{16,20},{18,... | collective-permute-start | bytes 1179656 | tf_op jit(solution)/shard_map/ppermute | solution.py:161
  10.9 11.4 %collective-permute-start.3 = (bf16[384,512]{1,0:T(8,128)(2,1)S(1)}, bf16[384,512]{1,0:T(8,128)(2,1)S(1)}, u32[]{:S(2)}, u32[]{:S(2)}) collective-permute-start(bf16[384,512]{1,0:T(8,128)(2,1)S(1)} %get-tuple-element.93.refs_8_), channel_id=1, source_target_pairs={{0,1},{1,0},{2,3},{3,2},{4,5},{5,4},{6,7},{7,6},{8,9},{9,8},{10,11... | collective-permute-start | bytes 1179656 | tf_op jit(solution)/shard_map/ppermute | solution.py:165
  12.4 27.4 %collective-permute-start.7 = (bf16[512,1024]{1,0:T(8,128)(2,1)S(1)}, bf16[512,1024]{1,0:T(8,128)(2,1)S(1)}, u32[]{:S(2)}, u32[]{:S(2)}) collective-permute-start(bf16[512,1024]{1,0:T(8,128)(2,1)S(1)} %get-tuple-element.97.refs_5_), channel_id=1, source_target_pairs={{0,0},{2,2},{4,4},{6,6},{8,16},{10,18},{12,20},{14,22},{16,8},{18,... | collective-permute-start | bytes 3145736 | tf_op jit(solution)/shard_map/ppermute | solution.py:170
  13.2 27.2 %collective-permute-start.6 = (bf16[512,1024]{1,0:T(8,128)(2,1)S(1)}, bf16[512,1024]{1,0:T(8,128)(2,1)S(1)}, u32[]{:S(2)}, u32[]{:S(2)}) collective-permute-start(bf16[512,1024]{1,0:T(8,128)(2,1)S(1)} %get-tuple-element.97.refs_5_), channel_id=1, source_target_pairs={{0,8},{2,10},{4,12},{6,14},{8,0},{10,2},{12,4},{14,6},{16,24},{18,... | collective-permute-start | bytes 3145736 | tf_op jit(solution)/shard_map/ppermute | solution.py:170
  20.6 19.2 %collective-permute-start.4 = (bf16[384,1024]{1,0:T(8,128)(2,1)S(1)}, bf16[384,1024]{1,0:T(8,128)(2,1)S(1)}, u32[]{:S(2)}, u32[]{:S(2)}) collective-permute-start(bf16[384,1024]{1,0:T(8,128)(2,1)S(1)} %get-tuple-element.91.refs_0_.refs_2_), channel_id=1, source_target_pairs={{0,4},{2,6},{4,0},{6,2},{8,12},{10,14},{12,8},{14,10},{16,20},{18,... | collective-permute-start | bytes 2359304 | tf_op jit(solution)/shard_map/ppermute | solution.py:161
  24.0 16.4 %collective-permute-start.5 = (bf16[384,512]{1,0:T(8,128)(2,1)S(1)}, bf16[384,512]{1,0:T(8,128)(2,1)S(1)}, u32[]{:S(2)}, u32[]{:S(2)}) collective-permute-start(bf16[384,512]{1,0:T(8,128)(2,1)S(1)} %get-tuple-element.96.refs_10_), channel_id=1, source_target_pairs={{0,1},{1,0},{2,3},{3,2},{4,5},{5,4},{6,7},{7,6},{8,9},{9,8},{10,11... | collective-permute-start | bytes 1179656 | tf_op jit(solution)/shard_map/ppermute | solution.py:165
  25.6 34.8 %collective-permute-start.14 = (bf16[1152,512]{1,0:T(8,128)(2,1)S(1)}, bf16[1152,512]{1,0:T(8,128)(2,1)S(1)}, u32[]{:S(2)}, u32[]{:S(2)}) collective-permute-start(bf16[1152,512]{1,0:T(8,128)(2,1)S(1)} %get-tuple-element.117.refs_0_.refs_4_), channel_id=1, source_target_pairs={{0,1},{1,0},{2,3},{3,2},{4,5},{5,4},{6,7},{7,6},{8,9},{9,8},{10,11... | collective-permute-start | bytes 3538952 | tf_op jit(solution)/shard_map/ppermute | solution.py:165
  41.0 11.1 %collective-permute-start.13 = (bf16[384,512]{1,0:T(8,128)(2,1)S(1)}, bf16[384,512]{1,0:T(8,128)(2,1)S(1)}, u32[]{:S(2)}, u32[]{:S(2)}) collective-permute-start(bf16[384,512]{1,0:T(8,128)(2,1)S(1)} %get-tuple-element.118), channel_id=1, source_target_pairs={{0,4},{2,6},{4,0},{6,2},{8,12},{10,14},{12,8},{14,10},{16,20},{18,... | collective-permute-start | bytes 1179656 | tf_op jit(solution)/shard_map/ppermute | solution.py:161
  42.0 30.8 %collective-permute-start.17 = (bf16[512,1024]{1,0:T(8,128)(2,1)S(1)}, bf16[512,1024]{1,0:T(8,128)(2,1)S(1)}, u32[]{:S(2)}, u32[]{:S(2)}) collective-permute-start(bf16[512,1024]{1,0:T(8,128)(2,1)S(1)} %get-tuple-element.129.refs_4_), channel_id=1, source_target_pairs={{0,0},{2,2},{4,4},{6,6},{8,16},{10,18},{12,20},{14,22},{16,8},{18,... | collective-permute-start | bytes 3145736 | tf_op jit(solution)/shard_map/ppermute | solution.py:170
  45.1 27.6 %collective-permute-start.18 = (bf16[512,1024]{1,0:T(8,128)(2,1)S(1)}, bf16[512,1024]{1,0:T(8,128)(2,1)S(1)}, u32[]{:S(2)}, u32[]{:S(2)}) collective-permute-start(bf16[512,1024]{1,0:T(8,128)(2,1)S(1)} %get-tuple-element.130), channel_id=1, source_target_pairs={{0,8},{2,10},{4,12},{6,14},{8,0},{10,2},{12,4},{14,6},{16,24},{18,... | collective-permute-start | bytes 3145736 | tf_op jit(solution)/shard_map/ppermute | solution.py:170
  60.5 10.3 %collective-permute-start.15 = (bf16[384,512]{1,0:T(8,128)(2,1)S(1)}, bf16[384,512]{1,0:T(8,128)(2,1)S(1)}, u32[]{:S(2)}, u32[]{:S(2)}) collective-permute-start(bf16[384,512]{1,0:T(8,128)(2,1)S(1)} %get-tuple-element.125.refs_2_), channel_id=1, source_target_pairs={{0,1},{1,0},{2,3},{3,2},{4,5},{5,4},{6,7},{7,6},{8,9},{9,8},{10,11... | collective-permute-start | bytes 1179656 | tf_op jit(solution)/shard_map/ppermute | solution.py:165
  62.0 18.5 %collective-permute-start.16 = (bf16[768,512]{1,0:T(8,128)(2,1)S(1)}, bf16[768,512]{1,0:T(8,128)(2,1)S(1)}, u32[]{:S(2)}, u32[]{:S(2)}) collective-permute-start(bf16[768,512]{1,0:T(8,128)(2,1)S(1)} %get-tuple-element.128), channel_id=1, source_target_pairs={{0,4},{2,6},{4,0},{6,2},{8,12},{10,14},{12,8},{14,10},{16,20},{18,... | collective-permute-start | bytes 2359304 | tf_op jit(solution)/shard_map/ppermute | solution.py:161
  72.9 27.3 %collective-permute-start.21 = (bf16[512,1024]{1,0:T(8,128)(2,1)S(1)}, bf16[512,1024]{1,0:T(8,128)(2,1)S(1)}, u32[]{:S(2)}, u32[]{:S(2)}) collective-permute-start(bf16[512,1024]{1,0:T(8,128)(2,1)S(1)} %get-tuple-element.138), channel_id=1, source_target_pairs={{0,8},{2,10},{4,12},{6,14},{8,0},{10,2},{12,4},{14,6},{16,24},{18,... | collective-permute-start | bytes 3145736 | tf_op jit(solution)/shard_map/ppermute | solution.py:170
  74.7 25.5 %collective-permute-start.22 = (bf16[512,1024]{1,0:T(8,128)(2,1)S(1)}, bf16[512,1024]{1,0:T(8,128)(2,1)S(1)}, u32[]{:S(2)}, u32[]{:S(2)}) collective-permute-start(bf16[512,1024]{1,0:T(8,128)(2,1)S(1)} %get-tuple-element.139), channel_id=1, source_target_pairs={{0,0},{2,2},{4,4},{6,6},{8,16},{10,18},{12,20},{14,22},{16,8},{18,... | collective-permute-start | bytes 3145736 | tf_op jit(solution)/shard_map/ppermute | solution.py:170
  80.5 12.1 %collective-permute-start.19 = (bf16[384,512]{1,0:T(8,128)(2,1)S(1)}, bf16[384,512]{1,0:T(8,128)(2,1)S(1)}, u32[]{:S(2)}, u32[]{:S(2)}) collective-permute-start(bf16[384,512]{1,0:T(8,128)(2,1)S(1)} %get-tuple-element.133.refs_2_), channel_id=1, source_target_pairs={{0,1},{1,0},{2,3},{3,2},{4,5},{5,4},{6,7},{7,6},{8,9},{9,8},{10,11... | collective-permute-start | bytes 1179656 | tf_op jit(solution)/shard_map/ppermute | solution.py:165
  81.1 17.0 %collective-permute-start.20 = (bf16[384,512]{1,0:T(8,128)(2,1)S(1)}, bf16[384,512]{1,0:T(8,128)(2,1)S(1)}, u32[]{:S(2)}, u32[]{:S(2)}) collective-permute-start(bf16[384,512]{1,0:T(8,128)(2,1)S(1)} %get-tuple-element.134.refs_6_), channel_id=1, source_target_pairs={{0,1},{1,0},{2,3},{3,2},{4,5},{5,4},{6,7},{7,6},{8,9},{9,8},{10,11... | collective-permute-start | bytes 1179656 | tf_op jit(solution)/shard_map/ppermute | solution.py:165
  100.3 22.5 %collective-permute-start.29 = (bf16[512,1024]{1,0:T(8,128)(2,1)S(1)}, bf16[512,1024]{1,0:T(8,128)(2,1)S(1)}, u32[]{:S(2)}, u32[]{:S(2)}) collective-permute-start(bf16[512,1024]{1,0:T(8,128)(2,1)S(1)} %get-tuple-element.164), channel_id=1, source_target_pairs={{0,8},{2,10},{4,12},{6,14},{8,0},{10,2},{12,4},{14,6},{16,24},{18,... | collective-permute-start | bytes 3145736 | tf_op jit(solution)/shard_map/ppermute | solution.py:170
  102.3 21.0 %collective-permute-start.30 = (bf16[512,1024]{1,0:T(8,128)(2,1)S(1)}, bf16[512,1024]{1,0:T(8,128)(2,1)S(1)}, u32[]{:S(2)}, u32[]{:S(2)}) collective-permute-start(bf16[512,1024]{1,0:T(8,128)(2,1)S(1)} %get-tuple-element.165), channel_id=1, source_target_pairs={{0,0},{2,2},{4,4},{6,6},{8,16},{10,18},{12,20},{14,22},{16,8},{18,... | collective-permute-start | bytes 3145736 | tf_op jit(solution)/shard_map/ppermute | solution.py:170
  109.8 16.0 %collective-permute-start.25 = (bf16[192,1024]{1,0:T(8,128)(2,1)S(1)}, bf16[192,1024]{1,0:T(8,128)(2,1)S(1)}, u32[]{:S(2)}, u32[]{:S(2)}) collective-permute-start(bf16[192,1024]{1,0:T(8,128)(2,1)S(1)} %get-tuple-element.154), channel_id=1, source_target_pairs={{0,4},{2,6},{4,0},{6,2},{8,12},{10,14},{12,8},{14,10},{16,20},{18,... | collective-permute-start | bytes 1179656 | tf_op jit(solution)/shard_map/ppermute | solution.py:161
  114.1 11.7 %collective-permute-start.24 = (bf16[192,1024]{1,0:T(8,128)(2,1)S(1)}, bf16[192,1024]{1,0:T(8,128)(2,1)S(1)}, u32[]{:S(2)}, u32[]{:S(2)}) collective-permute-start(bf16[192,1024]{1,0:T(8,128)(2,1)S(1)} %get-tuple-element.153), channel_id=1, source_target_pairs={{0,2},{2,0},{4,6},{6,4},{8,10},{10,8},{12,14},{14,12},{16,18},{18,... | collective-permute-start | bytes 1179656 | tf_op jit(solution)/shard_map/ppermute | solution.py:158
  114.1 11.6 %collective-permute-start.27 = (bf16[192,1024]{1,0:T(8,128)(2,1)S(1)}, bf16[192,1024]{1,0:T(8,128)(2,1)S(1)}, u32[]{:S(2)}, u32[]{:S(2)}) collective-permute-start(bf16[192,1024]{1,0:T(8,128)(2,1)S(1)} %get-tuple-element.161), channel_id=1, source_target_pairs={{0,2},{2,0},{4,6},{6,4},{8,10},{10,8},{12,14},{14,12},{16,18},{18,... | collective-permute-start | bytes 1179656 | tf_op jit(solution)/shard_map/ppermute | solution.py:158
  122.8 7.8 %collective-permute-start.28 = (bf16[192,1024]{1,0:T(8,128)(2,1)S(1)}, bf16[192,1024]{1,0:T(8,128)(2,1)S(1)}, u32[]{:S(2)}, u32[]{:S(2)}) collective-permute-start(bf16[192,1024]{1,0:T(8,128)(2,1)S(1)} %get-tuple-element.162), channel_id=1, source_target_pairs={{0,4},{2,6},{4,0},{6,2},{8,12},{10,14},{12,8},{14,10},{16,20},{18,... | collective-permute-start | bytes 1179656 | tf_op jit(solution)/shard_map/ppermute | solution.py:161
  (11 other events, 33.4 us)

commit v5 on v3

--- a/solution.py
+++ b/solution.py
@@ -281,8 +281,10 @@
     (cots, normed_0), _ = line.run("head", [join(pieces), gather(near_0, near_y, cross_0, cross_y, (0, 0))])
     normed, terms = [normed_0], [terms_of(normed_0)]
     phase(2, [0])
-    _, (cross_1, rest, *near_rest_y) = line.run("arrived", [], [cross_1, rest, *near_rest_y])
-    cross_1_y, rest = over_y(cross_1), over_x(rest)
+    _, (cross_1, rest) = line.run("arrived", [], [cross_1, rest])
+    rest = over_x(rest)
+    _, (cross_1, *near_rest_y) = line.run("arrived", [], [cross_1, *near_rest_y])
+    cross_1_y = over_y(cross_1)
     (normed_1,), _ = line.run("rows", [gather(near_rest, near_rest_y, cross_1, cross_1_y, (0, 0))])
     normed.append(normed_1)
     terms.append(terms_of(normed_1))
@@ -340,17 +342,21 @@
         kept, sent = line.run("project", [(kernel, ins, outs)], grid=(half,))[0]
         return kept, over_core(sent)
 
-    def add_kernel(kept, sent, out):
-        out[...] = (kept[...] + sent[...].astype(F32)).astype(BF)
-
     halves = range(teams // half)
     theirs = [project(1, h) for h in halves]
-    arrived = []
-    mine = []
-    for h in halves:
-        (a,), _ = line.run("cross_sum", [(add_kernel, [(a, whole(part)) for a in theirs[h]], [new(part)])])
-        arrived.append(over_x(a))
-        mine.append(project(0, h))
+
+    def sum_kernel(*refs):
+        out = refs[-1]
+        for h in halves:
+            out[h * half * rows:(h + 1) * half * rows, :] = (refs[2 * h][...] + refs[2 * h + 1][...].astype(F32)).astype(BF)
+
+    (a,), (terms[-1],) = line.run(
+        "cross_sum",
+        [(sum_kernel, [(a, whole(part)) for h in halves for a in theirs[h]], [new((teams * rows, cols))])],
+        [terms[-1]],
+    )
+    arrived = over_x(a)
+    mine = [project(0, h) for h in halves]
 
     def own_kernel(mask, term, even, odd, out):
         z = spot()[0]
@@ -365,16 +371,21 @@
     ins = [(block_mask, SCALARS)] + [(a, whole(panel)) for a in [terms[layers - 1], *came[layers]]]
     (weight_grad,), _ = line.run("own_gradient", [(own_kernel, ins, [new(panel, F32)])])
 
+    held = [*normed, cots]
+    for _ in range(1):
+        _, held = line.run("spacer", [], held)
+
     def last_sum(*refs):
         out = refs[-1]
         for h in halves:
-            kept, sent, a = refs[3 * h:3 * h + 3]
-            total = (kept[...] + sent[...].astype(F32) + a[...].astype(F32)).astype(BF)
+            kept, sent = refs[2 * h:2 * h + 2]
+            came_x = refs[-2][h * half * rows:(h + 1) * half * rows, :].astype(F32)
+            total = (kept[...] + sent[...].astype(F32) + came_x).astype(BF)
             for i in range(half):
                 j = lax.rem(spot()[3] + teams - h * half - i, teams)
                 out[pl.ds(pl.multiple_of(j * rows, rows), rows), :] = total[i * rows:(i + 1) * rows]
 
-    ins = [(a, whole(part)) for h in halves for a in (*mine[h], arrived[h])]
+    ins = [(a, whole(part)) for h in halves for a in mine[h]] + [(arrived, whole((teams * rows, cols)))]
     (projected,), _ = line.run("projected", [(last_sum, ins, [new((teams * rows, cols))])])
     return (projected, weight_grad)
 

time: 134 us -> 132 us (0.985)
  waiting for transfers between devices: 76.1 us -> 72.1 us
  starting transfers between devices: 30.5 us -> 32.3 us
    ppermute x6, waiting for transfers between devices: 38.5 us -> 32.1 us  [over_y(): lax.ppermute(a, 'tensor', [(i, (i + s) % teams) for i in range(teams)])]
    ppermute x6 -> x5, waiting for transfers between devices: 24.7 us -> 28.5 us  [over_x(): return lax.ppermute(a, 'fsdp', [(i, i ^ 2) for i in range(group)])]
    ppermute x8, starting transfers between devices: 12.6 us -> 15.3 us  [over_z(): lax.ppermute(a, 'fsdp', [(4 * p + i, 4 * q + i) for p, q in pairs for i i...]
    ppermute x8, waiting for transfers between devices: 10.4 us -> 8.83 us  [over_z(): lax.ppermute(a, 'fsdp', [(4 * p + i, 4 * q + i) for p, q in pairs for i i...]
    ppermute x6 -> x5, starting transfers between devices: 6.53 us -> 6.42 us  [over_x(): return lax.ppermute(a, 'fsdp', [(i, i ^ 2) for i in range(group)])]
    pallas_call x24 -> x25, Pallas kernels: 13.6 us -> 13.5 us  [run(): pl.pallas_call(body, out_shape=[shape for shape, _ in made] + [jax.ShapeD...]
  transfers between devices with their start and end apart: 31 -> 30, of which waited for: 12 -> 14; matrix products, arithmetic and copies ran while one was open for 6% -> 6% of each run, Pallas kernels for 9% -> 9%
where the time goes in v5:
time: 132 us; the launch traced here: 130 us
  waiting for transfers between devices  72.1 us (55%)
  starting transfers between devices  32.3 us (24%)
  Pallas kernels  15.3 us (12%)
  matrix products  7.22 us (5%)
  local copies, waits for them, and re-layouts  2.63 us (2%)
    ppermute x6, waiting for transfers between devices, over_y(): lax.ppermute(a, 'tensor', [(i, (i + s) % teams) for i in range(teams)])  32.1 us
    ppermute x5, waiting for transfers between devices, over_x(): return lax.ppermute(a, 'fsdp', [(i, i ^ 2) for i in range(group)])  28.5 us
    ppermute x8, starting transfers between devices, over_z(): lax.ppermute(a, 'fsdp', [(4 * p + i, 4 * q + i) for p, q in pairs for i i...  15.3 us
    pallas_call x25, Pallas kernels, run(): pl.pallas_call(body, out_shape=[shape for shape, _ in made] + [jax.ShapeD...  13.5 us
    ppermute x8, waiting for transfers between devices, over_z(): lax.ppermute(a, 'fsdp', [(4 * p + i, 4 * q + i) for p, q in pairs for i i...  8.83 us
    ppermute x6, starting transfers between devices, over_y(): lax.ppermute(a, 'tensor', [(i, (i + s) % teams) for i in range(teams)])  7.27 us
    dot_general x4, matrix products, terms_of(): lax.dot_general(a, cots, (((0,), (0,)), ((), ())), preferred_element_type...  7.22 us
    ppermute x5, starting transfers between devices, over_x(): return lax.ppermute(a, 'fsdp', [(i, i ^ 2) for i in range(group)])  6.42 us
  transfers between devices with their start and end apart: 30, of which 14 were waited for; matrix products, arithmetic and copies ran while one was open for 6% of the time, Pallas kernels for 9%

profile of v5, /device:TPU:0, one launch (start us, length us, event | category | flops | bytes accessed | tf_op | source)
XLA Modules:
  0.0 130.5 jit_solution(11748848407027340248)
XLA Ops:
  1.4 1.9 %copy-done = bf16[192,8192]{1,0:T(8,128)(2,1)S(1)} copy-done((bf16[192,8192]{1,0:T(8,128)(2,1)S(1)}, bf16[192,8192]{1,0:T(8,128)(2,1)}, u32[]{:S(2)}) %copy-start) | copy-done | bytes 3145752
  8.3 2.6 %collective-permute-start.1 = (bf16[384,512]{1,0:T(8,128)(2,1)S(1)}, bf16[384,512]{1,0:T(8,128)(2,1)S(1)}, u32[]{:S(2)}, u32[]{:S(2)}) collective-permute-start(bf16[384,512]{1,0:T(8,128)(2,1)S(1)} %get-tuple-element.92), channel_id=1, source_target_pairs={{0,4},{2,6},{4,0},{6,2},{8,12},{10,14},{12,8},{14,10},{16,20},{18,... | collective-permute-start | bytes 1179656 | tf_op jit(solution)/shard_map/ppermute | solution.py:161
  13.2 4.4 %collective-permute-start.6 = (bf16[512,1024]{1,0:T(8,128)(2,1)S(1)}, bf16[512,1024]{1,0:T(8,128)(2,1)S(1)}, u32[]{:S(2)}, u32[]{:S(2)}) collective-permute-start(bf16[512,1024]{1,0:T(8,128)(2,1)S(1)} %get-tuple-element.97.refs_5_), channel_id=1, source_target_pairs={{0,8},{2,10},{4,12},{6,14},{8,0},{10,2},{12,4},{14,6},{16,24},{18,... | collective-permute-start | bytes 3145736 | tf_op jit(solution)/shard_map/ppermute | solution.py:170
  17.6 3.0 %collective-permute-done.1.refs_0_ = bf16[384,512]{1,0:T(8,128)(2,1)S(1)} collective-permute-done((bf16[384,512]{1,0:T(8,128)(2,1)S(1)}, bf16[384,512]{1,0:T(8,128)(2,1)S(1)}, u32[]{:S(2)}, u32[]{:S(2)}) %collective-permute-start.1) | collective-permute-done | bytes 393248 | tf_op jit(solution)/shard_map/ppermute | solution.py:161
  26.3 13.5 %collective-permute-done.4.refs_0_.refs_4_.refs_6_ = bf16[384,1024]{1,0:T(8,128)(2,1)S(1)} collective-permute-done((bf16[384,1024]{1,0:T(8,128)(2,1)S(1)}, bf16[384,1024]{1,0:T(8,128)(2,1)S(1)}, u32[]{:S(2)}, u32[]{:S(2)}) %collective-permute-start.4) | collective-permute-done | bytes 786464 | tf_op jit(solution)/shard_map/ppermute | solution.py:161
  43.1 1.8 %fusion.refs_0_.refs_2_ = f32[512,1024]{1,0:T(8,128)S(1)} fusion(bf16[1536,512]{1,0:T(8,128)(2,1)S(1)} %get-tuple-element.116.refs_0_, bf16[1536,1024]{1,0:T(8,128)(2,1)S(1)} %get-tuple-element.120.refs_4_), kind=kOutput, calls=%fused_computation | convolution fusion | flops 1610612736 | bytes 6815744 | tf_op jit(solution)/shard_map/dot_general | solution.py:238
  45.1 4.2 %collective-permute-start.18 = (bf16[512,1024]{1,0:T(8,128)(2,1)S(1)}, bf16[512,1024]{1,0:T(8,128)(2,1)S(1)}, u32[]{:S(2)}, u32[]{:S(2)}) collective-permute-start(bf16[512,1024]{1,0:T(8,128)(2,1)S(1)} %get-tuple-element.132), channel_id=1, source_target_pairs={{0,8},{2,10},{4,12},{6,14},{8,0},{10,2},{12,4},{14,6},{16,24},{18,... | collective-permute-start | bytes 3145736 | tf_op jit(solution)/shard_map/ppermute | solution.py:170
  49.3 2.8 %collective-permute-done.13.refs_0_ = bf16[384,512]{1,0:T(8,128)(2,1)S(1)} collective-permute-done((bf16[384,512]{1,0:T(8,128)(2,1)S(1)}, bf16[384,512]{1,0:T(8,128)(2,1)S(1)}, u32[]{:S(2)}, u32[]{:S(2)}) %collective-permute-start.13) | collective-permute-done | bytes 393248 | tf_op jit(solution)/shard_map/ppermute | solution.py:161
  52.1 8.3 %collective-permute-done.14.refs_1_ = bf16[1152,512]{1,0:T(8,128)(2,1)S(1)} collective-permute-done((bf16[1152,512]{1,0:T(8,128)(2,1)S(1)}, bf16[1152,512]{1,0:T(8,128)(2,1)S(1)}, u32[]{:S(2)}, u32[]{:S(2)}) %collective-permute-start.14) | collective-permute-done | bytes 1179680 | tf_op jit(solution)/shard_map/ppermute | solution.py:165
  62.5 8.3 %collective-permute-done.15.refs_3_ = bf16[384,512]{1,0:T(8,128)(2,1)S(1)} collective-permute-done((bf16[384,512]{1,0:T(8,128)(2,1)S(1)}, bf16[384,512]{1,0:T(8,128)(2,1)S(1)}, u32[]{:S(2)}, u32[]{:S(2)}) %collective-permute-start.15) | collective-permute-done | bytes 393248 | tf_op jit(solution)/shard_map/ppermute | solution.py:165
  70.9 1.8 %fusion.1.refs_0_.refs_3_ = f32[512,1024]{1,0:T(8,128)S(1)} fusion(bf16[1536,512]{1,0:T(8,128)(2,1)S(1)} %get-tuple-element.129.refs_1_, bf16[1536,1024]{1,0:T(8,128)(2,1)S(1)} %get-tuple-element.120.refs_4_), kind=kOutput, calls=%fused_computation.1 | convolution fusion | flops 1610612736 | bytes 6815744 | tf_op jit(solution)/shard_map/dot_general | solution.py:238
  75.4 5.1 %collective-permute-done.16.refs_0_.refs_1_ = bf16[768,512]{1,0:T(8,128)(2,1)S(1)} collective-permute-done((bf16[768,512]{1,0:T(8,128)(2,1)S(1)}, bf16[768,512]{1,0:T(8,128)(2,1)S(1)}, u32[]{:S(2)}, u32[]{:S(2)}) %collective-permute-start.16) | collective-permute-done | bytes 786464 | tf_op jit(solution)/shard_map/ppermute | solution.py:161
  82.6 10.0 %collective-permute-done.19.refs_3_ = bf16[384,512]{1,0:T(8,128)(2,1)S(1)} collective-permute-done((bf16[384,512]{1,0:T(8,128)(2,1)S(1)}, bf16[384,512]{1,0:T(8,128)(2,1)S(1)}, u32[]{:S(2)}, u32[]{:S(2)}) %collective-permute-start.19) | collective-permute-done | bytes 393248 | tf_op jit(solution)/shard_map/ppermute | solution.py:165
  92.6 5.5 %collective-permute-done.20.refs_7_ = bf16[384,512]{1,0:T(8,128)(2,1)S(1)} collective-permute-done((bf16[384,512]{1,0:T(8,128)(2,1)S(1)}, bf16[384,512]{1,0:T(8,128)(2,1)S(1)}, u32[]{:S(2)}, u32[]{:S(2)}) %collective-permute-start.20) | collective-permute-done | bytes 393248 | tf_op jit(solution)/shard_map/ppermute | solution.py:165
  98.3 1.8 %fusion.2.refs_0_.refs_1_ = f32[512,1024]{1,0:T(8,128)S(1)} fusion(bf16[1536,512]{1,0:T(8,128)(2,1)S(1)} %get-tuple-element.138.refs_2_, bf16[1536,1024]{1,0:T(8,128)(2,1)S(1)} %get-tuple-element.120.refs_4_), kind=kOutput, calls=%fused_computation.2 | convolution fusion | flops 1610612736 | bytes 6815744 | tf_op jit(solution)/shard_map/dot_general | solution.py:238
  100.3 2.0 %collective-permute-start.28 = (bf16[512,1024]{1,0:T(8,128)(2,1)S(1)}, bf16[512,1024]{1,0:T(8,128)(2,1)S(1)}, u32[]{:S(2)}, u32[]{:S(2)}) collective-permute-start(bf16[512,1024]{1,0:T(8,128)(2,1)S(1)} %get-tuple-element.163), channel_id=1, source_target_pairs={{0,8},{2,10},{4,12},{6,14},{8,0},{10,2},{12,4},{14,6},{16,24},{18,... | collective-permute-start | bytes 3145736 | tf_op jit(solution)/shard_map/ppermute | solution.py:170
  103.5 1.8 %project.4 = (f32[192,1024]{1,0:T(8,128)S(1)}, bf16[192,1024]{1,0:T(8,128)(2,1)S(1)}, f32[8,128]{1,0:T(8,128)S(1)}) custom-call(bf16[1536,512]{1,0:T(8,128)(2,1)S(1)} %get-tuple-element.116.refs_0_, bf16[1536,512]{1,0:T(8,128)(2,1)S(1)} %get-tuple-element.129.refs_1_, bf16[1536,512]{1,0:T(8,128)(2,1)S(1)} %get-tuple-element.138.refs_2_, ...), custom_call_target="tpu_custom_call" | custom-call | bytes 1 | tf_op jit(solution)/shard_map/project/pallas_call | solution.py:108
  105.4 1.8 %project.5 = (f32[192,1024]{1,0:T(8,128)S(1)}, bf16[192,1024]{1,0:T(8,128)(2,1)S(1)}, f32[8,128]{1,0:T(8,128)S(1)}) custom-call(bf16[1536,512]{1,0:T(8,128)(2,1)S(1)} %get-tuple-element.116.refs_0_, bf16[1536,512]{1,0:T(8,128)(2,1)S(1)} %get-tuple-element.129.refs_1_, bf16[1536,512]{1,0:T(8,128)(2,1)S(1)} %get-tuple-element.138.refs_2_, ...), custom_call_target="tpu_custom_call" | custom-call | bytes 1 | tf_op jit(solution)/shard_map/project/pallas_call | solution.py:108
  107.8 1.8 %fusion.3.refs_4_ = f32[512,1024]{1,0:T(8,128)S(1)} fusion(bf16[1536,512]{1,0:T(8,128)(2,1)S(1)} %get-tuple-element.139.refs_3_, bf16[1536,1024]{1,0:T(8,128)(2,1)S(1)} %get-tuple-element.120.refs_4_), kind=kOutput, calls=%fused_computation.3 | convolution fusion | flops 1610612736 | bytes 6815744 | tf_op jit(solution)/shard_map/dot_general | solution.py:238
  110.4 1.8 %project.6 = (f32[192,1024]{1,0:T(8,128)S(1)}, bf16[192,1024]{1,0:T(8,128)(2,1)S(1)}, f32[8,128]{1,0:T(8,128)S(1)}) custom-call(bf16[1536,512]{1,0:T(8,128)(2,1)S(1)} %get-tuple-element.116.refs_0_, bf16[1536,512]{1,0:T(8,128)(2,1)S(1)} %get-tuple-element.129.refs_1_, bf16[1536,512]{1,0:T(8,128)(2,1)S(1)} %get-tuple-element.138.refs_2_, ...), custom_call_target="tpu_custom_call" | custom-call | bytes 1 | tf_op jit(solution)/shard_map/project/pallas_call | solution.py:108
  112.2 1.8 %project.7 = (f32[192,1024]{1,0:T(8,128)S(1)}, bf16[192,1024]{1,0:T(8,128)(2,1)S(1)}, f32[8,128]{1,0:T(8,128)S(1)}) custom-call(bf16[1536,512]{1,0:T(8,128)(2,1)S(1)} %get-tuple-element.116.refs_0_, bf16[1536,512]{1,0:T(8,128)(2,1)S(1)} %get-tuple-element.129.refs_1_, bf16[1536,512]{1,0:T(8,128)(2,1)S(1)} %get-tuple-element.138.refs_2_, ...), custom_call_target="tpu_custom_call" | custom-call | bytes 1 | tf_op jit(solution)/shard_map/project/pallas_call | solution.py:108
  114.6 8.2 %collective-permute-done.28.refs_2_ = bf16[512,1024]{1,0:T(8,128)(2,1)S(1)} collective-permute-done((bf16[512,1024]{1,0:T(8,128)(2,1)S(1)}, bf16[512,1024]{1,0:T(8,128)(2,1)S(1)}, u32[]{:S(2)}, u32[]{:S(2)}) %collective-permute-start.28) | collective-permute-done | bytes 1048608 | tf_op jit(solution)/shard_map/ppermute | solution.py:170
  122.8 2.3 %own_gradient.1 = (f32[512,1024]{1,0:T(8,128)}, f32[8,128]{1,0:T(8,128)S(1)}) custom-call(s32[4,8]{1,0:T(4,128)S(1)} %copy-done.3, f32[512,1024]{1,0:T(8,128)S(1)} %get-tuple-element.162.refs_1_, bf16[512,1024]{1,0:T(8,128)(2,1)S(1)} %collective-permute-done.28.refs_2_, bf16[512,1024]{1,0:T(8,128)(2,1)S(1)} %collective-permute-done.29.refs_3_, ...), custom_call_target="tpu_custom_call" | custom-call | bytes 1 | tf_op jit(solution)/shard_map/own_gradient/pallas_call | solution.py:108
  125.2 4.2 %collective-permute-done.27.refs_4_ = bf16[384,1024]{1,0:T(8,128)(2,1)S(1)} collective-permute-done((bf16[384,1024]{1,0:T(8,128)(2,1)S(1)}, bf16[384,1024]{1,0:T(8,128)(2,1)S(1)}, u32[]{:S(2)}, u32[]{:S(2)}) %collective-permute-start.27) | collective-permute-done | bytes 786464 | tf_op jit(solution)/shard_map/ppermute | solution.py:161
  (75 shorter events, 28.7 us)
Async XLA Ops:
  5.5 7.6 %collective-permute-start.8 = (bf16[2,192,512]{2,1,0:T(8,128)(2,1)S(1)}, bf16[2,192,512]{2,1,0:T(8,128)(2,1)S(1)}, u32[]{:S(2)}, u32[]{:S(2)}) collective-permute-start(bf16[2,192,512]{2,1,0:T(8,128)(2,1)S(1)} %get-tuple-element.99), channel_id=1, source_target_pairs={{0,2},{2,0},{4,6},{6,4},{8,10},{10,8},{12,14},{14,12},{16,18},{18,... | collective-permute-start | bytes 1179656 | tf_op jit(solution)/shard_map/ppermute | solution.py:158
  7.8 14.5 %collective-permute-start.2 = (bf16[384,1024]{1,0:T(8,128)(2,1)S(1)}, bf16[384,1024]{1,0:T(8,128)(2,1)S(1)}, u32[]{:S(2)}, u32[]{:S(2)}) collective-permute-start(bf16[384,1024]{1,0:T(8,128)(2,1)S(1)} %get-tuple-element.91.refs_0_.refs_2_), channel_id=1, source_target_pairs={{0,2},{2,0},{4,6},{6,4},{8,10},{10,8},{12,14},{14,12},{16,18},{18,... | collective-permute-start | bytes 2359304 | tf_op jit(solution)/shard_map/ppermute | solution.py:158
  8.3 12.3 %collective-permute-start.1 = (bf16[384,512]{1,0:T(8,128)(2,1)S(1)}, bf16[384,512]{1,0:T(8,128)(2,1)S(1)}, u32[]{:S(2)}, u32[]{:S(2)}) collective-permute-start(bf16[384,512]{1,0:T(8,128)(2,1)S(1)} %get-tuple-element.92), channel_id=1, source_target_pairs={{0,4},{2,6},{4,0},{6,2},{8,12},{10,14},{12,8},{14,10},{16,20},{18,... | collective-permute-start | bytes 1179656 | tf_op jit(solution)/shard_map/ppermute | solution.py:161
  10.9 11.4 %collective-permute-start.3 = (bf16[384,512]{1,0:T(8,128)(2,1)S(1)}, bf16[384,512]{1,0:T(8,128)(2,1)S(1)}, u32[]{:S(2)}, u32[]{:S(2)}) collective-permute-start(bf16[384,512]{1,0:T(8,128)(2,1)S(1)} %get-tuple-element.93.refs_8_), channel_id=1, source_target_pairs={{0,1},{1,0},{2,3},{3,2},{4,5},{5,4},{6,7},{7,6},{8,9},{9,8},{10,11... | collective-permute-start | bytes 1179656 | tf_op jit(solution)/shard_map/ppermute | solution.py:165
  12.4 27.4 %collective-permute-start.7 = (bf16[512,1024]{1,0:T(8,128)(2,1)S(1)}, bf16[512,1024]{1,0:T(8,128)(2,1)S(1)}, u32[]{:S(2)}, u32[]{:S(2)}) collective-permute-start(bf16[512,1024]{1,0:T(8,128)(2,1)S(1)} %get-tuple-element.97.refs_5_), channel_id=1, source_target_pairs={{0,0},{2,2},{4,4},{6,6},{8,16},{10,18},{12,20},{14,22},{16,8},{18,... | collective-permute-start | bytes 3145736 | tf_op jit(solution)/shard_map/ppermute | solution.py:170
  13.2 27.2 %collective-permute-start.6 = (bf16[512,1024]{1,0:T(8,128)(2,1)S(1)}, bf16[512,1024]{1,0:T(8,128)(2,1)S(1)}, u32[]{:S(2)}, u32[]{:S(2)}) collective-permute-start(bf16[512,1024]{1,0:T(8,128)(2,1)S(1)} %get-tuple-element.97.refs_5_), channel_id=1, source_target_pairs={{0,8},{2,10},{4,12},{6,14},{8,0},{10,2},{12,4},{14,6},{16,24},{18,... | collective-permute-start | bytes 3145736 | tf_op jit(solution)/shard_map/ppermute | solution.py:170
  20.6 19.2 %collective-permute-start.4 = (bf16[384,1024]{1,0:T(8,128)(2,1)S(1)}, bf16[384,1024]{1,0:T(8,128)(2,1)S(1)}, u32[]{:S(2)}, u32[]{:S(2)}) collective-permute-start(bf16[384,1024]{1,0:T(8,128)(2,1)S(1)} %get-tuple-element.91.refs_0_.refs_2_), channel_id=1, source_target_pairs={{0,4},{2,6},{4,0},{6,2},{8,12},{10,14},{12,8},{14,10},{16,20},{18,... | collective-permute-start | bytes 2359304 | tf_op jit(solution)/shard_map/ppermute | solution.py:161
  24.0 16.4 %collective-permute-start.5 = (bf16[384,512]{1,0:T(8,128)(2,1)S(1)}, bf16[384,512]{1,0:T(8,128)(2,1)S(1)}, u32[]{:S(2)}, u32[]{:S(2)}) collective-permute-start(bf16[384,512]{1,0:T(8,128)(2,1)S(1)} %get-tuple-element.96.refs_10_), channel_id=1, source_target_pairs={{0,1},{1,0},{2,3},{3,2},{4,5},{5,4},{6,7},{7,6},{8,9},{9,8},{10,11... | collective-permute-start | bytes 1179656 | tf_op jit(solution)/shard_map/ppermute | solution.py:165
  25.6 34.8 %collective-permute-start.14 = (bf16[1152,512]{1,0:T(8,128)(2,1)S(1)}, bf16[1152,512]{1,0:T(8,128)(2,1)S(1)}, u32[]{:S(2)}, u32[]{:S(2)}) collective-permute-start(bf16[1152,512]{1,0:T(8,128)(2,1)S(1)} %get-tuple-element.117.refs_0_.refs_4_), channel_id=1, source_target_pairs={{0,1},{1,0},{2,3},{3,2},{4,5},{5,4},{6,7},{7,6},{8,9},{9,8},{10,11... | collective-permute-start | bytes 3538952 | tf_op jit(solution)/shard_map/ppermute | solution.py:165
  41.0 11.1 %collective-permute-start.13 = (bf16[384,512]{1,0:T(8,128)(2,1)S(1)}, bf16[384,512]{1,0:T(8,128)(2,1)S(1)}, u32[]{:S(2)}, u32[]{:S(2)}) collective-permute-start(bf16[384,512]{1,0:T(8,128)(2,1)S(1)} %get-tuple-element.118), channel_id=1, source_target_pairs={{0,4},{2,6},{4,0},{6,2},{8,12},{10,14},{12,8},{14,10},{16,20},{18,... | collective-permute-start | bytes 1179656 | tf_op jit(solution)/shard_map/ppermute | solution.py:161
  42.0 30.8 %collective-permute-start.17 = (bf16[512,1024]{1,0:T(8,128)(2,1)S(1)}, bf16[512,1024]{1,0:T(8,128)(2,1)S(1)}, u32[]{:S(2)}, u32[]{:S(2)}) collective-permute-start(bf16[512,1024]{1,0:T(8,128)(2,1)S(1)} %get-tuple-element.131.refs_4_), channel_id=1, source_target_pairs={{0,0},{2,2},{4,4},{6,6},{8,16},{10,18},{12,20},{14,22},{16,8},{18,... | collective-permute-start | bytes 3145736 | tf_op jit(solution)/shard_map/ppermute | solution.py:170
  45.1 27.6 %collective-permute-start.18 = (bf16[512,1024]{1,0:T(8,128)(2,1)S(1)}, bf16[512,1024]{1,0:T(8,128)(2,1)S(1)}, u32[]{:S(2)}, u32[]{:S(2)}) collective-permute-start(bf16[512,1024]{1,0:T(8,128)(2,1)S(1)} %get-tuple-element.132), channel_id=1, source_target_pairs={{0,8},{2,10},{4,12},{6,14},{8,0},{10,2},{12,4},{14,6},{16,24},{18,... | collective-permute-start | bytes 3145736 | tf_op jit(solution)/shard_map/ppermute | solution.py:170
  60.5 10.3 %collective-permute-start.15 = (bf16[384,512]{1,0:T(8,128)(2,1)S(1)}, bf16[384,512]{1,0:T(8,128)(2,1)S(1)}, u32[]{:S(2)}, u32[]{:S(2)}) collective-permute-start(bf16[384,512]{1,0:T(8,128)(2,1)S(1)} %get-tuple-element.127.refs_2_), channel_id=1, source_target_pairs={{0,1},{1,0},{2,3},{3,2},{4,5},{5,4},{6,7},{7,6},{8,9},{9,8},{10,11... | collective-permute-start | bytes 1179656 | tf_op jit(solution)/shard_map/ppermute | solution.py:165
  62.0 18.5 %collective-permute-start.16 = (bf16[768,512]{1,0:T(8,128)(2,1)S(1)}, bf16[768,512]{1,0:T(8,128)(2,1)S(1)}, u32[]{:S(2)}, u32[]{:S(2)}) collective-permute-start(bf16[768,512]{1,0:T(8,128)(2,1)S(1)} %get-tuple-element.130), channel_id=1, source_target_pairs={{0,4},{2,6},{4,0},{6,2},{8,12},{10,14},{12,8},{14,10},{16,20},{18,... | collective-permute-start | bytes 2359304 | tf_op jit(solution)/shard_map/ppermute | solution.py:161
  72.9 27.3 %collective-permute-start.21 = (bf16[512,1024]{1,0:T(8,128)(2,1)S(1)}, bf16[512,1024]{1,0:T(8,128)(2,1)S(1)}, u32[]{:S(2)}, u32[]{:S(2)}) collective-permute-start(bf16[512,1024]{1,0:T(8,128)(2,1)S(1)} %get-tuple-element.140), channel_id=1, source_target_pairs={{0,8},{2,10},{4,12},{6,14},{8,0},{10,2},{12,4},{14,6},{16,24},{18,... | collective-permute-start | bytes 3145736 | tf_op jit(solution)/shard_map/ppermute | solution.py:170
  74.6 25.5 %collective-permute-start.22 = (bf16[512,1024]{1,0:T(8,128)(2,1)S(1)}, bf16[512,1024]{1,0:T(8,128)(2,1)S(1)}, u32[]{:S(2)}, u32[]{:S(2)}) collective-permute-start(bf16[512,1024]{1,0:T(8,128)(2,1)S(1)} %get-tuple-element.141), channel_id=1, source_target_pairs={{0,0},{2,2},{4,4},{6,6},{8,16},{10,18},{12,20},{14,22},{16,8},{18,... | collective-permute-start | bytes 3145736 | tf_op jit(solution)/shard_map/ppermute | solution.py:170
  80.5 12.1 %collective-permute-start.19 = (bf16[384,512]{1,0:T(8,128)(2,1)S(1)}, bf16[384,512]{1,0:T(8,128)(2,1)S(1)}, u32[]{:S(2)}, u32[]{:S(2)}) collective-permute-start(bf16[384,512]{1,0:T(8,128)(2,1)S(1)} %get-tuple-element.135.refs_2_), channel_id=1, source_target_pairs={{0,1},{1,0},{2,3},{3,2},{4,5},{5,4},{6,7},{7,6},{8,9},{9,8},{10,11... | collective-permute-start | bytes 1179656 | tf_op jit(solution)/shard_map/ppermute | solution.py:165
  81.1 17.0 %collective-permute-start.20 = (bf16[384,512]{1,0:T(8,128)(2,1)S(1)}, bf16[384,512]{1,0:T(8,128)(2,1)S(1)}, u32[]{:S(2)}, u32[]{:S(2)}) collective-permute-start(bf16[384,512]{1,0:T(8,128)(2,1)S(1)} %get-tuple-element.136.refs_6_), channel_id=1, source_target_pairs={{0,1},{1,0},{2,3},{3,2},{4,5},{5,4},{6,7},{7,6},{8,9},{9,8},{10,11... | collective-permute-start | bytes 1179656 | tf_op jit(solution)/shard_map/ppermute | solution.py:165
  100.3 22.5 %collective-permute-start.28 = (bf16[512,1024]{1,0:T(8,128)(2,1)S(1)}, bf16[512,1024]{1,0:T(8,128)(2,1)S(1)}, u32[]{:S(2)}, u32[]{:S(2)}) collective-permute-start(bf16[512,1024]{1,0:T(8,128)(2,1)S(1)} %get-tuple-element.163), channel_id=1, source_target_pairs={{0,8},{2,10},{4,12},{6,14},{8,0},{10,2},{12,4},{14,6},{16,24},{18,... | collective-permute-start | bytes 3145736 | tf_op jit(solution)/shard_map/ppermute | solution.py:170
  102.3 20.5 %collective-permute-start.29 = (bf16[512,1024]{1,0:T(8,128)(2,1)S(1)}, bf16[512,1024]{1,0:T(8,128)(2,1)S(1)}, u32[]{:S(2)}, u32[]{:S(2)}) collective-permute-start(bf16[512,1024]{1,0:T(8,128)(2,1)S(1)} %get-tuple-element.164), channel_id=1, source_target_pairs={{0,0},{2,2},{4,4},{6,6},{8,16},{10,18},{12,20},{14,22},{16,8},{18,... | collective-permute-start | bytes 3145736 | tf_op jit(solution)/shard_map/ppermute | solution.py:170
  105.3 4.3 %collective-permute-start.23 = (bf16[192,1024]{1,0:T(8,128)(2,1)S(1)}, bf16[192,1024]{1,0:T(8,128)(2,1)S(1)}, u32[]{:S(2)}, u32[]{:S(2)}) collective-permute-start(bf16[192,1024]{1,0:T(8,128)(2,1)S(1)} %get-tuple-element.150), channel_id=1, source_target_pairs={{0,2},{2,0},{4,6},{6,4},{8,10},{10,8},{12,14},{14,12},{16,18},{18,... | collective-permute-start | bytes 1179656 | tf_op jit(solution)/shard_map/ppermute | solution.py:158
  109.8 19.5 %collective-permute-start.27 = (bf16[384,1024]{1,0:T(8,128)(2,1)S(1)}, bf16[384,1024]{1,0:T(8,128)(2,1)S(1)}, u32[]{:S(2)}, u32[]{:S(2)}) collective-permute-start(bf16[384,1024]{1,0:T(8,128)(2,1)S(1)} %get-tuple-element.161), channel_id=1, source_target_pairs={{0,4},{2,6},{4,0},{6,2},{8,12},{10,14},{12,8},{14,10},{16,20},{18,... | collective-permute-start | bytes 2359304 | tf_op jit(solution)/shard_map/ppermute | solution.py:161
  114.0 11.1 %collective-permute-start.25 = (bf16[192,1024]{1,0:T(8,128)(2,1)S(1)}, bf16[192,1024]{1,0:T(8,128)(2,1)S(1)}, u32[]{:S(2)}, u32[]{:S(2)}) collective-permute-start(bf16[192,1024]{1,0:T(8,128)(2,1)S(1)} %get-tuple-element.157), channel_id=1, source_target_pairs={{0,2},{2,0},{4,6},{6,4},{8,10},{10,8},{12,14},{14,12},{16,18},{18,... | collective-permute-start | bytes 1179656 | tf_op jit(solution)/shard_map/ppermute | solution.py:158
  114.1 11.1 %collective-permute-start.26 = (bf16[192,1024]{1,0:T(8,128)(2,1)S(1)}, bf16[192,1024]{1,0:T(8,128)(2,1)S(1)}, u32[]{:S(2)}, u32[]{:S(2)}) collective-permute-start(bf16[192,1024]{1,0:T(8,128)(2,1)S(1)} %get-tuple-element.160), channel_id=1, source_target_pairs={{0,2},{2,0},{4,6},{6,4},{8,10},{10,8},{12,14},{14,12},{16,18},{18,... | collective-permute-start | bytes 1179656 | tf_op jit(solution)/shard_map/ppermute | solution.py:158
  (10 other events, 26.6 us)

commit v6 on v5

--- a/solution.py
+++ b/solution.py
@@ -185,9 +185,6 @@
     def cross_of(k):
         return [(far[k], flat, (0, 0)), (swaps[k], one, (1, 0, 0))]
 
-    (cross_0, near_0), _ = line.run("first", [join(cross_of(0)), join(near_of(0))])
-    cross_0, near_y = over_x(cross_0), over_y(near_0)
-
     def turn_kernel(a, out):
         for i in range(teams):
             j = lax.rem(spot()[3] + teams - i, teams)
@@ -206,6 +203,8 @@
         ],
     )
     cot_x, cot_core = over_x(cot), over_core(cot)
+    (cross_0, near_0), _ = line.run("first", [join(cross_of(0)), join(near_of(0))])
+    cross_0, near_y = over_x(cross_0), over_y(near_0)
     came = {1: [over_edges(masked, i) for i in range(2)]}
 
     _, (cross_0, cot_core, *near_y) = line.run("arrived", [], [cross_0, cot_core, *near_y])

time: 132 us -> 131 us (level)
  transfers between devices with their start and end apart: 30 -> 30, of which waited for: 14 -> 13; matrix products, arithmetic and copies ran while one was open for 6% -> 6% of each run, Pallas kernels for 9% -> 10%
where the time goes in v6:
time: 131 us; the launch traced here: 129 us
  waiting for transfers between devices  71 us (54%)
  starting transfers between devices  32.3 us (25%)
  Pallas kernels  15.3 us (12%)
  matrix products  7.22 us (6%)
  local copies, waits for them, and re-layouts  2.64 us (2%)
    ppermute x6, waiting for transfers between devices, over_y(): lax.ppermute(a, 'tensor', [(i, (i + s) % teams) for i in range(teams)])  32.1 us
    ppermute x5, waiting for transfers between devices, over_x(): return lax.ppermute(a, 'fsdp', [(i, i ^ 2) for i in range(group)])  28.5 us
    ppermute x8, starting transfers between devices, over_z(): lax.ppermute(a, 'fsdp', [(4 * p + i, 4 * q + i) for p, q in pairs for i i...  15.2 us
    pallas_call x25, Pallas kernels, run(): pl.pallas_call(body, out_shape=[shape for shape, _ in made] + [jax.ShapeD...  13.5 us
    ppermute x8, waiting for transfers between devices, over_z(): lax.ppermute(a, 'fsdp', [(4 * p + i, 4 * q + i) for p, q in pairs for i i...  8.86 us
    ppermute x6, starting transfers between devices, over_y(): lax.ppermute(a, 'tensor', [(i, (i + s) % teams) for i in range(teams)])  7.27 us
    dot_general x4, matrix products, terms_of(): lax.dot_general(a, cots, (((0,), (0,)), ((), ())), preferred_element_type...  7.22 us
    ppermute x5, starting transfers between devices, over_x(): return lax.ppermute(a, 'fsdp', [(i, i ^ 2) for i in range(group)])  6.47 us
  transfers between devices with their start and end apart: 30, of which 13 were waited for; matrix products, arithmetic and copies ran while one was open for 6% of the time, Pallas kernels for 10%

profile of v6, /device:TPU:0, one launch (start us, length us, event | category | flops | bytes accessed | tf_op | source)
XLA Modules:
  0.0 129.3 jit_solution(2712915085069851956)
XLA Ops:
  1.4 1.9 %copy-done = bf16[192,8192]{1,0:T(8,128)(2,1)S(1)} copy-done((bf16[192,8192]{1,0:T(8,128)(2,1)S(1)}, bf16[192,8192]{1,0:T(8,128)(2,1)}, u32[]{:S(2)}) %copy-start) | copy-done | bytes 3145752
  7.1 2.8 %collective-permute-start.1 = (bf16[384,512]{1,0:T(8,128)(2,1)S(1)}, bf16[384,512]{1,0:T(8,128)(2,1)S(1)}, u32[]{:S(2)}, u32[]{:S(2)}) collective-permute-start(bf16[384,512]{1,0:T(8,128)(2,1)S(1)} %get-tuple-element.92), channel_id=1, source_target_pairs={{0,4},{2,6},{4,0},{6,2},{8,12},{10,14},{12,8},{14,10},{16,20},{18,... | collective-permute-start | bytes 1179656 | tf_op jit(solution)/shard_map/ppermute | solution.py:161
  12.1 4.4 %collective-permute-start.6 = (bf16[512,1024]{1,0:T(8,128)(2,1)S(1)}, bf16[512,1024]{1,0:T(8,128)(2,1)S(1)}, u32[]{:S(2)}, u32[]{:S(2)}) collective-permute-start(bf16[512,1024]{1,0:T(8,128)(2,1)S(1)} %get-tuple-element.97.refs_5_), channel_id=1, source_target_pairs={{0,8},{2,10},{4,12},{6,14},{8,0},{10,2},{12,4},{14,6},{16,24},{18,... | collective-permute-start | bytes 3145736 | tf_op jit(solution)/shard_map/ppermute | solution.py:170
  16.5 2.9 %collective-permute-done.1.refs_0_ = bf16[384,512]{1,0:T(8,128)(2,1)S(1)} collective-permute-done((bf16[384,512]{1,0:T(8,128)(2,1)S(1)}, bf16[384,512]{1,0:T(8,128)(2,1)S(1)}, u32[]{:S(2)}, u32[]{:S(2)}) %collective-permute-start.1) | collective-permute-done | bytes 393248 | tf_op jit(solution)/shard_map/ppermute | solution.py:161
  25.2 13.4 %collective-permute-done.4.refs_0_.refs_4_.refs_6_ = bf16[384,1024]{1,0:T(8,128)(2,1)S(1)} collective-permute-done((bf16[384,1024]{1,0:T(8,128)(2,1)S(1)}, bf16[384,1024]{1,0:T(8,128)(2,1)S(1)}, u32[]{:S(2)}, u32[]{:S(2)}) %collective-permute-start.4) | collective-permute-done | bytes 786464 | tf_op jit(solution)/shard_map/ppermute | solution.py:161
  42.0 1.8 %fusion.refs_0_.refs_2_ = f32[512,1024]{1,0:T(8,128)S(1)} fusion(bf16[1536,512]{1,0:T(8,128)(2,1)S(1)} %get-tuple-element.116.refs_0_, bf16[1536,1024]{1,0:T(8,128)(2,1)S(1)} %get-tuple-element.120.refs_4_), kind=kOutput, calls=%fused_computation | convolution fusion | flops 1610612736 | bytes 6815744 | tf_op jit(solution)/shard_map/dot_general | solution.py:237
  43.9 4.1 %collective-permute-start.18 = (bf16[512,1024]{1,0:T(8,128)(2,1)S(1)}, bf16[512,1024]{1,0:T(8,128)(2,1)S(1)}, u32[]{:S(2)}, u32[]{:S(2)}) collective-permute-start(bf16[512,1024]{1,0:T(8,128)(2,1)S(1)} %get-tuple-element.132), channel_id=1, source_target_pairs={{0,8},{2,10},{4,12},{6,14},{8,0},{10,2},{12,4},{14,6},{16,24},{18,... | collective-permute-start | bytes 3145736 | tf_op jit(solution)/shard_map/ppermute | solution.py:170
  48.1 2.9 %collective-permute-done.13.refs_0_ = bf16[384,512]{1,0:T(8,128)(2,1)S(1)} collective-permute-done((bf16[384,512]{1,0:T(8,128)(2,1)S(1)}, bf16[384,512]{1,0:T(8,128)(2,1)S(1)}, u32[]{:S(2)}, u32[]{:S(2)}) %collective-permute-start.13) | collective-permute-done | bytes 393248 | tf_op jit(solution)/shard_map/ppermute | solution.py:161
  51.0 8.3 %collective-permute-done.14.refs_1_ = bf16[1152,512]{1,0:T(8,128)(2,1)S(1)} collective-permute-done((bf16[1152,512]{1,0:T(8,128)(2,1)S(1)}, bf16[1152,512]{1,0:T(8,128)(2,1)S(1)}, u32[]{:S(2)}, u32[]{:S(2)}) %collective-permute-start.14) | collective-permute-done | bytes 1179680 | tf_op jit(solution)/shard_map/ppermute | solution.py:165
  61.4 8.3 %collective-permute-done.15.refs_3_ = bf16[384,512]{1,0:T(8,128)(2,1)S(1)} collective-permute-done((bf16[384,512]{1,0:T(8,128)(2,1)S(1)}, bf16[384,512]{1,0:T(8,128)(2,1)S(1)}, u32[]{:S(2)}, u32[]{:S(2)}) %collective-permute-start.15) | collective-permute-done | bytes 393248 | tf_op jit(solution)/shard_map/ppermute | solution.py:165
  69.7 1.8 %fusion.1.refs_0_.refs_3_ = f32[512,1024]{1,0:T(8,128)S(1)} fusion(bf16[1536,512]{1,0:T(8,128)(2,1)S(1)} %get-tuple-element.129.refs_1_, bf16[1536,1024]{1,0:T(8,128)(2,1)S(1)} %get-tuple-element.120.refs_4_), kind=kOutput, calls=%fused_computation.1 | convolution fusion | flops 1610612736 | bytes 6815744 | tf_op jit(solution)/shard_map/dot_general | solution.py:237
  74.2 5.1 %collective-permute-done.16.refs_0_.refs_1_ = bf16[768,512]{1,0:T(8,128)(2,1)S(1)} collective-permute-done((bf16[768,512]{1,0:T(8,128)(2,1)S(1)}, bf16[768,512]{1,0:T(8,128)(2,1)S(1)}, u32[]{:S(2)}, u32[]{:S(2)}) %collective-permute-start.16) | collective-permute-done | bytes 786464 | tf_op jit(solution)/shard_map/ppermute | solution.py:161
  81.5 10.0 %collective-permute-done.19.refs_3_ = bf16[384,512]{1,0:T(8,128)(2,1)S(1)} collective-permute-done((bf16[384,512]{1,0:T(8,128)(2,1)S(1)}, bf16[384,512]{1,0:T(8,128)(2,1)S(1)}, u32[]{:S(2)}, u32[]{:S(2)}) %collective-permute-start.19) | collective-permute-done | bytes 393248 | tf_op jit(solution)/shard_map/ppermute | solution.py:165
  91.5 5.5 %collective-permute-done.20.refs_7_ = bf16[384,512]{1,0:T(8,128)(2,1)S(1)} collective-permute-done((bf16[384,512]{1,0:T(8,128)(2,1)S(1)}, bf16[384,512]{1,0:T(8,128)(2,1)S(1)}, u32[]{:S(2)}, u32[]{:S(2)}) %collective-permute-start.20) | collective-permute-done | bytes 393248 | tf_op jit(solution)/shard_map/ppermute | solution.py:165
  97.2 1.8 %fusion.2.refs_0_.refs_1_ = f32[512,1024]{1,0:T(8,128)S(1)} fusion(bf16[1536,512]{1,0:T(8,128)(2,1)S(1)} %get-tuple-element.138.refs_2_, bf16[1536,1024]{1,0:T(8,128)(2,1)S(1)} %get-tuple-element.120.refs_4_), kind=kOutput, calls=%fused_computation.2 | convolution fusion | flops 1610612736 | bytes 6815744 | tf_op jit(solution)/shard_map/dot_general | solution.py:237
  99.2 2.0 %collective-permute-start.28 = (bf16[512,1024]{1,0:T(8,128)(2,1)S(1)}, bf16[512,1024]{1,0:T(8,128)(2,1)S(1)}, u32[]{:S(2)}, u32[]{:S(2)}) collective-permute-start(bf16[512,1024]{1,0:T(8,128)(2,1)S(1)} %get-tuple-element.163), channel_id=1, source_target_pairs={{0,8},{2,10},{4,12},{6,14},{8,0},{10,2},{12,4},{14,6},{16,24},{18,... | collective-permute-start | bytes 3145736 | tf_op jit(solution)/shard_map/ppermute | solution.py:170
  102.4 1.8 %project.4 = (f32[192,1024]{1,0:T(8,128)S(1)}, bf16[192,1024]{1,0:T(8,128)(2,1)S(1)}, f32[8,128]{1,0:T(8,128)S(1)}) custom-call(bf16[1536,512]{1,0:T(8,128)(2,1)S(1)} %get-tuple-element.116.refs_0_, bf16[1536,512]{1,0:T(8,128)(2,1)S(1)} %get-tuple-element.129.refs_1_, bf16[1536,512]{1,0:T(8,128)(2,1)S(1)} %get-tuple-element.138.refs_2_, ...), custom_call_target="tpu_custom_call" | custom-call | bytes 1 | tf_op jit(solution)/shard_map/project/pallas_call | solution.py:108
  104.2 1.8 %project.5 = (f32[192,1024]{1,0:T(8,128)S(1)}, bf16[192,1024]{1,0:T(8,128)(2,1)S(1)}, f32[8,128]{1,0:T(8,128)S(1)}) custom-call(bf16[1536,512]{1,0:T(8,128)(2,1)S(1)} %get-tuple-element.116.refs_0_, bf16[1536,512]{1,0:T(8,128)(2,1)S(1)} %get-tuple-element.129.refs_1_, bf16[1536,512]{1,0:T(8,128)(2,1)S(1)} %get-tuple-element.138.refs_2_, ...), custom_call_target="tpu_custom_call" | custom-call | bytes 1 | tf_op jit(solution)/shard_map/project/pallas_call | solution.py:108
  106.6 1.8 %fusion.3.refs_4_ = f32[512,1024]{1,0:T(8,128)S(1)} fusion(bf16[1536,512]{1,0:T(8,128)(2,1)S(1)} %get-tuple-element.139.refs_3_, bf16[1536,1024]{1,0:T(8,128)(2,1)S(1)} %get-tuple-element.120.refs_4_), kind=kOutput, calls=%fused_computation.3 | convolution fusion | flops 1610612736 | bytes 6815744 | tf_op jit(solution)/shard_map/dot_general | solution.py:237
  109.3 1.8 %project.6 = (f32[192,1024]{1,0:T(8,128)S(1)}, bf16[192,1024]{1,0:T(8,128)(2,1)S(1)}, f32[8,128]{1,0:T(8,128)S(1)}) custom-call(bf16[1536,512]{1,0:T(8,128)(2,1)S(1)} %get-tuple-element.116.refs_0_, bf16[1536,512]{1,0:T(8,128)(2,1)S(1)} %get-tuple-element.129.refs_1_, bf16[1536,512]{1,0:T(8,128)(2,1)S(1)} %get-tuple-element.138.refs_2_, ...), custom_call_target="tpu_custom_call" | custom-call | bytes 1 | tf_op jit(solution)/shard_map/project/pallas_call | solution.py:108
  111.1 1.8 %project.7 = (f32[192,1024]{1,0:T(8,128)S(1)}, bf16[192,1024]{1,0:T(8,128)(2,1)S(1)}, f32[8,128]{1,0:T(8,128)S(1)}) custom-call(bf16[1536,512]{1,0:T(8,128)(2,1)S(1)} %get-tuple-element.116.refs_0_, bf16[1536,512]{1,0:T(8,128)(2,1)S(1)} %get-tuple-element.129.refs_1_, bf16[1536,512]{1,0:T(8,128)(2,1)S(1)} %get-tuple-element.138.refs_2_, ...), custom_call_target="tpu_custom_call" | custom-call | bytes 1 | tf_op jit(solution)/shard_map/project/pallas_call | solution.py:108
  113.5 8.2 %collective-permute-done.28.refs_2_ = bf16[512,1024]{1,0:T(8,128)(2,1)S(1)} collective-permute-done((bf16[512,1024]{1,0:T(8,128)(2,1)S(1)}, bf16[512,1024]{1,0:T(8,128)(2,1)S(1)}, u32[]{:S(2)}, u32[]{:S(2)}) %collective-permute-start.28) | collective-permute-done | bytes 1048608 | tf_op jit(solution)/shard_map/ppermute | solution.py:170
  121.7 2.3 %own_gradient.1 = (f32[512,1024]{1,0:T(8,128)}, f32[8,128]{1,0:T(8,128)S(1)}) custom-call(s32[4,8]{1,0:T(4,128)S(1)} %copy-done.3, f32[512,1024]{1,0:T(8,128)S(1)} %get-tuple-element.162.refs_1_, bf16[512,1024]{1,0:T(8,128)(2,1)S(1)} %collective-permute-done.28.refs_2_, bf16[512,1024]{1,0:T(8,128)(2,1)S(1)} %collective-permute-done.29.refs_3_, ...), custom_call_target="tpu_custom_call" | custom-call | bytes 1 | tf_op jit(solution)/shard_map/own_gradient/pallas_call | solution.py:108
  124.0 4.2 %collective-permute-done.27.refs_4_ = bf16[384,1024]{1,0:T(8,128)(2,1)S(1)} collective-permute-done((bf16[384,1024]{1,0:T(8,128)(2,1)S(1)}, bf16[384,1024]{1,0:T(8,128)(2,1)S(1)}, u32[]{:S(2)}, u32[]{:S(2)}) %collective-permute-start.27) | collective-permute-done | bytes 786464 | tf_op jit(solution)/shard_map/ppermute | solution.py:161
  (75 shorter events, 27.6 us)
Async XLA Ops:
  5.5 6.6 %collective-permute-start.8 = (bf16[2,192,512]{2,1,0:T(8,128)(2,1)S(1)}, bf16[2,192,512]{2,1,0:T(8,128)(2,1)S(1)}, u32[]{:S(2)}, u32[]{:S(2)}) collective-permute-start(bf16[2,192,512]{2,1,0:T(8,128)(2,1)S(1)} %get-tuple-element.99), channel_id=1, source_target_pairs={{0,2},{2,0},{4,6},{6,4},{8,10},{10,8},{12,14},{14,12},{16,18},{18,... | collective-permute-start | bytes 1179656 | tf_op jit(solution)/shard_map/ppermute | solution.py:158
  6.5 14.6 %collective-permute-start.2 = (bf16[384,1024]{1,0:T(8,128)(2,1)S(1)}, bf16[384,1024]{1,0:T(8,128)(2,1)S(1)}, u32[]{:S(2)}, u32[]{:S(2)}) collective-permute-start(bf16[384,1024]{1,0:T(8,128)(2,1)S(1)} %get-tuple-element.87.refs_0_.refs_2_), channel_id=1, source_target_pairs={{0,2},{2,0},{4,6},{6,4},{8,10},{10,8},{12,14},{14,12},{16,18},{18,... | collective-permute-start | bytes 2359304 | tf_op jit(solution)/shard_map/ppermute | solution.py:158
  7.1 12.3 %collective-permute-start.1 = (bf16[384,512]{1,0:T(8,128)(2,1)S(1)}, bf16[384,512]{1,0:T(8,128)(2,1)S(1)}, u32[]{:S(2)}, u32[]{:S(2)}) collective-permute-start(bf16[384,512]{1,0:T(8,128)(2,1)S(1)} %get-tuple-element.92), channel_id=1, source_target_pairs={{0,4},{2,6},{4,0},{6,2},{8,12},{10,14},{12,8},{14,10},{16,20},{18,... | collective-permute-start | bytes 1179656 | tf_op jit(solution)/shard_map/ppermute | solution.py:161
  9.9 11.3 %collective-permute-start.3 = (bf16[384,512]{1,0:T(8,128)(2,1)S(1)}, bf16[384,512]{1,0:T(8,128)(2,1)S(1)}, u32[]{:S(2)}, u32[]{:S(2)}) collective-permute-start(bf16[384,512]{1,0:T(8,128)(2,1)S(1)} %get-tuple-element.93.refs_8_), channel_id=1, source_target_pairs={{0,1},{1,0},{2,3},{3,2},{4,5},{5,4},{6,7},{7,6},{8,9},{9,8},{10,11... | collective-permute-start | bytes 1179656 | tf_op jit(solution)/shard_map/ppermute | solution.py:165
  11.4 27.2 %collective-permute-start.7 = (bf16[512,1024]{1,0:T(8,128)(2,1)S(1)}, bf16[512,1024]{1,0:T(8,128)(2,1)S(1)}, u32[]{:S(2)}, u32[]{:S(2)}) collective-permute-start(bf16[512,1024]{1,0:T(8,128)(2,1)S(1)} %get-tuple-element.97.refs_5_), channel_id=1, source_target_pairs={{0,0},{2,2},{4,4},{6,6},{8,16},{10,18},{12,20},{14,22},{16,8},{18,... | collective-permute-start | bytes 3145736 | tf_op jit(solution)/shard_map/ppermute | solution.py:170
  12.1 27.1 %collective-permute-start.6 = (bf16[512,1024]{1,0:T(8,128)(2,1)S(1)}, bf16[512,1024]{1,0:T(8,128)(2,1)S(1)}, u32[]{:S(2)}, u32[]{:S(2)}) collective-permute-start(bf16[512,1024]{1,0:T(8,128)(2,1)S(1)} %get-tuple-element.97.refs_5_), channel_id=1, source_target_pairs={{0,8},{2,10},{4,12},{6,14},{8,0},{10,2},{12,4},{14,6},{16,24},{18,... | collective-permute-start | bytes 3145736 | tf_op jit(solution)/shard_map/ppermute | solution.py:170
  19.4 19.2 %collective-permute-start.4 = (bf16[384,1024]{1,0:T(8,128)(2,1)S(1)}, bf16[384,1024]{1,0:T(8,128)(2,1)S(1)}, u32[]{:S(2)}, u32[]{:S(2)}) collective-permute-start(bf16[384,1024]{1,0:T(8,128)(2,1)S(1)} %get-tuple-element.87.refs_0_.refs_2_), channel_id=1, source_target_pairs={{0,4},{2,6},{4,0},{6,2},{8,12},{10,14},{12,8},{14,10},{16,20},{18,... | collective-permute-start | bytes 2359304 | tf_op jit(solution)/shard_map/ppermute | solution.py:161
  22.9 16.4 %collective-permute-start.5 = (bf16[384,512]{1,0:T(8,128)(2,1)S(1)}, bf16[384,512]{1,0:T(8,128)(2,1)S(1)}, u32[]{:S(2)}, u32[]{:S(2)}) collective-permute-start(bf16[384,512]{1,0:T(8,128)(2,1)S(1)} %get-tuple-element.96.refs_10_), channel_id=1, source_target_pairs={{0,1},{1,0},{2,3},{3,2},{4,5},{5,4},{6,7},{7,6},{8,9},{9,8},{10,11... | collective-permute-start | bytes 1179656 | tf_op jit(solution)/shard_map/ppermute | solution.py:165
  24.5 34.8 %collective-permute-start.14 = (bf16[1152,512]{1,0:T(8,128)(2,1)S(1)}, bf16[1152,512]{1,0:T(8,128)(2,1)S(1)}, u32[]{:S(2)}, u32[]{:S(2)}) collective-permute-start(bf16[1152,512]{1,0:T(8,128)(2,1)S(1)} %get-tuple-element.117.refs_0_.refs_4_), channel_id=1, source_target_pairs={{0,1},{1,0},{2,3},{3,2},{4,5},{5,4},{6,7},{7,6},{8,9},{9,8},{10,11... | collective-permute-start | bytes 3538952 | tf_op jit(solution)/shard_map/ppermute | solution.py:165
  39.9 11.1 %collective-permute-start.13 = (bf16[384,512]{1,0:T(8,128)(2,1)S(1)}, bf16[384,512]{1,0:T(8,128)(2,1)S(1)}, u32[]{:S(2)}, u32[]{:S(2)}) collective-permute-start(bf16[384,512]{1,0:T(8,128)(2,1)S(1)} %get-tuple-element.118), channel_id=1, source_target_pairs={{0,4},{2,6},{4,0},{6,2},{8,12},{10,14},{12,8},{14,10},{16,20},{18,... | collective-permute-start | bytes 1179656 | tf_op jit(solution)/shard_map/ppermute | solution.py:161
  40.7 30.9 %collective-permute-start.17 = (bf16[512,1024]{1,0:T(8,128)(2,1)S(1)}, bf16[512,1024]{1,0:T(8,128)(2,1)S(1)}, u32[]{:S(2)}, u32[]{:S(2)}) collective-permute-start(bf16[512,1024]{1,0:T(8,128)(2,1)S(1)} %get-tuple-element.131.refs_4_), channel_id=1, source_target_pairs={{0,0},{2,2},{4,4},{6,6},{8,16},{10,18},{12,20},{14,22},{16,8},{18,... | collective-permute-start | bytes 3145736 | tf_op jit(solution)/shard_map/ppermute | solution.py:170
  43.9 27.6 %collective-permute-start.18 = (bf16[512,1024]{1,0:T(8,128)(2,1)S(1)}, bf16[512,1024]{1,0:T(8,128)(2,1)S(1)}, u32[]{:S(2)}, u32[]{:S(2)}) collective-permute-start(bf16[512,1024]{1,0:T(8,128)(2,1)S(1)} %get-tuple-element.132), channel_id=1, source_target_pairs={{0,8},{2,10},{4,12},{6,14},{8,0},{10,2},{12,4},{14,6},{16,24},{18,... | collective-permute-start | bytes 3145736 | tf_op jit(solution)/shard_map/ppermute | solution.py:170
  59.3 10.3 %collective-permute-start.15 = (bf16[384,512]{1,0:T(8,128)(2,1)S(1)}, bf16[384,512]{1,0:T(8,128)(2,1)S(1)}, u32[]{:S(2)}, u32[]{:S(2)}) collective-permute-start(bf16[384,512]{1,0:T(8,128)(2,1)S(1)} %get-tuple-element.127.refs_2_), channel_id=1, source_target_pairs={{0,1},{1,0},{2,3},{3,2},{4,5},{5,4},{6,7},{7,6},{8,9},{9,8},{10,11... | collective-permute-start | bytes 1179656 | tf_op jit(solution)/shard_map/ppermute | solution.py:165
  60.8 18.5 %collective-permute-start.16 = (bf16[768,512]{1,0:T(8,128)(2,1)S(1)}, bf16[768,512]{1,0:T(8,128)(2,1)S(1)}, u32[]{:S(2)}, u32[]{:S(2)}) collective-permute-start(bf16[768,512]{1,0:T(8,128)(2,1)S(1)} %get-tuple-element.130), channel_id=1, source_target_pairs={{0,4},{2,6},{4,0},{6,2},{8,12},{10,14},{12,8},{14,10},{16,20},{18,... | collective-permute-start | bytes 2359304 | tf_op jit(solution)/shard_map/ppermute | solution.py:161
  71.7 27.3 %collective-permute-start.21 = (bf16[512,1024]{1,0:T(8,128)(2,1)S(1)}, bf16[512,1024]{1,0:T(8,128)(2,1)S(1)}, u32[]{:S(2)}, u32[]{:S(2)}) collective-permute-start(bf16[512,1024]{1,0:T(8,128)(2,1)S(1)} %get-tuple-element.140), channel_id=1, source_target_pairs={{0,8},{2,10},{4,12},{6,14},{8,0},{10,2},{12,4},{14,6},{16,24},{18,... | collective-permute-start | bytes 3145736 | tf_op jit(solution)/shard_map/ppermute | solution.py:170
  73.5 25.5 %collective-permute-start.22 = (bf16[512,1024]{1,0:T(8,128)(2,1)S(1)}, bf16[512,1024]{1,0:T(8,128)(2,1)S(1)}, u32[]{:S(2)}, u32[]{:S(2)}) collective-permute-start(bf16[512,1024]{1,0:T(8,128)(2,1)S(1)} %get-tuple-element.141), channel_id=1, source_target_pairs={{0,0},{2,2},{4,4},{6,6},{8,16},{10,18},{12,20},{14,22},{16,8},{18,... | collective-permute-start | bytes 3145736 | tf_op jit(solution)/shard_map/ppermute | solution.py:170
  79.4 12.1 %collective-permute-start.19 = (bf16[384,512]{1,0:T(8,128)(2,1)S(1)}, bf16[384,512]{1,0:T(8,128)(2,1)S(1)}, u32[]{:S(2)}, u32[]{:S(2)}) collective-permute-start(bf16[384,512]{1,0:T(8,128)(2,1)S(1)} %get-tuple-element.135.refs_2_), channel_id=1, source_target_pairs={{0,1},{1,0},{2,3},{3,2},{4,5},{5,4},{6,7},{7,6},{8,9},{9,8},{10,11... | collective-permute-start | bytes 1179656 | tf_op jit(solution)/shard_map/ppermute | solution.py:165
  79.9 17.0 %collective-permute-start.20 = (bf16[384,512]{1,0:T(8,128)(2,1)S(1)}, bf16[384,512]{1,0:T(8,128)(2,1)S(1)}, u32[]{:S(2)}, u32[]{:S(2)}) collective-permute-start(bf16[384,512]{1,0:T(8,128)(2,1)S(1)} %get-tuple-element.136.refs_6_), channel_id=1, source_target_pairs={{0,1},{1,0},{2,3},{3,2},{4,5},{5,4},{6,7},{7,6},{8,9},{9,8},{10,11... | collective-permute-start | bytes 1179656 | tf_op jit(solution)/shard_map/ppermute | solution.py:165
  99.2 22.5 %collective-permute-start.28 = (bf16[512,1024]{1,0:T(8,128)(2,1)S(1)}, bf16[512,1024]{1,0:T(8,128)(2,1)S(1)}, u32[]{:S(2)}, u32[]{:S(2)}) collective-permute-start(bf16[512,1024]{1,0:T(8,128)(2,1)S(1)} %get-tuple-element.163), channel_id=1, source_target_pairs={{0,8},{2,10},{4,12},{6,14},{8,0},{10,2},{12,4},{14,6},{16,24},{18,... | collective-permute-start | bytes 3145736 | tf_op jit(solution)/shard_map/ppermute | solution.py:170
  101.1 20.5 %collective-permute-start.29 = (bf16[512,1024]{1,0:T(8,128)(2,1)S(1)}, bf16[512,1024]{1,0:T(8,128)(2,1)S(1)}, u32[]{:S(2)}, u32[]{:S(2)}) collective-permute-start(bf16[512,1024]{1,0:T(8,128)(2,1)S(1)} %get-tuple-element.164), channel_id=1, source_target_pairs={{0,0},{2,2},{4,4},{6,6},{8,16},{10,18},{12,20},{14,22},{16,8},{18,... | collective-permute-start | bytes 3145736 | tf_op jit(solution)/shard_map/ppermute | solution.py:170
  104.2 4.3 %collective-permute-start.23 = (bf16[192,1024]{1,0:T(8,128)(2,1)S(1)}, bf16[192,1024]{1,0:T(8,128)(2,1)S(1)}, u32[]{:S(2)}, u32[]{:S(2)}) collective-permute-start(bf16[192,1024]{1,0:T(8,128)(2,1)S(1)} %get-tuple-element.150), channel_id=1, source_target_pairs={{0,2},{2,0},{4,6},{6,4},{8,10},{10,8},{12,14},{14,12},{16,18},{18,... | collective-permute-start | bytes 1179656 | tf_op jit(solution)/shard_map/ppermute | solution.py:158
  108.7 19.5 %collective-permute-start.27 = (bf16[384,1024]{1,0:T(8,128)(2,1)S(1)}, bf16[384,1024]{1,0:T(8,128)(2,1)S(1)}, u32[]{:S(2)}, u32[]{:S(2)}) collective-permute-start(bf16[384,1024]{1,0:T(8,128)(2,1)S(1)} %get-tuple-element.161), channel_id=1, source_target_pairs={{0,4},{2,6},{4,0},{6,2},{8,12},{10,14},{12,8},{14,10},{16,20},{18,... | collective-permute-start | bytes 2359304 | tf_op jit(solution)/shard_map/ppermute | solution.py:161
  112.9 11.1 %collective-permute-start.25 = (bf16[192,1024]{1,0:T(8,128)(2,1)S(1)}, bf16[192,1024]{1,0:T(8,128)(2,1)S(1)}, u32[]{:S(2)}, u32[]{:S(2)}) collective-permute-start(bf16[192,1024]{1,0:T(8,128)(2,1)S(1)} %get-tuple-element.157), channel_id=1, source_target_pairs={{0,2},{2,0},{4,6},{6,4},{8,10},{10,8},{12,14},{14,12},{16,18},{18,... | collective-permute-start | bytes 1179656 | tf_op jit(solution)/shard_map/ppermute | solution.py:158
  113.0 11.1 %collective-permute-start.26 = (bf16[192,1024]{1,0:T(8,128)(2,1)S(1)}, bf16[192,1024]{1,0:T(8,128)(2,1)S(1)}, u32[]{:S(2)}, u32[]{:S(2)}) collective-permute-start(bf16[192,1024]{1,0:T(8,128)(2,1)S(1)} %get-tuple-element.160), channel_id=1, source_target_pairs={{0,2},{2,0},{4,6},{6,4},{8,10},{10,8},{12,14},{14,12},{16,18},{18,... | collective-permute-start | bytes 1179656 | tf_op jit(solution)/shard_map/ppermute | solution.py:158
  (10 other events, 25.3 us)
